TPU v7x, 32 devices: a whole 2x2x4 slice. The times are simulated.
32 devices in a mesh: refl: 2 (over y), slab: 16 (over z, x, core).
Axes of the slice: x: 2, y: 2, z: 4, core: 2. Of those that a mesh axis runs over, the one named last changes fastest.
Arguments:
- amplitude: float32 [128, 128, 128], P('slab', 'refl'), may hold values from 1 to 3
- displacement: float32 [3, 128, 128, 128], P(None, 'slab', 'refl'), may hold values from -12 to 12
- support: int32 [128, 128, 128], P('slab'), may hold values from 0 to 1, as said below
- miller: int32 [2, 3], P('refl'), may hold values from -2 to 2, as said below
- shift_kz: int32 [2], P('refl'), may hold values from 0 to 255
- intensity: float32 [2, 256, 256, 256], P('refl', None, 'slab'), may hold values from 0.02 to 0.5
Outputs:
- grad_amplitude: float32 [128, 128, 128], P('slab', 'refl')
- grad_displacement: float32 [3, 128, 128, 128], P(None, 'slab', 'refl')
Inputs may be any that keep to these rules, and one draw needn't show every extreme that they name: 1 inside the object's support, 0 outside. `miller`: no index is zero.
All inputs are finite; a program needn't handle non-finite values.
Results may differ from a plain program's by a relative error of at most 0.0003.
Values sent between devices are 32-bit elements; how exact they have to be, the bound alone decides.
No kernel may reach another device: no remote copies, remote signals or barrier semaphores. Data moves between devices by JAX's collectives and lax.ppermute only.
A program may use at most 64 MiB of HBM per device.

v0:
```python
import functools

import jax
import jax.numpy as jnp
import ml_dtypes
import numpy as np
from jax import lax
from jax.experimental import pallas as pl
from jax.experimental.pallas import tpu as pltpu
from jax.sharding import PartitionSpec as P

STRAIN_WEIGHT = 0.05
EDGE_WEIGHT = 0.05
F32 = jnp.float32
BF16 = jnp.bfloat16


def split_table(table):
    high = table.astype(ml_dtypes.bfloat16)
    low = (table - high.astype(np.float64)).astype(ml_dtypes.bfloat16)
    return high, low


def forward_table(freqs, places, length):
    angle = 2.0 * np.pi / length * (freqs[:, None] * places[None, :] % length)
    cosine = np.cos(angle) * length ** (-0.5)
    sine = np.sin(angle) * length ** (-0.5)
    return np.block([[cosine, sine], [-sine, cosine]])


def turn_fits():
    nodes = np.cos(np.pi * (np.arange(400) + 0.5) / 400)
    t = (nodes + 1.0) / 8.0
    r = np.sqrt(t)
    fits = []
    for values, degree in ((np.cos(2 * np.pi * r), 8), (np.sin(2 * np.pi * r) / r, 8)):
        cheb = np.polynomial.chebyshev.Chebyshev.fit(t, values, degree, domain=[0.0, 0.25])
        fits.append([float(c) for c in cheb.convert(kind=np.polynomial.Polynomial).coef])
    return fits


COS_FIT, SIN_FIT = turn_fits()


def series(coefs, t):
    total = jnp.full_like(t, coefs[-1])
    for coef in coefs[-2::-1]:
        total = total * t + coef
    return total


def halves(x):
    high = x.astype(BF16)
    return high, (x - high.astype(F32)).astype(BF16)


def dot(a, b):
    return jnp.dot(a, b, preferred_element_type=F32)


def dot_pairs(a, b):
    return dot(a[0], b[0]) + (dot(a[0], b[1]) + dot(a[1], b[0]))


def vmem(count):
    return [pl.BlockSpec(memory_space=pltpu.VMEM)] * count


SMEM = pl.BlockSpec(memory_space=pltpu.SMEM)


def call(kernel, outs, in_specs, scratch, flops, moved, name, grid=()):
    return pl.pallas_call(
        kernel,
        grid=grid,
        out_shape=[jax.ShapeDtypeStruct(s, F32) for s in outs],
        in_specs=in_specs,
        out_specs=vmem(len(outs)),
        scratch_shapes=scratch,
        compiler_params=pltpu.CompilerParams(vmem_limit_bytes=48 * 1024 * 1024),
        cost_estimate=pl.CostEstimate(flops=flops, bytes_accessed=moved, transcendentals=0),
        name=name,
    )


def object_kernel(refls, grid, place, params, amp, disp, sup, *outs):
    planes, rows, depth = amp.shape
    first = pl.multiple_of(place[2] * rows, rows)
    zed = lax.broadcasted_iota(jnp.int32, (rows, depth), 1).astype(F32) * (1.0 / grid)

    def plane(p, carry):
        weight = sup[p, pl.ds(first, rows), :].astype(F32) * amp[p]
        parts = [disp[0, p], disp[1, p], disp[2, p]]
        for k in range(refls):
            phase = params[4 * k] * parts[0] + params[4 * k + 1] * parts[1] + params[4 * k + 2] * parts[2]
            shifted = params[4 * k + 3] * zed
            turns = phase * (0.5 / np.pi) + (shifted - jnp.floor(shifted))
            turns = turns - jnp.floor(turns + 0.5)
            square = turns * turns
            cosine = series(COS_FIT, square)
            sine = series(SIN_FIT, square) * turns
            outs[k][0, p] = weight * cosine
            outs[k][1, p] = weight * sine
            outs[refls + k][0, p] = cosine
            outs[refls + k][1, p] = sine
        return carry

    lax.fori_loop(0, planes, plane, 0)


def y_forward_kernel(refls, chips, place, *refs):
    parts, (high, low), outs = refs[: 2 * refls], refs[2 * refls : 2 * refls + 2], refs[2 * refls + 2 : -2]
    hold_high, hold_low = refs[-2:]
    chip, core, refl = place[0], place[1], place[2]
    planes, rows, depth = parts[0].shape[1:]
    length = rows * refls
    share = high.shape[1] // chips

    def order(table):
        return jnp.concatenate(
            [table[core, pl.ds(pl.multiple_of((chip ^ k) * share, share), share), :] for k in range(chips)], axis=0
        )

    table = (order(high), order(low))
    for src in range(2):
        for p in range(planes):
            lane = (src * planes + p) * depth
            for c in range(2):
                for k in range(refls):
                    one, two = halves(parts[src * refls + k][c, p])
                    at = pl.ds(pl.multiple_of(c * length + (refl ^ k) * rows, rows), rows)
                    hold_high[at, lane : lane + depth] = one
                    hold_low[at, lane : lane + depth] = two
    for src in range(2):
        for p in range(0, planes, 2):
            lane = (src * planes + p) * depth
            operand = (hold_high[:, lane : lane + 2 * depth], hold_low[:, lane : lane + 2 * depth])
            result = dot_pairs(table, operand)
            base = (core if src == 0 else 1 - core) * planes + p
            for k in range(chips):
                for j in range(2):
                    outs[k][base + j] = result[k * share : (k + 1) * share, j * depth : (j + 1) * depth]


def middle_kernel(chips, place, *refs):
    got, intensity = refs[:chips], refs[chips]
    fwd_high, fwd_low, bwd_high, bwd_low = refs[chips + 1 : chips + 5]
    outs = refs[chips + 5 : 2 * chips + 5]
    gather, scatter = refs[2 * chips + 5 :]
    chip = place[0]
    group, width, depth = got[0].shape
    rows = width // 2
    edge = group * chips
    grid = 2 * edge
    for pair in range(0, rows, 2):
        for k in range(chips):
            for c in range(2):
                at = pl.ds(pl.multiple_of(c * edge + (chip ^ k) * group, group), group)
                for j in range(2):
                    gather[at, j * depth : (j + 1) * depth] = got[k][:, c * rows + pair + j, :]
        forward = (fwd_high[...], fwd_low[...])
        adjoint = (bwd_high[...], bwd_low[...])
        one = dot_pairs(forward, halves(gather[...]))
        lines = jnp.concatenate(
            [
                jnp.concatenate([one[:grid, j * depth : (j + 1) * depth], one[grid:, j * depth : (j + 1) * depth]], axis=1)
                for j in range(2)
            ],
            axis=0,
        )
        spectrum = dot_pairs(halves(lines), adjoint)
        real, imag = spectrum[:, :grid], spectrum[:, grid:]
        measured = jnp.concatenate([intensity[0, :, pair, :], intensity[0, :, pair + 1, :]], axis=0)
        excess = 4.0 * (real * real + imag * imag - measured)
        residual = jnp.concatenate([excess * real, excess * imag], axis=1)
        back = dot_pairs(halves(residual), forward)
        lines = jnp.concatenate(
            [
                jnp.concatenate([back[:grid, c * depth : (c + 1) * depth], back[grid:, c * depth : (c + 1) * depth]], axis=1)
                for c in range(2)
            ],
            axis=0,
        )
        scatter[...] = dot_pairs(adjoint, halves(lines))
        for k in range(chips):
            for c in range(2):
                at = pl.ds(pl.multiple_of(c * edge + (chip ^ k) * group, group), group)
                for j in range(2):
                    outs[k][:, c * rows + pair + j, :] = scatter[at, j * depth : (j + 1) * depth]


def y_adjoint_kernel(refls, chips, chunks, mate, place, *refs):
    got, (high, low), outs = refs[: chunks * chips], refs[chunks * chips : chunks * chips + 2], refs[chunks * chips + 2 : -1]
    hold = refs[-1]
    chip, core, refl = place[0], place[1], place[2]
    parts, planes, rows, depth = outs[0].shape
    length = rows * refls
    width = got[0].shape[1]
    table = (high[core], low[core])
    base = (1 - core if mate else core) * planes
    for p in range(0, planes, 2):
        for q in range(chunks):
            for k in range(chips):
                at = pl.ds(pl.multiple_of((q * chips + (chip ^ k)) * width, width), width)
                for j in range(2):
                    hold[at, (p + j) * depth : (p + j + 1) * depth] = got[q * chips + k][base + p + j]
    for p in range(0, planes, 2):
        result = dot_pairs(table, halves(hold[:, p * depth : (p + 2) * depth]))
        for q in range(refls):
            for c in range(2):
                at = (q * 2 + c) * rows
                for j in range(2):
                    value = result[at : at + rows, j * depth : (j + 1) * depth]
                    for k in range(refls):

                        @pl.when((refl ^ k) == q)
                        def _():
                            outs[k][c, p + j] = value


def add_kernel(a, b, out):
    out[...] = a[...] + b[...]


def final_kernel(refls, place, params, *refs):
    amp, sup, lapped, own, mate = refs[:5]
    others = refs[5 : 5 + refls - 1]
    phases = refs[5 + refls - 1 : 5 + 2 * refls - 1]
    out_amp, out_disp = refs[-2:]
    planes, rows, depth = amp.shape
    first = pl.multiple_of(place[2] * rows, rows)

    def plane(p, carry):
        mask = sup[p, pl.ds(first, rows), :].astype(F32)
        weight = mask * amp[p]
        total = jnp.zeros((rows, depth), F32)
        moved = [jnp.zeros((rows, depth), F32) for _ in range(3)]
        for k in range(refls):
            if k == 0:
                real, imag = own[0, p] + mate[0, p], own[1, p] + mate[1, p]
            else:
                real, imag = others[k - 1][0, p], others[k - 1][1, p]
            cosine, sine = phases[k][0, p], phases[k][1, p]
            total = total + (real * cosine + imag * sine)
            across = weight * (imag * cosine - real * sine)
            moved = [m + params[4 * k + c] * across for c, m in enumerate(moved)]
        out_amp[p] = mask * total + (2.0 * EDGE_WEIGHT) * (mask * lapped[0, p])
        for c in range(3):
            out_disp[c, p] = moved[c] + (2.0 * STRAIN_WEIGHT) * lapped[c + 1, p]
        return carry

    lax.fori_loop(0, planes, plane, 0)


def with_halo(cells, sides, width):
    for axis, dim in sides:
        count = lax.axis_size(axis)
        ends = count - 1
        head = lax.slice_in_dim(cells, 0, width, axis=dim)
        tail = lax.slice_in_dim(cells, cells.shape[dim] - width, cells.shape[dim], axis=dim)
        cells = jnp.concatenate(
            [
                lax.ppermute(tail, axis, [(i, (i + 1) % count) for i in range(ends)]),
                cells,
                lax.ppermute(head, axis, [((i + 1) % count, i) for i in range(ends)]),
            ],
            axis=dim,
        )
    return cells


def regulariser(fields):
    extended = with_halo(fields, (("refl", 2), ("slab", 1)), 1)
    extended = jnp.pad(extended, ((0, 0), (0, 0), (0, 0), (1, 1)))
    centre = extended[:, 1:-1, 1:-1, 1:-1]
    beside = extended[:, 2:, 1:-1, 1:-1] + extended[:, :-2, 1:-1, 1:-1]
    beside = beside + extended[:, 1:-1, 2:, 1:-1] + extended[:, 1:-1, :-2, 1:-1]
    beside = beside + extended[:, 1:-1, 1:-1, 2:] + extended[:, 1:-1, 1:-1, :-2]
    return 6.0 * centre - beside


def swap(x, axis, bits):
    count = lax.axis_size(axis)
    return lax.ppermute(x, axis, [(i, i ^ bits) for i in range(count)])


def body(amplitude, displacement, support, miller, shift_kz, intensity):
    refls = lax.axis_size("refl")
    slabs = lax.axis_size("slab")
    chips = slabs // 2
    planes, rows, depth = amplitude.shape
    edge = planes * slabs
    grid = 2 * edge
    keys = grid // slabs
    chunk = 8
    chunks = keys // chunk
    refl = lax.axis_index("refl")
    slab = lax.axis_index("slab")
    place = jnp.stack([slab // 2, slab % 2, refl]).astype(jnp.int32)
    cells = planes * rows * depth

    every, inner = np.arange(grid), np.arange(edge)
    table = forward_table(every, inner, grid)
    fwd, bwd = split_table(table), split_table(table.T)
    y_fwd, y_bwd = [], []
    by_chunk = table.reshape(2, chips, 2, chunks, chunk, 2 * edge)
    for q in range(chunks):
        y_fwd.append(split_table(by_chunk[:, :, :, q].transpose(2, 1, 0, 3, 4).reshape(2, chips * 2 * chunk, 2 * edge)))
    back = by_chunk.transpose(2, 5, 3, 1, 0, 4).reshape(2, 2, refls, rows, chunks * chips * 2 * chunk)
    y_bwd = split_table(back.transpose(0, 2, 1, 3, 4).reshape(2, 2 * edge, chunks * chips * 2 * chunk))

    own_params = jnp.concatenate([miller[0].astype(F32), shift_kz.astype(F32)])
    params = jnp.concatenate([own_params] + [swap(own_params, "refl", k) for k in range(1, refls)])

    made = call(
        functools.partial(object_kernel, refls, grid),
        [(2, planes, rows, depth)] * (2 * refls),
        [SMEM, SMEM] + vmem(3),
        [],
        100 * refls * cells,
        cells * 4 * (5 + 4 * refls),
        "object",
    )(place, params, amplitude, displacement, support)
    parts, phases = made[:refls], made[refls:]
    held = [parts[0]] + [swap(parts[k], "refl", k) for k in range(1, refls)]
    mates = [swap(x, "slab", 1) for x in held]

    mask_own = lax.dynamic_slice_in_dim(support, refl * rows, rows, 1).astype(F32)
    fields = jnp.concatenate([(mask_own * amplitude)[None], displacement], axis=0)
    lapped = regulariser(fields)

    group = 2 * planes
    sent_shape = (group, 2 * chunk, depth)
    returned = []
    arrived = []
    for q in range(chunks):
        high, low = y_fwd[q]
        sends = call(
            functools.partial(y_forward_kernel, refls, chips),
            [sent_shape] * chips,
            [SMEM] + vmem(2 * refls + 2),
            [pltpu.VMEM((2 * edge, group * depth), BF16)] * 2,
            6 * group * depth * 2 * edge * high.shape[1],
            4 * group * depth * (2 * edge + high.shape[1]),
            "y_forward",
        )(place, *held, *mates, jnp.asarray(high), jnp.asarray(low))
        arrived.append([sends[0]] + [swap(sends[k], "slab", 2 * k) for k in range(1, chips)])
    for q in range(chunks):
        backs = call(
            functools.partial(middle_kernel, chips),
            [sent_shape] * chips,
            [SMEM]
            + vmem(chips)
            + [pl.BlockSpec((1, grid, chunk, grid), functools.partial(lambda at, step: (0, 0, at, 0), q))]
            + vmem(4),
            [pltpu.VMEM((2 * edge, 2 * depth), F32)] * 2,
            6 * chunk * (2 * edge * 2 * grid * depth * 2 + grid * 2 * depth * 2 * grid * 2),
            4 * (2 * chips * group * 2 * chunk * depth + grid * grid * chunk),
            "middle",
            (1,),
        )(place, *arrived[q], intensity, *[jnp.asarray(t) for t in fwd + bwd])
        returned.append([backs[0]] + [swap(backs[k], "slab", 2 * k) for k in range(1, chips)])

    flat = [x for chunk_of in returned for x in chunk_of]

    def y_adjoint(mate):
        return call(
            functools.partial(y_adjoint_kernel, refls, chips, chunks, mate),
            [(2, planes, rows, depth)] * refls,
            [SMEM] + vmem(chunks * chips + 2),
            [pltpu.VMEM((2 * edge, planes * depth), F32)],
            6 * planes * depth * 4 * edge * edge,
            4 * planes * depth * 4 * edge,
            "y_adjoint",
        )(place, *flat, jnp.asarray(y_bwd[0]), jnp.asarray(y_bwd[1]))

    for_mate = y_adjoint(True)
    from_mate = [swap(x, "slab", 1) for x in for_mate]
    mine = y_adjoint(False)
    others = []
    for k in range(1, refls):
        (whole,) = call(
            add_kernel, [(2, planes, rows, depth)], vmem(2), [], 2 * cells, 24 * cells, "add"
        )(mine[k], from_mate[k])
        others.append(swap(whole, "refl", k))

    return tuple(
        call(
            functools.partial(final_kernel, refls),
            [(planes, rows, depth), (3, planes, rows, depth)],
            [SMEM, SMEM] + vmem(5 + refls - 1 + refls),
            [],
            20 * refls * cells,
            4 * cells * (12 + 4 * refls),
            "final",
        )(place, params, amplitude, support, lapped, mine[0], from_mate[0], *others, *phases)
    )


def solution(mesh):
    placed = (
        P("slab", "refl", None),
        P(None, "slab", "refl", None),
        P("slab", None, None),
        P("refl", None),
        P("refl"),
        P("refl", None, "slab", None),
    )
    return jax.shard_map(
        body,
        mesh=mesh,
        in_specs=placed,
        out_specs=(P("slab", "refl", None), P(None, "slab", "refl", None)),
        check_vma=False,
    )
```

profile of v0, /device:TPU:13, one launch (start us, length us, event | category | flops | bytes accessed | tf_op | source)
XLA Modules:
  0.0 177.5 jit_solution(5123918007162469359)
XLA Ops:
  2.3 2.1 %collective-permute-done = f32[4]{0:T(128)S(1)} collective-permute-done((f32[4]{0:T(128)S(1)}, f32[4]{0:T(128)S(1)}, u32[]{:S(2)}, u32[]{:S(2)}) %collective-permute-start) | collective-permute-done | bytes 48 | tf_op jit(solution)/shard_map/ppermute | solution.py:284
  9.4 2.1 %collective-permute-start.6 = (f32[2,8,64,128]{3,2,1,0:T(8,128)S(1)}, f32[2,8,64,128]{3,2,1,0:T(8,128)S(1)}, u32[]{:S(2)}, u32[]{:S(2)}) collective-permute-start(f32[2,8,64,128]{3,2,1,0:T(8,128)S(1)} %get-tuple-element.42.refs_0_), channel_id=1, source_target_pairs={{0,1},{1,0},{2,3},{3,2},{4,5},{5,4},{6,7},{7,6},{8,9},{9,8},{10,11... | collective-permute-start | bytes 1572872 | tf_op jit(solution)/shard_map/ppermute | solution.py:284
  11.5 9.3 %collective-permute-done.5.refs_1_ = f32[2,8,64,128]{3,2,1,0:T(8,128)S(1)} collective-permute-done((f32[2,8,64,128]{3,2,1,0:T(8,128)S(1)}, f32[2,8,64,128]{3,2,1,0:T(8,128)S(1)}, u32[]{:S(2)}, u32[]{:S(2)}) %collective-permute-start.5) | collective-permute-done | bytes 524320 | tf_op jit(solution)/shard_map/ppermute | solution.py:284
  20.8 2.7 %collective-permute-start.7 = (f32[2,8,64,128]{3,2,1,0:T(8,128)S(1)}, f32[2,8,64,128]{3,2,1,0:T(8,128)S(1)}, u32[]{:S(2)}, u32[]{:S(2)}) collective-permute-start(f32[2,8,64,128]{3,2,1,0:T(8,128)S(1)} %collective-permute-done.5.refs_1_), channel_id=1, source_target_pairs={{0,1},{1,0},{2,3},{3,2},{4,5},{5,4},{6,7},{7,6},{8,9},{9,8},{10,11... | collective-permute-start | bytes 1572872 | tf_op jit(solution)/shard_map/ppermute | solution.py:284
  26.9 1.7 y_forward.2
  31.3 2.3 %collective-permute-start.11 = (f32[16,16,128]{2,1,0:T(8,128)S(1)}, f32[16,16,128]{2,1,0:T(8,128)S(1)}, u32[]{:S(2)}, u32[]{:S(2)}) collective-permute-start(f32[16,16,128]{2,1,0:T(8,128)S(1)} %get-tuple-element.48), channel_id=1, source_target_pairs={{0,8},{1,9},{2,10},{3,11},{4,12},{5,13},{6,14},{7,15},{8,0},{9,1},... | collective-permute-start | bytes 393224 | tf_op jit(solution)/shard_map/ppermute | solution.py:284
  34.6 1.8 y_forward.3
  40.9 2.1 %collective-permute-start.23 = (f32[16,16,128]{2,1,0:T(8,128)S(1)}, f32[16,16,128]{2,1,0:T(8,128)S(1)}, u32[]{:S(2)}, u32[]{:S(2)}) collective-permute-start(f32[16,16,128]{2,1,0:T(8,128)S(1)} %get-tuple-element.62), channel_id=1, source_target_pairs={{0,4},{1,5},{2,6},{3,7},{4,0},{5,1},{6,2},{7,3},{8,12},{9,13},{10,... | collective-permute-start | bytes 393224 | tf_op jit(solution)/shard_map/ppermute | solution.py:284
  43.0 5.6 %collective-permute-done.12.refs_5_ = f32[16,16,128]{2,1,0:T(8,128)S(1)} collective-permute-done((f32[16,16,128]{2,1,0:T(8,128)S(1)}, f32[16,16,128]{2,1,0:T(8,128)S(1)}, u32[]{:S(2)}, u32[]{:S(2)}) %collective-permute-start.12) | collective-permute-done | bytes 131104 | tf_op jit(solution)/shard_map/ppermute | solution.py:284
  48.6 4.1 %collective-permute-done.13.refs_6_ = f32[16,16,128]{2,1,0:T(8,128)S(1)} collective-permute-done((f32[16,16,128]{2,1,0:T(8,128)S(1)}, f32[16,16,128]{2,1,0:T(8,128)S(1)}, u32[]{:S(2)}, u32[]{:S(2)}) %collective-permute-start.13) | collective-permute-done | bytes 131104 | tf_op jit(solution)/shard_map/ppermute | solution.py:284
  53.8 3.0 %collective-permute-done.14.refs_7_ = f32[16,16,128]{2,1,0:T(8,128)S(1)} collective-permute-done((f32[16,16,128]{2,1,0:T(8,128)S(1)}, f32[16,16,128]{2,1,0:T(8,128)S(1)}, u32[]{:S(2)}, u32[]{:S(2)}) %collective-permute-start.14) | collective-permute-done | bytes 131104 | tf_op jit(solution)/shard_map/ppermute | solution.py:284
  56.8 1.7 collective-permute-start.27
  58.5 12.1 %middle.2 = (f32[16,16,128]{2,1,0:T(8,128)S(1)}, f32[16,16,128]{2,1,0:T(8,128)S(1)}, f32[16,16,128]{2,1,0:T(8,128)S(1)}, f32[16,16,128]{2,1,0:T(8,128)S(1)}, f32...) custom-call(s32[3]{0:T(128)S(1)} %pad_add_fusion.place, ...), custom_call_target="tpu_custom_call" | custom-call | flops 4831838208 | bytes 4194304 | tf_op jit(solution)/shard_map/middle/pallas_call | solution.py:349
  72.0 4.2 %collective-permute-start.16 = (f32[16,16,128]{2,1,0:T(8,128)S(1)}, f32[16,16,128]{2,1,0:T(8,128)S(1)}, u32[]{:S(2)}, u32[]{:S(2)}) collective-permute-start(f32[16,16,128]{2,1,0:T(8,128)S(1)} %get-tuple-element.54), channel_id=1, source_target_pairs={{0,4},{1,5},{2,6},{3,7},{4,0},{5,1},{6,2},{7,3},{8,12},{9,13},{10,... | collective-permute-start | bytes 393224 | tf_op jit(solution)/shard_map/ppermute | solution.py:284
  79.7 13.0 %middle.3 = (f32[16,16,128]{2,1,0:T(8,128)S(1)}, f32[16,16,128]{2,1,0:T(8,128)S(1)}, f32[16,16,128]{2,1,0:T(8,128)S(1)}, f32[16,16,128]{2,1,0:T(8,128)}, f32[16,...) custom-call(s32[3]{0:T(128)S(1)} %pad_add_fusion.place, ...), custom_call_target="tpu_custom_call" | custom-call | flops 4831838208 | bytes 4194304 | tf_op jit(solution)/shard_map/middle/pallas_call | solution.py:349
  97.5 4.1 %collective-permute-start.30 = (f32[16,16,128]{2,1,0:T(8,128)S(1)}, f32[16,16,128]{2,1,0:T(8,128)S(1)}, u32[]{:S(2)}, u32[]{:S(2)}) collective-permute-start(f32[16,16,128]{2,1,0:T(8,128)S(1)} %get-tuple-element.70), channel_id=1, source_target_pairs={{0,4},{1,5},{2,6},{3,7},{4,0},{5,1},{6,2},{7,3},{8,12},{9,13},{10,... | collective-permute-start | bytes 393224 | tf_op jit(solution)/shard_map/ppermute | solution.py:284
  105.1 2.0 %collective-permute-start.33 = (f32[16,16,128]{2,1,0:T(8,128)}, f32[16,16,128]{2,1,0:T(8,128)}, u32[]{:S(2)}, u32[]{:S(2)}) collective-permute-start(f32[16,16,128]{2,1,0:T(8,128)} %get-tuple-element.73), channel_id=1, source_target_pairs={{0,10},{1,11},{2,8},{3,9},{4,14},{5,15},{6,12},{7,13},{8,2},{9,3},... | collective-permute-start | bytes 393224 | tf_op jit(solution)/shard_map/ppermute | solution.py:284
  108.7 2.1 %collective-permute-start.35 = (f32[16,16,128]{2,1,0:T(8,128)}, f32[16,16,128]{2,1,0:T(8,128)}, u32[]{:S(2)}, u32[]{:S(2)}) collective-permute-start(f32[16,16,128]{2,1,0:T(8,128)} %get-tuple-element.75), channel_id=1, source_target_pairs={{0,14},{1,15},{2,12},{3,13},{4,10},{5,11},{6,8},{7,9},{8,6},{9,7},... | collective-permute-start | bytes 393224 | tf_op jit(solution)/shard_map/ppermute | solution.py:284
  110.8 3.7 %collective-permute-done.32.refs_12_ = f32[16,16,128]{2,1,0:T(8,128)} collective-permute-done((f32[16,16,128]{2,1,0:T(8,128)}, f32[16,16,128]{2,1,0:T(8,128)}, u32[]{:S(2)}, u32[]{:S(2)}) %collective-permute-start.32) | collective-permute-done | bytes 131104 | tf_op jit(solution)/shard_map/ppermute | solution.py:284
  114.4 4.5 %collective-permute-done.33.refs_13_ = f32[16,16,128]{2,1,0:T(8,128)} collective-permute-done((f32[16,16,128]{2,1,0:T(8,128)}, f32[16,16,128]{2,1,0:T(8,128)}, u32[]{:S(2)}, u32[]{:S(2)}) %collective-permute-start.33) | collective-permute-done | bytes 131104 | tf_op jit(solution)/shard_map/ppermute | solution.py:284
  119.0 6.9 %collective-permute-done.34.refs_14_ = f32[16,16,128]{2,1,0:T(8,128)} collective-permute-done((f32[16,16,128]{2,1,0:T(8,128)}, f32[16,16,128]{2,1,0:T(8,128)}, u32[]{:S(2)}, u32[]{:S(2)}) %collective-permute-start.34) | collective-permute-done | bytes 131104 | tf_op jit(solution)/shard_map/ppermute | solution.py:284
  125.9 5.4 %collective-permute-done.35.refs_15_ = f32[16,16,128]{2,1,0:T(8,128)} collective-permute-done((f32[16,16,128]{2,1,0:T(8,128)}, f32[16,16,128]{2,1,0:T(8,128)}, u32[]{:S(2)}, u32[]{:S(2)}) %collective-permute-start.35) | collective-permute-done | bytes 131104 | tf_op jit(solution)/shard_map/ppermute | solution.py:284
  138.5 2.9 %y_adjoint.3 = (f32[2,8,64,128]{3,2,1,0:T(8,128)S(1)}, f32[2,8,64,128]{3,2,1,0:T(8,128)S(1)}) custom-call(s32[3]{0:T(128)S(1)} %pad_add_fusion.place, f32[16,16,128]{2,1,0:T(8,128)S(1)} %get-tuple-element.52.refs_0_, f32[16,16,128]{2,1,0:T(8,128)S(1)} %collective-permute-done.15.refs_1_, f32[16,16,128]{2,1,0:T(8,128)S(1)} %collective-permute-done.16.refs_2_, ...), custom_call_target="tpu_custom_call" | custom-call | flops 402653184 | bytes 2097152 | tf_op jit(solution)/shard_map/y_adjoint/pallas_call | solution.py:367
  141.4 4.9 %collective-permute-start.37 = (f32[2,8,64,128]{3,2,1,0:T(8,128)S(1)}, f32[2,8,64,128]{3,2,1,0:T(8,128)S(1)}, u32[]{:S(2)}, u32[]{:S(2)}) collective-permute-start(f32[2,8,64,128]{3,2,1,0:T(8,128)S(1)} %get-tuple-element.79), channel_id=1, source_target_pairs={{0,1},{1,0},{2,3},{3,2},{4,5},{5,4},{6,7},{7,6},{8,9},{9,8},{10,11... | collective-permute-start | bytes 1572872 | tf_op jit(solution)/shard_map/ppermute | solution.py:284
  146.4 2.1 %collective-permute-start.2 = (f32[4,8,1,128]{3,2,1,0:T(1,128)S(1)}, f32[4,8,1,128]{3,2,1,0:T(1,128)S(1)}, u32[]{:S(2)}, u32[]{:S(2)}) collective-permute-start(f32[4,8,1,128]{3,2,1,0:T(1,128)S(1)} %get-tuple-element.85), channel_id=1, source_target_pairs={{16,0},{17,1},{18,2},{19,3},{20,4},{21,5},{22,6},{23,7},{24,8},{25... | collective-permute-start | bytes 49160 | tf_op jit(solution)/shard_map/ppermute | solution.py:265
  149.9 3.2 %collective-permute-done.1 = f32[4,8,1,128]{3,2,1,0:T(1,128)S(1)} collective-permute-done((f32[4,8,1,128]{3,2,1,0:T(1,128)S(1)}, f32[4,8,1,128]{3,2,1,0:T(1,128)S(1)}, u32[]{:S(2)}, u32[]{:S(2)}) %collective-permute-start.1) | collective-permute-done | bytes 16416 | tf_op jit(solution)/shard_map/ppermute | solution.py:263
  153.1 3.4 %collective-permute-start.3 = (f32[4,1,66,128]{3,2,1,0:T(8,128)S(1)}, f32[4,1,66,128]{3,2,1,0:T(8,128)S(1)}, u32[]{:S(2)}, u32[]{:S(2)}) collective-permute-start(f32[4,1,66,128]{3,2,1,0:T(8,128)S(1)} %get-tuple-element.83), channel_id=1, source_target_pairs={{1,0},{2,1},{3,2},{4,3},{5,4},{6,5},{7,6},{8,7},{9,8},{10,9},{11,1... | collective-permute-start | bytes 405512 | tf_op jit(solution)/shard_map/ppermute | solution.py:265
  156.5 3.0 %collective-permute-start.4 = (f32[4,1,66,128]{3,2,1,0:T(8,128)S(1)}, f32[4,1,66,128]{3,2,1,0:T(8,128)S(1)}, u32[]{:S(2)}, u32[]{:S(2)}) collective-permute-start(f32[4,1,66,128]{3,2,1,0:T(8,128)S(1)} %get-tuple-element.82), channel_id=1, source_target_pairs={{0,1},{1,2},{2,3},{3,4},{4,5},{5,6},{6,7},{7,8},{8,9},{9,10},{10,1... | collective-permute-start | bytes 405512 | tf_op jit(solution)/shard_map/ppermute | solution.py:263
  159.5 2.9 %y_adjoint.2 = (f32[2,8,64,128]{3,2,1,0:T(8,128)S(1)}, f32[2,8,64,128]{3,2,1,0:T(8,128)S(1)}) custom-call(s32[3]{0:T(128)S(1)} %pad_add_fusion.place, f32[16,16,128]{2,1,0:T(8,128)S(1)} %get-tuple-element.52.refs_0_, f32[16,16,128]{2,1,0:T(8,128)S(1)} %collective-permute-done.15.refs_1_, f32[16,16,128]{2,1,0:T(8,128)S(1)} %collective-permute-done.16.refs_2_, ...), custom_call_target="tpu_custom_call" | custom-call | flops 402653184 | bytes 2097152 | tf_op jit(solution)/shard_map/y_adjoint/pallas_call | solution.py:367
  162.6 2.1 %select_maximum_fusion = f32[4,10,66,130]{3,2,1,0:T(8,128)S(1)} fusion(f32[4,1,66,128]{3,2,1,0:T(8,128)S(1)} %collective-permute-done.3, f32[4,1,66,128]{3,2,1,0:T(8,128)S(1)} %collective-permute-done.4, f32[4,8,1,128]{3,2,1,0:T(1,128)S(1)} %collective-permute-done.2, f32[4,8,1,128]{3,2,1,0:T(1,128)S(1)} %collective-permute-done.1, ...), kind=kLoop, calls=%fused_computation.2 | loop fusion | flops 4804800 | bytes 2724480 | tf_op jit(solution)/shard_map/concatenate | solution.py:261
  165.6 10.0 %collective-permute-done.38.refs_5_ = f32[2,8,64,128]{3,2,1,0:T(8,128)S(1)} collective-permute-done((f32[2,8,64,128]{3,2,1,0:T(8,128)S(1)}, f32[2,8,64,128]{3,2,1,0:T(8,128)S(1)}, u32[]{:S(2)}, u32[]{:S(2)}) %collective-permute-start.38) | collective-permute-done | bytes 524320 | tf_op jit(solution)/shard_map/ppermute | solution.py:284
  175.6 1.9 %final.1 = (f32[8,64,128]{2,1,0:T(8,128)}, f32[3,8,64,128]{3,2,1,0:T(8,128)}) custom-call(s32[3]{0:T(128)S(1)} %pad_add_fusion.place, f32[8]{0:T(128)S(1)} %pad_maximum_fusion.18.params, f32[8,64,128]{2,1,0:T(8,128)S(1)} %copy-done.5, s32[8,128,128]{2,1,0:T(8,128)S(1)} %copy-done.3, f32[4,8,64,128]{3,2,1,0:T(8,128)S(1)} %fusion.2.refs_2_, ...), custom_call_target="tpu_custom_call" | custom-call | flops 2621440 | bytes 5242880 | tf_op jit(solution)/shard_map/final/pallas_call | solution.py:388
  (128 shorter events, 43.1 us)
Async XLA Ops:
  9.1 11.7 %collective-permute-start.5 = (f32[2,8,64,128]{3,2,1,0:T(8,128)S(1)}, f32[2,8,64,128]{3,2,1,0:T(8,128)S(1)}, u32[]{:S(2)}, u32[]{:S(2)}) collective-permute-start(f32[2,8,64,128]{3,2,1,0:T(8,128)S(1)} %get-tuple-element.43), channel_id=1, source_target_pairs={{0,16},{16,0},{1,17},{17,1},{2,18},{18,2},{3,19},{19,3},{4,20},{20... | collective-permute-start | bytes 1572872 | tf_op jit(solution)/shard_map/ppermute | solution.py:284
  9.4 14.1 %collective-permute-start.6 = (f32[2,8,64,128]{3,2,1,0:T(8,128)S(1)}, f32[2,8,64,128]{3,2,1,0:T(8,128)S(1)}, u32[]{:S(2)}, u32[]{:S(2)}) collective-permute-start(f32[2,8,64,128]{3,2,1,0:T(8,128)S(1)} %get-tuple-element.42.refs_0_), channel_id=1, source_target_pairs={{0,1},{1,0},{2,3},{3,2},{4,5},{5,4},{6,7},{7,6},{8,9},{9,8},{10,11... | collective-permute-start | bytes 1572872 | tf_op jit(solution)/shard_map/ppermute | solution.py:284
  29.9 7.9 %collective-permute-start.9 = (f32[16,16,128]{2,1,0:T(8,128)S(1)}, f32[16,16,128]{2,1,0:T(8,128)S(1)}, u32[]{:S(2)}, u32[]{:S(2)}) collective-permute-start(f32[16,16,128]{2,1,0:T(8,128)S(1)} %get-tuple-element.46), channel_id=1, source_target_pairs={{0,4},{1,5},{2,6},{3,7},{4,0},{5,1},{6,2},{7,3},{8,12},{9,13},{10,... | collective-permute-start | bytes 393224 | tf_op jit(solution)/shard_map/ppermute | solution.py:284
  30.1 9.3 %collective-permute-start.10 = (f32[16,16,128]{2,1,0:T(8,128)S(1)}, f32[16,16,128]{2,1,0:T(8,128)S(1)}, u32[]{:S(2)}, u32[]{:S(2)}) collective-permute-start(f32[16,16,128]{2,1,0:T(8,128)S(1)} %get-tuple-element.47), channel_id=1, source_target_pairs={{0,6},{1,7},{2,4},{3,5},{4,2},{5,3},{6,0},{7,1},{8,14},{9,15},{10,... | collective-permute-start | bytes 393224 | tf_op jit(solution)/shard_map/ppermute | solution.py:284
  31.3 9.6 %collective-permute-start.11 = (f32[16,16,128]{2,1,0:T(8,128)S(1)}, f32[16,16,128]{2,1,0:T(8,128)S(1)}, u32[]{:S(2)}, u32[]{:S(2)}) collective-permute-start(f32[16,16,128]{2,1,0:T(8,128)S(1)} %get-tuple-element.48), channel_id=1, source_target_pairs={{0,8},{1,9},{2,10},{3,11},{4,12},{5,13},{6,14},{7,15},{8,0},{9,1},... | collective-permute-start | bytes 393224 | tf_op jit(solution)/shard_map/ppermute | solution.py:284
  33.6 15.0 %collective-permute-start.12 = (f32[16,16,128]{2,1,0:T(8,128)S(1)}, f32[16,16,128]{2,1,0:T(8,128)S(1)}, u32[]{:S(2)}, u32[]{:S(2)}) collective-permute-start(f32[16,16,128]{2,1,0:T(8,128)S(1)} %get-tuple-element.49), channel_id=1, source_target_pairs={{0,10},{1,11},{2,8},{3,9},{4,14},{5,15},{6,12},{7,13},{8,2},{9,3},... | collective-permute-start | bytes 393224 | tf_op jit(solution)/shard_map/ppermute | solution.py:284
  36.4 16.3 %collective-permute-start.13 = (f32[16,16,128]{2,1,0:T(8,128)S(1)}, f32[16,16,128]{2,1,0:T(8,128)S(1)}, u32[]{:S(2)}, u32[]{:S(2)}) collective-permute-start(f32[16,16,128]{2,1,0:T(8,128)S(1)} %get-tuple-element.50), channel_id=1, source_target_pairs={{0,12},{1,13},{2,14},{3,15},{4,8},{5,9},{6,10},{7,11},{8,4},{9,5},... | collective-permute-start | bytes 393224 | tf_op jit(solution)/shard_map/ppermute | solution.py:284
  37.8 19.0 %collective-permute-start.14 = (f32[16,16,128]{2,1,0:T(8,128)S(1)}, f32[16,16,128]{2,1,0:T(8,128)S(1)}, u32[]{:S(2)}, u32[]{:S(2)}) collective-permute-start(f32[16,16,128]{2,1,0:T(8,128)S(1)} %get-tuple-element.51), channel_id=1, source_target_pairs={{0,14},{1,15},{2,12},{3,13},{4,10},{5,11},{6,8},{7,9},{8,6},{9,7},... | collective-permute-start | bytes 393224 | tf_op jit(solution)/shard_map/ppermute | solution.py:284
  39.4 17.4 %collective-permute-start.22 = (f32[16,16,128]{2,1,0:T(8,128)S(1)}, f32[16,16,128]{2,1,0:T(8,128)S(1)}, u32[]{:S(2)}, u32[]{:S(2)}) collective-permute-start(f32[16,16,128]{2,1,0:T(8,128)S(1)} %get-tuple-element.61), channel_id=1, source_target_pairs={{0,2},{1,3},{2,0},{3,1},{4,6},{5,7},{6,4},{7,5},{8,10},{9,11},{10,... | collective-permute-start | bytes 393224 | tf_op jit(solution)/shard_map/ppermute | solution.py:284
  40.9 17.6 %collective-permute-start.23 = (f32[16,16,128]{2,1,0:T(8,128)S(1)}, f32[16,16,128]{2,1,0:T(8,128)S(1)}, u32[]{:S(2)}, u32[]{:S(2)}) collective-permute-start(f32[16,16,128]{2,1,0:T(8,128)S(1)} %get-tuple-element.62), channel_id=1, source_target_pairs={{0,4},{1,5},{2,6},{3,7},{4,0},{5,1},{6,2},{7,3},{8,12},{9,13},{10,... | collective-permute-start | bytes 393224 | tf_op jit(solution)/shard_map/ppermute | solution.py:284
  48.6 22.0 %collective-permute-start.24 = (f32[16,16,128]{2,1,0:T(8,128)S(1)}, f32[16,16,128]{2,1,0:T(8,128)S(1)}, u32[]{:S(2)}, u32[]{:S(2)}) collective-permute-start(f32[16,16,128]{2,1,0:T(8,128)S(1)} %get-tuple-element.63), channel_id=1, source_target_pairs={{0,6},{1,7},{2,4},{3,5},{4,2},{5,3},{6,0},{7,1},{8,14},{9,15},{10,... | collective-permute-start | bytes 393224 | tf_op jit(solution)/shard_map/ppermute | solution.py:284
  52.7 19.2 %collective-permute-start.25 = (f32[16,16,128]{2,1,0:T(8,128)S(1)}, f32[16,16,128]{2,1,0:T(8,128)S(1)}, u32[]{:S(2)}, u32[]{:S(2)}) collective-permute-start(f32[16,16,128]{2,1,0:T(8,128)S(1)} %get-tuple-element.64), channel_id=1, source_target_pairs={{0,8},{1,9},{2,10},{3,11},{4,12},{5,13},{6,14},{7,15},{8,0},{9,1},... | collective-permute-start | bytes 393224 | tf_op jit(solution)/shard_map/ppermute | solution.py:284
  56.8 19.3 %collective-permute-start.26 = (f32[16,16,128]{2,1,0:T(8,128)S(1)}, f32[16,16,128]{2,1,0:T(8,128)S(1)}, u32[]{:S(2)}, u32[]{:S(2)}) collective-permute-start(f32[16,16,128]{2,1,0:T(8,128)S(1)} %get-tuple-element.65), channel_id=1, source_target_pairs={{0,10},{1,11},{2,8},{3,9},{4,14},{5,15},{6,12},{7,13},{8,2},{9,3},... | collective-permute-start | bytes 393224 | tf_op jit(solution)/shard_map/ppermute | solution.py:284
  56.8 20.5 %collective-permute-start.27 = (f32[16,16,128]{2,1,0:T(8,128)S(1)}, f32[16,16,128]{2,1,0:T(8,128)S(1)}, u32[]{:S(2)}, u32[]{:S(2)}) collective-permute-start(f32[16,16,128]{2,1,0:T(8,128)S(1)} %get-tuple-element.66), channel_id=1, source_target_pairs={{0,12},{1,13},{2,14},{3,15},{4,8},{5,9},{6,10},{7,11},{8,4},{9,5},... | collective-permute-start | bytes 393224 | tf_op jit(solution)/shard_map/ppermute | solution.py:284
  58.5 19.8 %collective-permute-start.28 = (f32[16,16,128]{2,1,0:T(8,128)S(1)}, f32[16,16,128]{2,1,0:T(8,128)S(1)}, u32[]{:S(2)}, u32[]{:S(2)}) collective-permute-start(f32[16,16,128]{2,1,0:T(8,128)S(1)} %get-tuple-element.67), channel_id=1, source_target_pairs={{0,14},{1,15},{2,12},{3,13},{4,10},{5,11},{6,8},{7,9},{8,6},{9,7},... | collective-permute-start | bytes 393224 | tf_op jit(solution)/shard_map/ppermute | solution.py:284
  70.7 22.7 %collective-permute-start.15 = (f32[16,16,128]{2,1,0:T(8,128)S(1)}, f32[16,16,128]{2,1,0:T(8,128)S(1)}, u32[]{:S(2)}, u32[]{:S(2)}) collective-permute-start(f32[16,16,128]{2,1,0:T(8,128)S(1)} %get-tuple-element.53), channel_id=1, source_target_pairs={{0,2},{1,3},{2,0},{3,1},{4,6},{5,7},{6,4},{7,5},{8,10},{9,11},{10,... | collective-permute-start | bytes 393224 | tf_op jit(solution)/shard_map/ppermute | solution.py:284
  72.0 23.0 %collective-permute-start.16 = (f32[16,16,128]{2,1,0:T(8,128)S(1)}, f32[16,16,128]{2,1,0:T(8,128)S(1)}, u32[]{:S(2)}, u32[]{:S(2)}) collective-permute-start(f32[16,16,128]{2,1,0:T(8,128)S(1)} %get-tuple-element.54), channel_id=1, source_target_pairs={{0,4},{1,5},{2,6},{3,7},{4,0},{5,1},{6,2},{7,3},{8,12},{9,13},{10,... | collective-permute-start | bytes 393224 | tf_op jit(solution)/shard_map/ppermute | solution.py:284
  76.1 19.6 %collective-permute-start.17 = (f32[16,16,128]{2,1,0:T(8,128)S(1)}, f32[16,16,128]{2,1,0:T(8,128)S(1)}, u32[]{:S(2)}, u32[]{:S(2)}) collective-permute-start(f32[16,16,128]{2,1,0:T(8,128)S(1)} %get-tuple-element.55), channel_id=1, source_target_pairs={{0,6},{1,7},{2,4},{3,5},{4,2},{5,3},{6,0},{7,1},{8,14},{9,15},{10,... | collective-permute-start | bytes 393224 | tf_op jit(solution)/shard_map/ppermute | solution.py:284
  77.3 19.6 %collective-permute-start.18 = (f32[16,16,128]{2,1,0:T(8,128)S(1)}, f32[16,16,128]{2,1,0:T(8,128)S(1)}, u32[]{:S(2)}, u32[]{:S(2)}) collective-permute-start(f32[16,16,128]{2,1,0:T(8,128)S(1)} %get-tuple-element.56), channel_id=1, source_target_pairs={{0,8},{1,9},{2,10},{3,11},{4,12},{5,13},{6,14},{7,15},{8,0},{9,1},... | collective-permute-start | bytes 393224 | tf_op jit(solution)/shard_map/ppermute | solution.py:284
  78.3 23.3 %collective-permute-start.19 = (f32[16,16,128]{2,1,0:T(8,128)S(1)}, f32[16,16,128]{2,1,0:T(8,128)S(1)}, u32[]{:S(2)}, u32[]{:S(2)}) collective-permute-start(f32[16,16,128]{2,1,0:T(8,128)S(1)} %get-tuple-element.57), channel_id=1, source_target_pairs={{0,10},{1,11},{2,8},{3,9},{4,14},{5,15},{6,12},{7,13},{8,2},{9,3},... | collective-permute-start | bytes 393224 | tf_op jit(solution)/shard_map/ppermute | solution.py:284
  93.4 10.1 %collective-permute-start.20 = (f32[16,16,128]{2,1,0:T(8,128)S(1)}, f32[16,16,128]{2,1,0:T(8,128)S(1)}, u32[]{:S(2)}, u32[]{:S(2)}) collective-permute-start(f32[16,16,128]{2,1,0:T(8,128)S(1)} %get-tuple-element.58), channel_id=1, source_target_pairs={{0,12},{1,13},{2,14},{3,15},{4,8},{5,9},{6,10},{7,11},{8,4},{9,5},... | collective-permute-start | bytes 393224 | tf_op jit(solution)/shard_map/ppermute | solution.py:284
  94.9 9.5 %collective-permute-start.21 = (f32[16,16,128]{2,1,0:T(8,128)S(1)}, f32[16,16,128]{2,1,0:T(8,128)S(1)}, u32[]{:S(2)}, u32[]{:S(2)}) collective-permute-start(f32[16,16,128]{2,1,0:T(8,128)S(1)} %get-tuple-element.59), channel_id=1, source_target_pairs={{0,14},{1,15},{2,12},{3,13},{4,10},{5,11},{6,8},{7,9},{8,6},{9,7},... | collective-permute-start | bytes 393224 | tf_op jit(solution)/shard_map/ppermute | solution.py:284
  96.4 10.7 %collective-permute-start.29 = (f32[16,16,128]{2,1,0:T(8,128)S(1)}, f32[16,16,128]{2,1,0:T(8,128)S(1)}, u32[]{:S(2)}, u32[]{:S(2)}) collective-permute-start(f32[16,16,128]{2,1,0:T(8,128)S(1)} %get-tuple-element.69), channel_id=1, source_target_pairs={{0,2},{1,3},{2,0},{3,1},{4,6},{5,7},{6,4},{7,5},{8,10},{9,11},{10,... | collective-permute-start | bytes 393224 | tf_op jit(solution)/shard_map/ppermute | solution.py:284
  97.5 10.5 %collective-permute-start.30 = (f32[16,16,128]{2,1,0:T(8,128)S(1)}, f32[16,16,128]{2,1,0:T(8,128)S(1)}, u32[]{:S(2)}, u32[]{:S(2)}) collective-permute-start(f32[16,16,128]{2,1,0:T(8,128)S(1)} %get-tuple-element.70), channel_id=1, source_target_pairs={{0,4},{1,5},{2,6},{3,7},{4,0},{5,1},{6,2},{7,3},{8,12},{9,13},{10,... | collective-permute-start | bytes 393224 | tf_op jit(solution)/shard_map/ppermute | solution.py:284
  102.3 8.5 %collective-permute-start.31 = (f32[16,16,128]{2,1,0:T(8,128)}, f32[16,16,128]{2,1,0:T(8,128)}, u32[]{:S(2)}, u32[]{:S(2)}) collective-permute-start(f32[16,16,128]{2,1,0:T(8,128)} %get-tuple-element.71), channel_id=1, source_target_pairs={{0,6},{1,7},{2,4},{3,5},{4,2},{5,3},{6,0},{7,1},{8,14},{9,15},{10,... | collective-permute-start | bytes 393224 | tf_op jit(solution)/shard_map/ppermute | solution.py:284
  104.1 10.4 %collective-permute-start.32 = (f32[16,16,128]{2,1,0:T(8,128)}, f32[16,16,128]{2,1,0:T(8,128)}, u32[]{:S(2)}, u32[]{:S(2)}) collective-permute-start(f32[16,16,128]{2,1,0:T(8,128)} %get-tuple-element.72), channel_id=1, source_target_pairs={{0,8},{1,9},{2,10},{3,11},{4,12},{5,13},{6,14},{7,15},{8,0},{9,1},... | collective-permute-start | bytes 393224 | tf_op jit(solution)/shard_map/ppermute | solution.py:284
  105.1 13.9 %collective-permute-start.33 = (f32[16,16,128]{2,1,0:T(8,128)}, f32[16,16,128]{2,1,0:T(8,128)}, u32[]{:S(2)}, u32[]{:S(2)}) collective-permute-start(f32[16,16,128]{2,1,0:T(8,128)} %get-tuple-element.73), channel_id=1, source_target_pairs={{0,10},{1,11},{2,8},{3,9},{4,14},{5,15},{6,12},{7,13},{8,2},{9,3},... | collective-permute-start | bytes 393224 | tf_op jit(solution)/shard_map/ppermute | solution.py:284
  107.8 18.1 %collective-permute-start.34 = (f32[16,16,128]{2,1,0:T(8,128)}, f32[16,16,128]{2,1,0:T(8,128)}, u32[]{:S(2)}, u32[]{:S(2)}) collective-permute-start(f32[16,16,128]{2,1,0:T(8,128)} %get-tuple-element.74), channel_id=1, source_target_pairs={{0,12},{1,13},{2,14},{3,15},{4,8},{5,9},{6,10},{7,11},{8,4},{9,5},... | collective-permute-start | bytes 393224 | tf_op jit(solution)/shard_map/ppermute | solution.py:284
  108.7 22.6 %collective-permute-start.35 = (f32[16,16,128]{2,1,0:T(8,128)}, f32[16,16,128]{2,1,0:T(8,128)}, u32[]{:S(2)}, u32[]{:S(2)}) collective-permute-start(f32[16,16,128]{2,1,0:T(8,128)} %get-tuple-element.75), channel_id=1, source_target_pairs={{0,14},{1,15},{2,12},{3,13},{4,10},{5,11},{6,8},{7,9},{8,6},{9,7},... | collective-permute-start | bytes 393224 | tf_op jit(solution)/shard_map/ppermute | solution.py:284
  141.4 21.1 %collective-permute-start.37 = (f32[2,8,64,128]{3,2,1,0:T(8,128)S(1)}, f32[2,8,64,128]{3,2,1,0:T(8,128)S(1)}, u32[]{:S(2)}, u32[]{:S(2)}) collective-permute-start(f32[2,8,64,128]{3,2,1,0:T(8,128)S(1)} %get-tuple-element.79), channel_id=1, source_target_pairs={{0,1},{1,0},{2,3},{3,2},{4,5},{5,4},{6,7},{7,6},{8,9},{9,8},{10,11... | collective-permute-start | bytes 1572872 | tf_op jit(solution)/shard_map/ppermute | solution.py:284
  153.1 9.5 %collective-permute-start.3 = (f32[4,1,66,128]{3,2,1,0:T(8,128)S(1)}, f32[4,1,66,128]{3,2,1,0:T(8,128)S(1)}, u32[]{:S(2)}, u32[]{:S(2)}) collective-permute-start(f32[4,1,66,128]{3,2,1,0:T(8,128)S(1)} %get-tuple-element.83), channel_id=1, source_target_pairs={{1,0},{2,1},{3,2},{4,3},{5,4},{6,5},{7,6},{8,7},{9,8},{10,9},{11,1... | collective-permute-start | bytes 405512 | tf_op jit(solution)/shard_map/ppermute | solution.py:265
  162.5 13.1 %collective-permute-start.38 = (f32[2,8,64,128]{3,2,1,0:T(8,128)S(1)}, f32[2,8,64,128]{3,2,1,0:T(8,128)S(1)}, u32[]{:S(2)}, u32[]{:S(2)}) collective-permute-start(f32[2,8,64,128]{3,2,1,0:T(8,128)S(1)} %add.52), channel_id=1, source_target_pairs={{0,16},{16,0},{1,17},{17,1},{2,18},{18,2},{3,19},{19,3},{4,20},{20... | collective-permute-start | bytes 1572872 | tf_op jit(solution)/shard_map/ppermute | solution.py:284
  (39 other events, 599.1 us)
where the time goes:
time: 180 us; the launch traced here: 178 us
  waiting for transfers between devices  62 us (34%)
  starting transfers between devices  54.8 us (30%)
  Pallas kernels  37.9 us (21%)
  local copies, waits for them, and re-layouts  17.4 us (10%)
  other arithmetic  3.91 us (2%)
    ppermute x35, waiting for transfers between devices, swap(): return lax.ppermute(x, axis, [(i, i ^ bits) for i in range(count)])  58.8 us
    ppermute x35, starting transfers between devices, swap(): return lax.ppermute(x, axis, [(i, i ^ bits) for i in range(count)])  45 us
    pallas_call x2, Pallas kernels, body(): call(functools.partial(middle_kernel, chips), [sent_shape] * chips, [SMEM...  25.1 us
    unnamed x64, local copies, waits for them, and re-layouts  17.4 us
    pallas_call x2, Pallas kernels, y_adjoint(): call(functools.partial(y_adjoint_kernel, refls, chips, chunks, mate), [(2...  5.81 us
    ppermute x2, starting transfers between devices, with_halo(): lax.ppermute(head, axis, [((i + 1) % count, i) for i in range(ends)])  5.5 us
    ppermute x2, starting transfers between devices, with_halo(): lax.ppermute(tail, axis, [(i, (i + 1) % count) for i in range(ends)])  4.28 us
  transfers between devices with their start and end apart: 39, of which 15 were waited for; matrix products, arithmetic and copies ran while one was open for 2% of the time, Pallas kernels for 17%

commit v1 on v0

v1 whole, which is shorter than its diff:
```python
import functools

import jax
import jax.numpy as jnp
import ml_dtypes
import numpy as np
from jax import lax
from jax.experimental import pallas as pl
from jax.experimental.pallas import tpu as pltpu
from jax.sharding import PartitionSpec as P

STRAIN_WEIGHT = 0.05
EDGE_WEIGHT = 0.05
PIECES = (8, 8)
ORDER = (4, 5, 6, 7, 1, 2, 3)
LATE = (1, 2, 3)
F32 = jnp.float32
BF16 = jnp.bfloat16


def split_table(table):
    high = table.astype(ml_dtypes.bfloat16)
    low = (table - high.astype(np.float64)).astype(ml_dtypes.bfloat16)
    return high, low


def forward_table(freqs, places, length):
    angle = 2.0 * np.pi / length * (freqs[:, None] * places[None, :] % length)
    cosine = np.cos(angle) * length ** (-0.5)
    sine = np.sin(angle) * length ** (-0.5)
    return np.block([[cosine, sine], [-sine, cosine]])


def turn_fits():
    nodes = np.cos(np.pi * (np.arange(400) + 0.5) / 400)
    t = (nodes + 1.0) / 8.0
    r = np.sqrt(t)
    fits = []
    for values, degree in ((np.cos(2 * np.pi * r), 8), (np.sin(2 * np.pi * r) / r, 8)):
        cheb = np.polynomial.chebyshev.Chebyshev.fit(t, values, degree, domain=[0.0, 0.25])
        fits.append([float(c) for c in cheb.convert(kind=np.polynomial.Polynomial).coef])
    return fits


COS_FIT, SIN_FIT = turn_fits()


def series(coefs, t):
    total = jnp.full_like(t, coefs[-1])
    for coef in coefs[-2::-1]:
        total = total * t + coef
    return total


def halves(x):
    high = x.astype(BF16)
    return high, (x - high.astype(F32)).astype(BF16)


def dot(a, b):
    return jnp.dot(a, b, preferred_element_type=F32)


def dot_pairs(a, b):
    return dot(a[0], b[0]) + (dot(a[0], b[1]) + dot(a[1], b[0]))


SMEM = pl.BlockSpec(memory_space=pltpu.SMEM)


def whole(shape):
    return pl.BlockSpec(tuple(shape), lambda step, rank=len(shape): (0,) * rank)


def call(kernel, outs, scalars, operands, scratch, flops, name, blocks=None):
    blocks = blocks or {}
    specs = [SMEM] * len(scalars)
    moved = 4 * sum(int(np.prod(shape)) for shape in outs)
    for at, operand in enumerate(operands):
        if at in blocks:
            shape, index = blocks[at]
            specs.append(pl.BlockSpec(shape, lambda step, index=index: index))
        else:
            shape = operand.shape
            specs.append(whole(shape))
        moved += int(np.prod(shape)) * operand.dtype.itemsize
    return pl.pallas_call(
        kernel,
        grid=(1,),
        out_shape=[jax.ShapeDtypeStruct(shape, F32) for shape in outs],
        in_specs=specs,
        out_specs=[whole(shape) for shape in outs],
        scratch_shapes=scratch,
        compiler_params=pltpu.CompilerParams(vmem_limit_bytes=48 * 1024 * 1024),
        cost_estimate=pl.CostEstimate(flops=int(flops), bytes_accessed=int(moved), transcendentals=0),
        name=name,
    )(*scalars, *operands)


def edges_kernel(place, amp, disp, sup, x_mate, x_out, y_first, y_last):
    planes, rows, depth = amp.shape
    first = pl.multiple_of(place[2] * rows, rows)
    core = place[1]

    def field(f, p):
        if f == 0:
            return sup[p, pl.ds(first, rows), :].astype(F32) * amp[p]
        return disp[f - 1, p]

    for f in range(4):
        x_mate[f] = field(f, (1 - core) * (planes - 1))
        x_out[f] = field(f, core * (planes - 1))
        for p in range(planes):
            value = field(f, p)
            y_first[f, p : p + 1, :] = value[:1]
            y_last[f, p : p + 1, :] = value[rows - 1 :]


def laplace_kernel(place, amp, disp, sup, x_mate, x_out, y_before, y_after, out):
    planes, rows, depth = amp.shape
    first = pl.multiple_of(place[2] * rows, rows)
    low_core = place[1] == 0
    row = lax.broadcasted_iota(jnp.int32, (rows, depth), 0)
    lane = lax.broadcasted_iota(jnp.int32, (rows, depth), 1)

    def field(f, p):
        if f == 0:
            return sup[p, pl.ds(first, rows), :].astype(F32) * amp[p]
        return disp[f - 1, p]

    for f in range(4):
        for p in range(planes):
            centre = field(f, p)
            beside = jnp.where(low_core, x_out[f], x_mate[f]) if p == 0 else field(f, p - 1)
            beside = beside + (jnp.where(low_core, x_mate[f], x_out[f]) if p == planes - 1 else field(f, p + 1))
            beside = beside + jnp.where(row == 0, y_before[f, p : p + 1, :], pltpu.roll(centre, 1, 0))
            beside = beside + jnp.where(row == rows - 1, y_after[f, p : p + 1, :], pltpu.roll(centre, rows - 1, 0))
            beside = beside + jnp.where(lane == 0, 0.0, pltpu.roll(centre, 1, 1))
            beside = beside + jnp.where(lane == depth - 1, 0.0, pltpu.roll(centre, depth - 1, 1))
            out[f, p] = 6.0 * centre - beside


def object_kernel(which, grid, place, params, amp, disp, sup, *outs):
    planes, rows, depth = amp.shape
    first = pl.multiple_of(place[2] * rows, rows)
    zed = lax.broadcasted_iota(jnp.int32, (rows, depth), 1).astype(F32) * (1.0 / grid)
    each = len(outs) // len(which)
    portion = planes // (each - 1)

    for part in range(each - 1):

        def plane(i, carry, part=part):
            p = part * portion + i
            weight = sup[p, pl.ds(first, rows), :].astype(F32) * amp[p]
            parts = [disp[0, p], disp[1, p], disp[2, p]]
            for at, k in enumerate(which):
                phase = params[4 * k] * parts[0] + params[4 * k + 1] * parts[1] + params[4 * k + 2] * parts[2]
                shifted = params[4 * k + 3] * zed
                turns = phase * (0.5 / np.pi) + (shifted - jnp.floor(shifted))
                turns = turns - jnp.floor(turns + 0.5)
                square = turns * turns
                cosine = series(COS_FIT, square)
                sine = series(SIN_FIT, square) * turns
                outs[each * at][0, p] = cosine
                outs[each * at][1, p] = sine
                outs[each * at + 1 + part][0, i] = weight * cosine
                outs[each * at + 1 + part][1, i] = weight * sine
            return carry

        lax.fori_loop(0, portion, plane, 0)


def y_forward_kernel(refls, chips, splits, place, *refs):
    count = 2 * refls * splits
    parts, (high, low), outs = refs[:count], refs[count : count + 2], refs[count + 2 : -2]
    hold_high, hold_low = refs[-2:]
    chip, core, refl = place[0], place[1], place[2]
    portion, rows, depth = parts[0].shape[1:]
    planes = portion * splits
    length = rows * refls
    share = high.shape[1] // chips

    def order(table):
        return jnp.concatenate(
            [table[core, pl.ds(pl.multiple_of((chip ^ k) * share, share), share), :] for k in range(chips)], axis=0
        )

    table = (order(high), order(low))
    for src in range(2):
        for p in range(planes):
            lane = (src * planes + p) * depth
            for c in range(2):
                for k in range(refls):
                    part = parts[(src * refls + k) * splits + p // portion]
                    one, two = halves(part[c, p % portion])
                    at = pl.ds(pl.multiple_of(c * length + (refl ^ k) * rows, rows), rows)
                    hold_high[at, lane : lane + depth] = one
                    hold_low[at, lane : lane + depth] = two
    for src in range(2):
        for p in range(0, planes, 2):
            lane = (src * planes + p) * depth
            operand = (hold_high[:, lane : lane + 2 * depth], hold_low[:, lane : lane + 2 * depth])
            result = dot_pairs(table, operand)
            base = (core if src == 0 else 1 - core) * planes + p
            for k in range(chips):
                for j in range(2):
                    outs[k][base + j] = result[k * share : (k + 1) * share, j * depth : (j + 1) * depth]


def middle_kernel(chips, skip, place, *refs):
    got, intensity = refs[:chips], refs[chips]
    fwd = (refs[chips + 1][...], refs[chips + 2][...])
    bwd = (refs[chips + 3][...], refs[chips + 4][...])
    outs = refs[chips + 5 : -2]
    gather, scatter = refs[-2:]
    chip = place[0]
    group, width, depth = got[0].shape
    rows = width // 2
    edge = group * chips
    grid = 2 * edge
    batch = gather.shape[1] // depth

    def place_of(c, k):
        return pl.ds(pl.multiple_of(c * edge + (chip ^ k) * group, group), group)

    for key in range(0, rows, batch):
        for k in range(chips):
            for c in range(2):
                for j in range(batch):
                    gather[place_of(c, k), j * depth : (j + 1) * depth] = got[k][:, (key + j) * 2 + c, :]
        one = dot_pairs(fwd, halves(gather[...]))
        lines = jnp.concatenate(
            [
                jnp.concatenate([one[c * grid : (c + 1) * grid, j * depth : (j + 1) * depth] for c in range(2)], axis=1)
                for j in range(batch)
            ],
            axis=0,
        )
        spectrum = dot_pairs(halves(lines), bwd)
        real, imag = spectrum[:, :grid], spectrum[:, grid:]
        measured = jnp.concatenate([intensity[0, :, skip + key + j, :] for j in range(batch)], axis=0)
        excess = 4.0 * (real * real + imag * imag - measured)
        residual = jnp.concatenate([excess * real, excess * imag], axis=1)
        back = dot_pairs(halves(residual), fwd)
        lines = jnp.concatenate(
            [
                jnp.concatenate([back[j * grid : (j + 1) * grid, c * depth : (c + 1) * depth] for j in range(batch)], axis=1)
                for c in range(2)
            ],
            axis=0,
        )
        scatter[...] = dot_pairs(bwd, halves(lines))
        for k in range(chips):
            for c in range(2):
                for j in range(batch):
                    outs[k][:, (key + j) * 2 + c, :] = scatter[place_of(c, k), j * depth : (j + 1) * depth]


def y_adjoint_kernel(refls, chips, jobs, place, *refs):
    got, (high, low) = refs[:chips], refs[chips : chips + 2]
    total = refls * len(jobs)
    adds, outs = refs[chips + 2 : -1 - total], refs[-1 - total : -1]
    hold = refs[-1]
    chip, core, refl = place[0], place[1], place[2]
    planes, rows, depth = outs[0].shape[1:]
    width = got[0].shape[1]

    def order(table):
        pieces = []
        for q in range(refls):
            for c in range(2):
                at = pl.multiple_of(((refl ^ q) * 2 + c) * rows, rows)
                pieces.append(table[core, pl.ds(at, rows), :])
        return jnp.concatenate(pieces, axis=0)

    table = (order(high), order(low))
    for job, (mate, first) in enumerate(jobs):
        base = (1 - core if mate else core) * (got[0].shape[0] // 2) + first
        for p in range(planes):
            lane = (job * planes + p) * depth
            for k in range(chips):
                at = pl.ds(pl.multiple_of((chip ^ k) * width, width), width)
                hold[at, lane : lane + depth] = got[k][base + p]
    for job in range(len(jobs)):
        for p in range(0, planes, 2):
            lane = (job * planes + p) * depth
            result = dot_pairs(table, halves(hold[:, lane : lane + 2 * depth]))
            for k in range(refls):
                for c in range(2):
                    at = (k * 2 + c) * rows
                    for j in range(2):
                        value = result[at : at + rows, j * depth : (j + 1) * depth]
                        if adds:
                            value = value + adds[job * refls + k][c, p + j]
                        outs[job * refls + k][c, p + j] = value


def add_kernel(a, b, out):
    out[...] = a[...] + b[...]


def final_kernel(refls, splits, place, params, *refs):
    amp, sup, lapped = refs[:3]
    own, mate = refs[3 : 3 + splits], refs[3 + splits : 3 + 2 * splits]
    others = refs[3 + 2 * splits : 3 + (1 + refls) * splits]
    phases = refs[3 + (1 + refls) * splits : -2]
    out_amp, out_disp = refs[-2:]
    planes, rows, depth = amp.shape
    first = pl.multiple_of(place[2] * rows, rows)
    portion = planes // splits

    for part in range(splits):

        def plane(i, carry, part=part):
            p = part * portion + i
            mask = sup[p, pl.ds(first, rows), :].astype(F32)
            weight = mask * amp[p]
            total = jnp.zeros((rows, depth), F32)
            moved = [jnp.zeros((rows, depth), F32) for _ in range(3)]
            for k in range(refls):
                if k == 0:
                    real, imag = [own[part][c, i] + mate[part][c, i] for c in range(2)]
                else:
                    real, imag = [others[(k - 1) * splits + part][c, i] for c in range(2)]
                cosine, sine = phases[k][0, p], phases[k][1, p]
                total = total + (real * cosine + imag * sine)
                across = weight * (imag * cosine - real * sine)
                moved = [m + params[4 * k + c] * across for c, m in enumerate(moved)]
            out_amp[p] = mask * total + (2.0 * EDGE_WEIGHT) * (mask * lapped[0, p])
            for c in range(3):
                out_disp[c, p] = moved[c] + (2.0 * STRAIN_WEIGHT) * lapped[c + 1, p]
            return carry

        lax.fori_loop(0, portion, plane, 0)


def swap(x, axis, bits):
    count = lax.axis_size(axis)
    return lax.ppermute(x, axis, [(i, i ^ bits) for i in range(count)])


def swap_outward(x, axis):
    count = lax.axis_size(axis)
    return lax.ppermute(x, axis, [pair for i in range(1, count - 1, 2) for pair in ((i, i + 1), (i + 1, i))])


def step_up(x, axis):
    return lax.ppermute(x, axis, [(i, i + 1) for i in range(lax.axis_size(axis) - 1)])


def step_down(x, axis):
    return lax.ppermute(x, axis, [(i + 1, i) for i in range(lax.axis_size(axis) - 1)])


def after(value, *first):
    return lax.optimization_barrier((value, first))[0]


def body(amplitude, displacement, support, miller, shift_kz, intensity):
    refls = lax.axis_size("refl")
    slabs = lax.axis_size("slab")
    chips = slabs // 2
    planes, rows, depth = amplitude.shape
    edge = planes * slabs
    grid = 2 * edge
    keys = grid // slabs
    pieces = PIECES if sum(PIECES) == keys else (keys,)
    splits = 2 if planes % 8 == 0 else 1
    portion = planes // splits
    group = 2 * planes
    refl = lax.axis_index("refl")
    slab = lax.axis_index("slab")
    place = jnp.stack([slab // 2, slab % 2, refl]).astype(jnp.int32)
    cells = planes * rows * depth
    part_shape = (2, portion, rows, depth)

    every, inner = np.arange(grid), np.arange(edge)
    table = forward_table(every, inner, grid)
    constants = [jnp.asarray(t) for one in (table, table.T) for t in split_table(one)]
    by_key = table.reshape(2, chips, 2, keys, 2 * edge).transpose(2, 1, 3, 0, 4)

    def y_tables(at):
        first, count = sum(pieces[:at]), pieces[at]
        some = by_key[:, :, first : first + count].reshape(2, chips * count * 2, 2 * edge)
        fwd = [jnp.asarray(t) for t in split_table(some)]
        some = some.reshape(2, chips * count * 2, 2, refls, rows)
        some = some.transpose(0, 3, 2, 4, 1).reshape(2, 2 * edge, chips * count * 2)
        return fwd, [jnp.asarray(t) for t in split_table(some)]

    own_params = jnp.concatenate([miller[0].astype(F32), shift_kz.astype(F32)])
    fields = (amplitude, displacement, support)
    edges = call(
        edges_kernel, [(4, rows, depth)] * 2 + [(4, planes, depth)] * 2, [place], fields, [], cells, "edges"
    )

    def make(params, which, parts):
        made = call(
            functools.partial(object_kernel, which, grid),
            ([(2, planes, rows, depth)] + [(2, planes // parts, rows, depth)] * parts) * len(which),
            [place, params],
            fields,
            [],
            50 * len(which) * cells,
            "object",
        )
        return [made[i * (parts + 1) : (i + 1) * (parts + 1)] for i in range(len(which))]

    ((own_phase, *own_parts),) = make(own_params, [0], splits)
    params = jnp.concatenate([own_params] + [swap(own_params, "refl", k) for k in range(1, refls)])
    params = after(params, own_parts, edges)
    made = make(params, list(range(1, refls)), splits)
    phases = [own_phase] + [one[0] for one in made]
    own_mates = [swap(x, "slab", 1) for x in own_parts]
    held = [[swap(one[1], "refl", k + 1) for k, one in enumerate(made)]]
    if refls == 2:
        facing = swap(jnp.where(refl == 0, edges[3], edges[2]), "refl", 1)
        nothing = jnp.zeros_like(facing)
        y_halos = (jnp.where(refl == 0, nothing, facing), jnp.where(refl == 0, facing, nothing))
    else:
        y_halos = (step_up(edges[3], "refl"), step_down(edges[2], "refl"))
    halos = (swap(edges[0], "slab", 1), swap_outward(edges[1], "slab"), *y_halos)
    for part in range(1, splits):
        held.append([swap(after(one[1 + part], halos), "refl", k + 1) for k, one in enumerate(made)])

    held = [x for part in zip(*held) for x in part]
    mates = [swap(x, "slab", 1) for x in held]

    def y_forward(at):
        return call(
            functools.partial(y_forward_kernel, refls, chips, splits),
            [(group, 2 * pieces[at], depth)] * chips,
            [place],
            (*own_parts, *held, *own_mates, *mates, *y_tables(at)[0]),
            [pltpu.VMEM((2 * edge, group * depth), BF16)] * 2,
            6 * group * depth * 2 * edge * chips * pieces[at] * 2,
            "y_forward",
        )

    def middle(at, got):
        first, count = sum(pieces[:at]), pieces[at]
        block = (group, 2 * count, depth)
        held = min(keys, max(8, count))
        return call(
            functools.partial(middle_kernel, chips, first % held),
            [block] * chips,
            [place],
            (*got, intensity, *constants),
            [pltpu.VMEM((2 * edge, min(count, 4) * depth), F32)] * 2,
            6 * count * (2 * edge * 2 * grid * depth * 2 + grid * 2 * depth * 2 * grid * 2),
            "middle",
            {chips: ((1, grid, held, grid), (0, 0, first // held, 0))},
        )

    def y_adjoint(at, got, jobs, adds):
        count = pieces[at]
        made = call(
            functools.partial(y_adjoint_kernel, refls, chips, jobs),
            [part_shape] * (refls * len(jobs)),
            [place],
            (*got, *y_tables(at)[1], *[x for job in adds for x in job]),
            [pltpu.VMEM((chips * 2 * count, len(jobs) * portion * depth), F32)],
            6 * len(jobs) * portion * depth * 2 * edge * chips * 2 * count,
            "y_adjoint",
        )
        return [made[i * refls : (i + 1) * refls] for i in range(len(jobs))]

    def cross(sends, late=(), first=()):
        got = [sends[0]] + [None] * (chips - 1)
        for k in ORDER if len(ORDER) == chips - 1 else range(1, chips):
            got[k] = swap(after(sends[k], first) if k in late else sends[k], "slab", 2 * k)
        return got

    forward = [y_forward(at) for at in range(len(pieces))]
    arrived = cross(forward[0])
    (lapped,) = call(laplace_kernel, [(4, planes, rows, depth)], [place], (*fields, *halos), [], 30 * cells, "laplace")
    jobs = [(mate, part * portion) for part in range(splits) for mate in (True, False)]
    adds = []
    for at in range(len(pieces)):
        backs = middle(at, arrived)
        if at + 1 < len(pieces):
            arrived = cross(forward[at + 1], LATE, backs)
        returned = cross(backs)
        if at + 1 < len(pieces):
            adds = y_adjoint(at, returned, jobs, adds)
    own, mates, others = [], [], [[] for _ in range(1, refls)]
    mate_jobs = [job for job in range(len(jobs)) if jobs[job][0]]
    mine_jobs = [job for job in range(len(jobs)) if not jobs[job][0]]
    for_mate = y_adjoint(at, returned, [jobs[i] for i in mate_jobs], [adds[i] for i in mate_jobs if adds])
    mine = y_adjoint(at, returned, [jobs[i] for i in mine_jobs], [adds[i] for i in mine_jobs if adds])
    for part in range(splits):
        from_mate = [swap(x, "slab", 1) for x in for_mate[part]]
        own.append(mine[part][0])
        mates.append(from_mate[0])
        for k in range(1, refls):
            (total,) = call(add_kernel, [part_shape], [], (mine[part][k], from_mate[k]), [], 2 * cells, "add")
            others[k - 1].append(swap(total, "refl", k))
    others = [x for one in others for x in one]

    return tuple(
        call(
            functools.partial(final_kernel, refls, splits),
            [(planes, rows, depth), (3, planes, rows, depth)],
            [place, params],
            (amplitude, support, lapped, *own, *mates, *others, *phases),
            [],
            20 * refls * cells,
            "final",
        )
    )


def solution(mesh):
    placed = (
        P("slab", "refl", None),
        P(None, "slab", "refl", None),
        P("slab", None, None),
        P("refl", None),
        P("refl"),
        P("refl", None, "slab", None),
    )
    return jax.shard_map(
        body,
        mesh=mesh,
        in_specs=placed,
        out_specs=(P("slab", "refl", None), P(None, "slab", "refl", None)),
        check_vma=False,
    )
```

time: 180 us -> 157 us (0.87)
  local copies, waits for them, and re-layouts: 17.4 us -> 3.2 us
  starting transfers between devices: 54.8 us -> 47.5 us
  waiting for transfers between devices: 62 us -> 66.1 us
  other arithmetic: 3.91 us -> 0.9 us
    unnamed x64 -> x36, local copies, waits for them, and re-layouts: 17.4 us -> 3.2 us
    ppermute x4 -> x1, starting transfers between devices: 9.78 us -> 3 us  [swap_outward(): lax.ppermute(x, axis, [pair for i in range(1, count - 1, 2) for pair in (...]
    ppermute x35 -> x43, waiting for transfers between devices: 58.8 us -> 63.9 us  [swap(): return lax.ppermute(x, axis, [(i, i ^ bits) for i in range(count)])]
    concatenate x3 -> x0, other arithmetic: 2.16 us -> none  [the longest x2 2.13 us: with_halo(): jnp.concatenate([lax.ppermute(tail, axis, [(i, (i + 1) % count) for i in...]
    pallas_call x9 -> x14, Pallas kernels: 37.9 us -> 36.5 us  [call(): pl.pallas_call(kernel, grid=(1,), out_shape=[jax.ShapeDtypeStruct(shape,...]
    ppermute x35 -> x43, starting transfers between devices: 45 us -> 44.5 us  [swap(): return lax.ppermute(x, axis, [(i, i ^ bits) for i in range(count)])]
  transfers between devices with their start and end apart: 39 -> 44, of which waited for: 15 -> 16; matrix products, arithmetic and copies ran while one was open for 2% -> 0% of each run, Pallas kernels for 17% -> 20%
where the time goes in v1:
time: 157 us; the launch traced here: 156 us
  waiting for transfers between devices  66.1 us (42%)
  starting transfers between devices  47.5 us (30%)
  Pallas kernels  36.5 us (23%)
  local copies, waits for them, and re-layouts  3.2 us (2%)
  between operations  1.6 us (1%)
    ppermute x43, waiting for transfers between devices, swap(): return lax.ppermute(x, axis, [(i, i ^ bits) for i in range(count)])  63.9 us
    ppermute x43, starting transfers between devices, swap(): return lax.ppermute(x, axis, [(i, i ^ bits) for i in range(count)])  44.5 us
    pallas_call x14, Pallas kernels, call(): pl.pallas_call(kernel, grid=(1,), out_shape=[jax.ShapeDtypeStruct(shape,...  36.5 us
    unnamed x36, local copies, waits for them, and re-layouts  3.2 us
  transfers between devices with their start and end apart: 44, of which 16 were waited for; matrix products, arithmetic and copies ran while one was open for 0% of the time, Pallas kernels for 20%

profile of v1, /device:TPU:13, one launch (start us, length us, event | category | flops | bytes accessed | tf_op | source)
XLA Modules:
  0.0 155.7 jit_solution(6011213915971791878)
XLA Ops:
  6.1 1.3 collective-permute-start.3
  8.7 3.0 %collective-permute-start.2 = (f32[4,64,128]{2,1,0:T(8,128)S(1)}, f32[4,64,128]{2,1,0:T(8,128)S(1)}, u32[]{:S(2)}, u32[]{:S(2)}) collective-permute-start(f32[4,64,128]{2,1,0:T(8,128)S(1)} %get-tuple-element.68), channel_id=1, source_target_pairs={{1,2},{2,1},{3,4},{4,3},{5,6},{6,5},{7,8},{8,7},{9,10},{10,9},{11,... | collective-permute-start | bytes 393224 | tf_op jit(solution)/shard_map/ppermute | solution.py:344
  14.1 2.2 %collective-permute-done.2.x_out = f32[4,64,128]{2,1,0:T(8,128)S(1)} collective-permute-done((f32[4,64,128]{2,1,0:T(8,128)S(1)}, f32[4,64,128]{2,1,0:T(8,128)S(1)}, u32[]{:S(2)}, u32[]{:S(2)}) %collective-permute-start.2) | collective-permute-done | bytes 131104 | tf_op jit(solution)/shard_map/ppermute | solution.py:344
  17.1 4.3 %collective-permute-done.4.refs_2_ = f32[2,4,64,128]{3,2,1,0:T(8,128)S(1)} collective-permute-done((f32[2,4,64,128]{3,2,1,0:T(8,128)S(1)}, f32[2,4,64,128]{3,2,1,0:T(8,128)S(1)}, u32[]{:S(2)}, u32[]{:S(2)}) %collective-permute-start.4) | collective-permute-done | bytes 262176 | tf_op jit(solution)/shard_map/ppermute | solution.py:339
  21.4 2.1 %collective-permute-start.8 = (f32[2,4,64,128]{3,2,1,0:T(8,128)S(1)}, f32[2,4,64,128]{3,2,1,0:T(8,128)S(1)}, u32[]{:S(2)}, u32[]{:S(2)}) collective-permute-start(f32[2,4,64,128]{3,2,1,0:T(8,128)S(1)} %collective-permute-done.4.refs_2_), channel_id=1, source_target_pairs={{0,1},{1,0},{2,3},{3,2},{4,5},{5,4},{6,7},{7,6},{8,9},{9,8},{10,11... | collective-permute-start | bytes 786440 | tf_op jit(solution)/shard_map/ppermute | solution.py:339
  23.4 3.6 %collective-permute-done.5.refs_3_ = f32[2,4,64,128]{3,2,1,0:T(8,128)S(1)} collective-permute-done((f32[2,4,64,128]{3,2,1,0:T(8,128)S(1)}, f32[2,4,64,128]{3,2,1,0:T(8,128)S(1)}, u32[]{:S(2)}, u32[]{:S(2)}) %collective-permute-start.5) | collective-permute-done | bytes 262176 | tf_op jit(solution)/shard_map/ppermute | solution.py:339
  29.4 1.8 %y_forward.3 = (f32[16,16,128]{2,1,0:T(8,128)S(1)}, f32[16,16,128]{2,1,0:T(8,128)S(1)}, f32[16,16,128]{2,1,0:T(8,128)S(1)}, f32[16,16,128]{2,1,0:T(8,128)S(1)}, ...) custom-call(s32[3]{0:T(128)S(1)} %pad_add_fusion.place, ...), custom_call_target="tpu_custom_call" | custom-call | flops 402653184 | bytes 3407872 | tf_op jit(solution)/shard_map/y_forward/pallas_call | solution.py:87
  32.6 1.3 collective-permute-start.12
  33.9 2.3 %collective-permute-start.13 = (f32[16,16,128]{2,1,0:T(8,128)S(1)}, f32[16,16,128]{2,1,0:T(8,128)S(1)}, u32[]{:S(2)}, u32[]{:S(2)}) collective-permute-start(f32[16,16,128]{2,1,0:T(8,128)S(1)} %get-tuple-element.81), channel_id=1, source_target_pairs={{0,8},{1,9},{2,10},{3,11},{4,12},{5,13},{6,14},{7,15},{8,0},{9,1},... | collective-permute-start | bytes 393224 | tf_op jit(solution)/shard_map/ppermute | solution.py:339
  38.6 1.8 %y_forward.2 = (f32[16,16,128]{2,1,0:T(8,128)S(1)}, f32[16,16,128]{2,1,0:T(8,128)S(1)}, f32[16,16,128]{2,1,0:T(8,128)S(1)}, f32[16,16,128]{2,1,0:T(8,128)S(1)}, ...) custom-call(s32[3]{0:T(128)S(1)} %pad_add_fusion.place, ...), custom_call_target="tpu_custom_call" | custom-call | flops 402653184 | bytes 3407872 | tf_op jit(solution)/shard_map/y_forward/pallas_call | solution.py:87
  40.4 1.5 collective-permute-done.12.refs_3_
  41.8 3.4 %collective-permute-start.20 = (f32[16,16,128]{2,1,0:T(8,128)S(1)}, f32[16,16,128]{2,1,0:T(8,128)S(1)}, u32[]{:S(2)}, u32[]{:S(2)}) collective-permute-start(f32[16,16,128]{2,1,0:T(8,128)S(1)} %get-tuple-element.98), channel_id=1, source_target_pairs={{0,8},{1,9},{2,10},{3,11},{4,12},{5,13},{6,14},{7,15},{8,0},{9,1},... | collective-permute-start | bytes 393224 | tf_op jit(solution)/shard_map/ppermute | solution.py:339
  45.2 12.3 %collective-permute-done.14.refs_5_ = f32[16,16,128]{2,1,0:T(8,128)S(1)} collective-permute-done((f32[16,16,128]{2,1,0:T(8,128)S(1)}, f32[16,16,128]{2,1,0:T(8,128)S(1)}, u32[]{:S(2)}, u32[]{:S(2)}) %collective-permute-start.14) | collective-permute-done | bytes 131104 | tf_op jit(solution)/shard_map/ppermute | solution.py:339
  57.5 2.8 %collective-permute-done.15.refs_6_ = f32[16,16,128]{2,1,0:T(8,128)S(1)} collective-permute-done((f32[16,16,128]{2,1,0:T(8,128)S(1)}, f32[16,16,128]{2,1,0:T(8,128)S(1)}, u32[]{:S(2)}, u32[]{:S(2)}) %collective-permute-start.15) | collective-permute-done | bytes 131104 | tf_op jit(solution)/shard_map/ppermute | solution.py:339
  60.3 2.0 %collective-permute-start.23 = (f32[16,16,128]{2,1,0:T(8,128)S(1)}, f32[16,16,128]{2,1,0:T(8,128)S(1)}, u32[]{:S(2)}, u32[]{:S(2)}) collective-permute-start(f32[16,16,128]{2,1,0:T(8,128)S(1)} %get-tuple-element.101), channel_id=1, source_target_pairs={{0,14},{1,15},{2,12},{3,13},{4,10},{5,11},{6,8},{7,9},{8,6},{9,7},... | collective-permute-start | bytes 393224 | tf_op jit(solution)/shard_map/ppermute | solution.py:339
  62.3 6.8 %collective-permute-done.16.refs_7_ = f32[16,16,128]{2,1,0:T(8,128)S(1)} collective-permute-done((f32[16,16,128]{2,1,0:T(8,128)S(1)}, f32[16,16,128]{2,1,0:T(8,128)S(1)}, u32[]{:S(2)}, u32[]{:S(2)}) %collective-permute-start.16) | collective-permute-done | bytes 131104 | tf_op jit(solution)/shard_map/ppermute | solution.py:339
  69.1 11.5 %middle.2 = (f32[16,16,128]{2,1,0:T(8,128)S(1)}, f32[16,16,128]{2,1,0:T(8,128)S(1)}, f32[16,16,128]{2,1,0:T(8,128)S(1)}, f32[16,16,128]{2,1,0:T(8,128)S(1)}, f32...) custom-call(s32[3]{0:T(128)S(1)} %pad_add_fusion.place, ...), custom_call_target="tpu_custom_call" | custom-call | flops 4831838208 | bytes 5242880 | tf_op jit(solution)/shard_map/middle/pallas_call | solution.py:87
  80.8 2.5 %collective-permute-start.19 = (f32[16,16,128]{2,1,0:T(8,128)S(1)}, f32[16,16,128]{2,1,0:T(8,128)S(1)}, u32[]{:S(2)}, u32[]{:S(2)}) collective-permute-start(f32[16,16,128]{2,1,0:T(8,128)S(1)} %get-tuple-element.97), channel_id=1, source_target_pairs={{0,6},{1,7},{2,4},{3,5},{4,2},{5,3},{6,0},{7,1},{8,14},{9,15},{10,... | collective-permute-start | bytes 393224 | tf_op jit(solution)/shard_map/ppermute | solution.py:339
  84.5 1.5 collective-permute-start.33
  86.0 2.1 %collective-permute-start.34 = (f32[16,16,128]{2,1,0:T(8,128)S(1)}, f32[16,16,128]{2,1,0:T(8,128)S(1)}, u32[]{:S(2)}, u32[]{:S(2)}) collective-permute-start(f32[16,16,128]{2,1,0:T(8,128)S(1)} %get-tuple-element.89), channel_id=1, source_target_pairs={{0,8},{1,9},{2,10},{3,11},{4,12},{5,13},{6,14},{7,15},{8,0},{9,1},... | collective-permute-start | bytes 393224 | tf_op jit(solution)/shard_map/ppermute | solution.py:339
  89.3 2.1 %collective-permute-done.31.refs_1_ = f32[16,16,128]{2,1,0:T(8,128)S(1)} collective-permute-done((f32[16,16,128]{2,1,0:T(8,128)S(1)}, f32[16,16,128]{2,1,0:T(8,128)S(1)}, u32[]{:S(2)}, u32[]{:S(2)}) %collective-permute-start.31) | collective-permute-done | bytes 131104 | tf_op jit(solution)/shard_map/ppermute | solution.py:339
  92.7 11.7 %middle.3 = (f32[16,16,128]{2,1,0:T(8,128)S(1)}, f32[16,16,128]{2,1,0:T(8,128)S(1)}, f32[16,16,128]{2,1,0:T(8,128)S(1)}, f32[16,16,128]{2,1,0:T(8,128)S(1)}, f32...) custom-call(s32[3]{0:T(128)S(1)} %pad_add_fusion.place, ...), custom_call_target="tpu_custom_call" | custom-call | flops 4831838208 | bytes 5242880 | tf_op jit(solution)/shard_map/middle/pallas_call | solution.py:87
  112.4 1.5 collective-permute-start.30
  113.9 1.6 %y_adjoint.3 = (f32[2,4,64,128]{3,2,1,0:T(8,128)S(1)}, f32[2,4,64,128]{3,2,1,0:T(8,128)S(1)}, f32[2,4,64,128]{3,2,1,0:T(8,128)S(1)}, f32[2,4,64,128]{3,2,1,0:T(8...) custom-call(s32[3]{0:T(128)S(1)} %pad_add_fusion.place, ...), custom_call_target="tpu_custom_call" | custom-call | flops 402653184 | bytes 3407872 | tf_op jit(solution)/shard_map/y_adjoint/pallas_call | solution.py:87
  115.5 3.8 %collective-permute-done.28.refs_5_ = f32[16,16,128]{2,1,0:T(8,128)S(1)} collective-permute-done((f32[16,16,128]{2,1,0:T(8,128)S(1)}, f32[16,16,128]{2,1,0:T(8,128)S(1)}, u32[]{:S(2)}, u32[]{:S(2)}) %collective-permute-start.28) | collective-permute-done | bytes 131104 | tf_op jit(solution)/shard_map/ppermute | solution.py:339
  119.4 5.9 %collective-permute-done.29.refs_6_ = f32[16,16,128]{2,1,0:T(8,128)S(1)} collective-permute-done((f32[16,16,128]{2,1,0:T(8,128)S(1)}, f32[16,16,128]{2,1,0:T(8,128)S(1)}, u32[]{:S(2)}, u32[]{:S(2)}) %collective-permute-start.29) | collective-permute-done | bytes 131104 | tf_op jit(solution)/shard_map/ppermute | solution.py:339
  125.3 7.3 %collective-permute-done.30.refs_7_ = f32[16,16,128]{2,1,0:T(8,128)S(1)} collective-permute-done((f32[16,16,128]{2,1,0:T(8,128)S(1)}, f32[16,16,128]{2,1,0:T(8,128)S(1)}, u32[]{:S(2)}, u32[]{:S(2)}) %collective-permute-start.30) | collective-permute-done | bytes 131104 | tf_op jit(solution)/shard_map/ppermute | solution.py:339
  133.7 5.1 %collective-permute-start.40 = (f32[2,4,64,128]{3,2,1,0:T(8,128)S(1)}, f32[2,4,64,128]{3,2,1,0:T(8,128)S(1)}, u32[]{:S(2)}, u32[]{:S(2)}) collective-permute-start(f32[2,4,64,128]{3,2,1,0:T(8,128)S(1)} %get-tuple-element.123), channel_id=1, source_target_pairs={{0,1},{1,0},{2,3},{3,2},{4,5},{5,4},{6,7},{7,6},{8,9},{9,8},{10,11... | collective-permute-start | bytes 786440 | tf_op jit(solution)/shard_map/ppermute | solution.py:339
  141.0 1.3 collective-permute-start.43
  143.6 4.6 %collective-permute-done.41.refs_7_ = f32[2,4,64,128]{3,2,1,0:T(8,128)S(1)} collective-permute-done((f32[2,4,64,128]{3,2,1,0:T(8,128)S(1)}, f32[2,4,64,128]{3,2,1,0:T(8,128)S(1)}, u32[]{:S(2)}, u32[]{:S(2)}) %collective-permute-start.41) | collective-permute-done | bytes 262176 | tf_op jit(solution)/shard_map/ppermute | solution.py:339
  148.2 5.6 %collective-permute-done.43.refs_8_ = f32[2,4,64,128]{3,2,1,0:T(8,128)S(1)} collective-permute-done((f32[2,4,64,128]{3,2,1,0:T(8,128)S(1)}, f32[2,4,64,128]{3,2,1,0:T(8,128)S(1)}, u32[]{:S(2)}, u32[]{:S(2)}) %collective-permute-start.43) | collective-permute-done | bytes 262176 | tf_op jit(solution)/shard_map/ppermute | solution.py:339
  153.8 1.9 %final.1 = (f32[8,64,128]{2,1,0:T(8,128)}, f32[3,8,64,128]{3,2,1,0:T(8,128)}) custom-call(s32[3]{0:T(128)S(1)} %pad_add_fusion.place, f32[8]{0:T(128)S(1)} %pad_maximum_fusion.1.params, f32[8,64,128]{2,1,0:T(8,128)S(1)} %copy-done.5, s32[8,128,128]{2,1,0:T(8,128)S(1)} %copy-done.1, f32[4,8,64,128]{3,2,1,0:T(8,128)S(1)} %laplace.1.refs_2_, ...), custom_call_target="tpu_custom_call" | custom-call | flops 2621440 | bytes 5505024 | tf_op jit(solution)/shard_map/final/pallas_call | solution.py:87
  (112 shorter events, 31.7 us)
Async XLA Ops:
  2.0 10.7 %collective-permute-start = (f32[4]{0:T(128)S(1)}, f32[4]{0:T(128)S(1)}, u32[]{:S(2)}, u32[]{:S(2)}) collective-permute-start(f32[4]{0:T(128)S(1)} %pad_maximum_fusion.params), channel_id=1, source_target_pairs={{0,16},{16,0},{1,17},{17,1},{2,18},{18,2},{3,19},{19,3},{4,20},{20... | collective-permute-start | bytes 56 | tf_op jit(solution)/shard_map/ppermute | solution.py:339
  6.1 8.0 %collective-permute-start.3 = (f32[4,8,128]{2,1,0:T(8,128)S(1)}, f32[4,8,128]{2,1,0:T(8,128)S(1)}, u32[]{:S(2)}, u32[]{:S(2)}) collective-permute-start(f32[4,8,128]{2,1,0:T(8,128)S(1)} %broadcast_select_fusion.2), channel_id=1, source_target_pairs={{0,16},{16,0},{1,17},{17,1},{2,18},{18,2},{3,19},{19,3},{4,20},{20... | collective-permute-start | bytes 49160 | tf_op jit(solution)/shard_map/ppermute | solution.py:339
  8.7 7.7 %collective-permute-start.2 = (f32[4,64,128]{2,1,0:T(8,128)S(1)}, f32[4,64,128]{2,1,0:T(8,128)S(1)}, u32[]{:S(2)}, u32[]{:S(2)}) collective-permute-start(f32[4,64,128]{2,1,0:T(8,128)S(1)} %get-tuple-element.68), channel_id=1, source_target_pairs={{1,2},{2,1},{3,4},{4,3},{5,6},{6,5},{7,8},{8,7},{9,10},{10,9},{11,... | collective-permute-start | bytes 393224 | tf_op jit(solution)/shard_map/ppermute | solution.py:344
  13.8 7.6 %collective-permute-start.4 = (f32[2,4,64,128]{3,2,1,0:T(8,128)S(1)}, f32[2,4,64,128]{3,2,1,0:T(8,128)S(1)}, u32[]{:S(2)}, u32[]{:S(2)}) collective-permute-start(f32[2,4,64,128]{3,2,1,0:T(8,128)S(1)} %get-tuple-element.72), channel_id=1, source_target_pairs={{0,16},{16,0},{1,17},{17,1},{2,18},{18,2},{3,19},{19,3},{4,20},{20... | collective-permute-start | bytes 786440 | tf_op jit(solution)/shard_map/ppermute | solution.py:339
  16.3 10.7 %collective-permute-start.5 = (f32[2,4,64,128]{3,2,1,0:T(8,128)S(1)}, f32[2,4,64,128]{3,2,1,0:T(8,128)S(1)}, u32[]{:S(2)}, u32[]{:S(2)}) collective-permute-start(f32[2,4,64,128]{3,2,1,0:T(8,128)S(1)} %get-tuple-element.74), channel_id=1, source_target_pairs={{0,16},{16,0},{1,17},{17,1},{2,18},{18,2},{3,19},{19,3},{4,20},{20... | collective-permute-start | bytes 786440 | tf_op jit(solution)/shard_map/ppermute | solution.py:339
  16.6 11.7 %collective-permute-start.6 = (f32[2,4,64,128]{3,2,1,0:T(8,128)S(1)}, f32[2,4,64,128]{3,2,1,0:T(8,128)S(1)}, u32[]{:S(2)}, u32[]{:S(2)}) collective-permute-start(f32[2,4,64,128]{3,2,1,0:T(8,128)S(1)} %get-tuple-element.65.refs_0_), channel_id=1, source_target_pairs={{0,1},{1,0},{2,3},{3,2},{4,5},{5,4},{6,7},{7,6},{8,9},{9,8},{10,11... | collective-permute-start | bytes 786440 | tf_op jit(solution)/shard_map/ppermute | solution.py:339
  16.6 11.7 %collective-permute-start.7 = (f32[2,4,64,128]{3,2,1,0:T(8,128)S(1)}, f32[2,4,64,128]{3,2,1,0:T(8,128)S(1)}, u32[]{:S(2)}, u32[]{:S(2)}) collective-permute-start(f32[2,4,64,128]{3,2,1,0:T(8,128)S(1)} %get-tuple-element.66.refs_1_), channel_id=1, source_target_pairs={{0,1},{1,0},{2,3},{3,2},{4,5},{5,4},{6,7},{7,6},{8,9},{9,8},{10,11... | collective-permute-start | bytes 786440 | tf_op jit(solution)/shard_map/ppermute | solution.py:339
  21.4 6.9 %collective-permute-start.8 = (f32[2,4,64,128]{3,2,1,0:T(8,128)S(1)}, f32[2,4,64,128]{3,2,1,0:T(8,128)S(1)}, u32[]{:S(2)}, u32[]{:S(2)}) collective-permute-start(f32[2,4,64,128]{3,2,1,0:T(8,128)S(1)} %collective-permute-done.4.refs_2_), channel_id=1, source_target_pairs={{0,1},{1,0},{2,3},{3,2},{4,5},{5,4},{6,7},{7,6},{8,9},{9,8},{10,11... | collective-permute-start | bytes 786440 | tf_op jit(solution)/shard_map/ppermute | solution.py:339
  32.6 9.3 %collective-permute-start.12 = (f32[16,16,128]{2,1,0:T(8,128)S(1)}, f32[16,16,128]{2,1,0:T(8,128)S(1)}, u32[]{:S(2)}, u32[]{:S(2)}) collective-permute-start(f32[16,16,128]{2,1,0:T(8,128)S(1)} %get-tuple-element.80), channel_id=1, source_target_pairs={{0,6},{1,7},{2,4},{3,5},{4,2},{5,3},{6,0},{7,1},{8,14},{9,15},{10,... | collective-permute-start | bytes 393224 | tf_op jit(solution)/shard_map/ppermute | solution.py:339
  33.9 11.3 %collective-permute-start.13 = (f32[16,16,128]{2,1,0:T(8,128)S(1)}, f32[16,16,128]{2,1,0:T(8,128)S(1)}, u32[]{:S(2)}, u32[]{:S(2)}) collective-permute-start(f32[16,16,128]{2,1,0:T(8,128)S(1)} %get-tuple-element.81), channel_id=1, source_target_pairs={{0,8},{1,9},{2,10},{3,11},{4,12},{5,13},{6,14},{7,15},{8,0},{9,1},... | collective-permute-start | bytes 393224 | tf_op jit(solution)/shard_map/ppermute | solution.py:339
  36.2 21.3 %collective-permute-start.14 = (f32[16,16,128]{2,1,0:T(8,128)S(1)}, f32[16,16,128]{2,1,0:T(8,128)S(1)}, u32[]{:S(2)}, u32[]{:S(2)}) collective-permute-start(f32[16,16,128]{2,1,0:T(8,128)S(1)} %get-tuple-element.82), channel_id=1, source_target_pairs={{0,10},{1,11},{2,8},{3,9},{4,14},{5,15},{6,12},{7,13},{8,2},{9,3},... | collective-permute-start | bytes 393224 | tf_op jit(solution)/shard_map/ppermute | solution.py:339
  37.1 23.2 %collective-permute-start.15 = (f32[16,16,128]{2,1,0:T(8,128)S(1)}, f32[16,16,128]{2,1,0:T(8,128)S(1)}, u32[]{:S(2)}, u32[]{:S(2)}) collective-permute-start(f32[16,16,128]{2,1,0:T(8,128)S(1)} %get-tuple-element.83), channel_id=1, source_target_pairs={{0,12},{1,13},{2,14},{3,15},{4,8},{5,9},{6,10},{7,11},{8,4},{9,5},... | collective-permute-start | bytes 393224 | tf_op jit(solution)/shard_map/ppermute | solution.py:339
  38.4 30.7 %collective-permute-start.16 = (f32[16,16,128]{2,1,0:T(8,128)S(1)}, f32[16,16,128]{2,1,0:T(8,128)S(1)}, u32[]{:S(2)}, u32[]{:S(2)}) collective-permute-start(f32[16,16,128]{2,1,0:T(8,128)S(1)} %get-tuple-element.84), channel_id=1, source_target_pairs={{0,14},{1,15},{2,12},{3,13},{4,10},{5,11},{6,8},{7,9},{8,6},{9,7},... | collective-permute-start | bytes 393224 | tf_op jit(solution)/shard_map/ppermute | solution.py:339
  41.8 38.8 %collective-permute-start.20 = (f32[16,16,128]{2,1,0:T(8,128)S(1)}, f32[16,16,128]{2,1,0:T(8,128)S(1)}, u32[]{:S(2)}, u32[]{:S(2)}) collective-permute-start(f32[16,16,128]{2,1,0:T(8,128)S(1)} %get-tuple-element.98), channel_id=1, source_target_pairs={{0,8},{1,9},{2,10},{3,11},{4,12},{5,13},{6,14},{7,15},{8,0},{9,1},... | collective-permute-start | bytes 393224 | tf_op jit(solution)/shard_map/ppermute | solution.py:339
  45.2 35.6 %collective-permute-start.21 = (f32[16,16,128]{2,1,0:T(8,128)S(1)}, f32[16,16,128]{2,1,0:T(8,128)S(1)}, u32[]{:S(2)}, u32[]{:S(2)}) collective-permute-start(f32[16,16,128]{2,1,0:T(8,128)S(1)} %get-tuple-element.99), channel_id=1, source_target_pairs={{0,10},{1,11},{2,8},{3,9},{4,14},{5,15},{6,12},{7,13},{8,2},{9,3},... | collective-permute-start | bytes 393224 | tf_op jit(solution)/shard_map/ppermute | solution.py:339
  57.5 25.8 %collective-permute-start.22 = (f32[16,16,128]{2,1,0:T(8,128)S(1)}, f32[16,16,128]{2,1,0:T(8,128)S(1)}, u32[]{:S(2)}, u32[]{:S(2)}) collective-permute-start(f32[16,16,128]{2,1,0:T(8,128)S(1)} %get-tuple-element.100), channel_id=1, source_target_pairs={{0,12},{1,13},{2,14},{3,15},{4,8},{5,9},{6,10},{7,11},{8,4},{9,5},... | collective-permute-start | bytes 393224 | tf_op jit(solution)/shard_map/ppermute | solution.py:339
  60.3 23.1 %collective-permute-start.23 = (f32[16,16,128]{2,1,0:T(8,128)S(1)}, f32[16,16,128]{2,1,0:T(8,128)S(1)}, u32[]{:S(2)}, u32[]{:S(2)}) collective-permute-start(f32[16,16,128]{2,1,0:T(8,128)S(1)} %get-tuple-element.101), channel_id=1, source_target_pairs={{0,14},{1,15},{2,12},{3,13},{4,10},{5,11},{6,8},{7,9},{8,6},{9,7},... | collective-permute-start | bytes 393224 | tf_op jit(solution)/shard_map/ppermute | solution.py:339
  80.8 7.3 %collective-permute-start.19 = (f32[16,16,128]{2,1,0:T(8,128)S(1)}, f32[16,16,128]{2,1,0:T(8,128)S(1)}, u32[]{:S(2)}, u32[]{:S(2)}) collective-permute-start(f32[16,16,128]{2,1,0:T(8,128)S(1)} %get-tuple-element.97), channel_id=1, source_target_pairs={{0,6},{1,7},{2,4},{3,5},{4,2},{5,3},{6,0},{7,1},{8,14},{9,15},{10,... | collective-permute-start | bytes 393224 | tf_op jit(solution)/shard_map/ppermute | solution.py:339
  83.3 8.1 %collective-permute-start.31 = (f32[16,16,128]{2,1,0:T(8,128)S(1)}, f32[16,16,128]{2,1,0:T(8,128)S(1)}, u32[]{:S(2)}, u32[]{:S(2)}) collective-permute-start(f32[16,16,128]{2,1,0:T(8,128)S(1)} %get-tuple-element.86), channel_id=1, source_target_pairs={{0,2},{1,3},{2,0},{3,1},{4,6},{5,7},{6,4},{7,5},{8,10},{9,11},{10,... | collective-permute-start | bytes 393224 | tf_op jit(solution)/shard_map/ppermute | solution.py:339
  83.4 21.0 %collective-permute-start.32 = (f32[16,16,128]{2,1,0:T(8,128)S(1)}, f32[16,16,128]{2,1,0:T(8,128)S(1)}, u32[]{:S(2)}, u32[]{:S(2)}) collective-permute-start(f32[16,16,128]{2,1,0:T(8,128)S(1)} %get-tuple-element.87), channel_id=1, source_target_pairs={{0,4},{1,5},{2,6},{3,7},{4,0},{5,1},{6,2},{7,3},{8,12},{9,13},{10,... | collective-permute-start | bytes 393224 | tf_op jit(solution)/shard_map/ppermute | solution.py:339
  84.5 20.8 %collective-permute-start.33 = (f32[16,16,128]{2,1,0:T(8,128)S(1)}, f32[16,16,128]{2,1,0:T(8,128)S(1)}, u32[]{:S(2)}, u32[]{:S(2)}) collective-permute-start(f32[16,16,128]{2,1,0:T(8,128)S(1)} %get-tuple-element.88), channel_id=1, source_target_pairs={{0,6},{1,7},{2,4},{3,5},{4,2},{5,3},{6,0},{7,1},{8,14},{9,15},{10,... | collective-permute-start | bytes 393224 | tf_op jit(solution)/shard_map/ppermute | solution.py:339
  86.0 19.9 %collective-permute-start.34 = (f32[16,16,128]{2,1,0:T(8,128)S(1)}, f32[16,16,128]{2,1,0:T(8,128)S(1)}, u32[]{:S(2)}, u32[]{:S(2)}) collective-permute-start(f32[16,16,128]{2,1,0:T(8,128)S(1)} %get-tuple-element.89), channel_id=1, source_target_pairs={{0,8},{1,9},{2,10},{3,11},{4,12},{5,13},{6,14},{7,15},{8,0},{9,1},... | collective-permute-start | bytes 393224 | tf_op jit(solution)/shard_map/ppermute | solution.py:339
  88.1 19.0 %collective-permute-start.35 = (f32[16,16,128]{2,1,0:T(8,128)S(1)}, f32[16,16,128]{2,1,0:T(8,128)S(1)}, u32[]{:S(2)}, u32[]{:S(2)}) collective-permute-start(f32[16,16,128]{2,1,0:T(8,128)S(1)} %get-tuple-element.90), channel_id=1, source_target_pairs={{0,10},{1,11},{2,8},{3,9},{4,14},{5,15},{6,12},{7,13},{8,2},{9,3},... | collective-permute-start | bytes 393224 | tf_op jit(solution)/shard_map/ppermute | solution.py:339
  91.4 16.6 %collective-permute-start.36 = (f32[16,16,128]{2,1,0:T(8,128)S(1)}, f32[16,16,128]{2,1,0:T(8,128)S(1)}, u32[]{:S(2)}, u32[]{:S(2)}) collective-permute-start(f32[16,16,128]{2,1,0:T(8,128)S(1)} %get-tuple-element.91), channel_id=1, source_target_pairs={{0,12},{1,13},{2,14},{3,15},{4,8},{5,9},{6,10},{7,11},{8,4},{9,5},... | collective-permute-start | bytes 393224 | tf_op jit(solution)/shard_map/ppermute | solution.py:339
  107.1 8.4 %collective-permute-start.26 = (f32[16,16,128]{2,1,0:T(8,128)S(1)}, f32[16,16,128]{2,1,0:T(8,128)S(1)}, u32[]{:S(2)}, u32[]{:S(2)}) collective-permute-start(f32[16,16,128]{2,1,0:T(8,128)S(1)} %get-tuple-element.105), channel_id=1, source_target_pairs={{0,6},{1,7},{2,4},{3,5},{4,2},{5,3},{6,0},{7,1},{8,14},{9,15},{10,... | collective-permute-start | bytes 393224 | tf_op jit(solution)/shard_map/ppermute | solution.py:339
  108.0 7.6 %collective-permute-start.27 = (f32[16,16,128]{2,1,0:T(8,128)S(1)}, f32[16,16,128]{2,1,0:T(8,128)S(1)}, u32[]{:S(2)}, u32[]{:S(2)}) collective-permute-start(f32[16,16,128]{2,1,0:T(8,128)S(1)} %get-tuple-element.106), channel_id=1, source_target_pairs={{0,8},{1,9},{2,10},{3,11},{4,12},{5,13},{6,14},{7,15},{8,0},{9,1},... | collective-permute-start | bytes 393224 | tf_op jit(solution)/shard_map/ppermute | solution.py:339
  110.5 8.9 %collective-permute-start.28 = (f32[16,16,128]{2,1,0:T(8,128)S(1)}, f32[16,16,128]{2,1,0:T(8,128)S(1)}, u32[]{:S(2)}, u32[]{:S(2)}) collective-permute-start(f32[16,16,128]{2,1,0:T(8,128)S(1)} %get-tuple-element.107), channel_id=1, source_target_pairs={{0,10},{1,11},{2,8},{3,9},{4,14},{5,15},{6,12},{7,13},{8,2},{9,3},... | collective-permute-start | bytes 393224 | tf_op jit(solution)/shard_map/ppermute | solution.py:339
  111.3 13.9 %collective-permute-start.29 = (f32[16,16,128]{2,1,0:T(8,128)S(1)}, f32[16,16,128]{2,1,0:T(8,128)S(1)}, u32[]{:S(2)}, u32[]{:S(2)}) collective-permute-start(f32[16,16,128]{2,1,0:T(8,128)S(1)} %get-tuple-element.108), channel_id=1, source_target_pairs={{0,12},{1,13},{2,14},{3,15},{4,8},{5,9},{6,10},{7,11},{8,4},{9,5},... | collective-permute-start | bytes 393224 | tf_op jit(solution)/shard_map/ppermute | solution.py:339
  112.4 20.2 %collective-permute-start.30 = (f32[16,16,128]{2,1,0:T(8,128)S(1)}, f32[16,16,128]{2,1,0:T(8,128)S(1)}, u32[]{:S(2)}, u32[]{:S(2)}) collective-permute-start(f32[16,16,128]{2,1,0:T(8,128)S(1)} %get-tuple-element.109), channel_id=1, source_target_pairs={{0,14},{1,15},{2,12},{3,13},{4,10},{5,11},{6,8},{7,9},{8,6},{9,7},... | collective-permute-start | bytes 393224 | tf_op jit(solution)/shard_map/ppermute | solution.py:339
  133.7 6.9 %collective-permute-start.40 = (f32[2,4,64,128]{3,2,1,0:T(8,128)S(1)}, f32[2,4,64,128]{3,2,1,0:T(8,128)S(1)}, u32[]{:S(2)}, u32[]{:S(2)}) collective-permute-start(f32[2,4,64,128]{3,2,1,0:T(8,128)S(1)} %get-tuple-element.123), channel_id=1, source_target_pairs={{0,1},{1,0},{2,3},{3,2},{4,5},{5,4},{6,7},{7,6},{8,9},{9,8},{10,11... | collective-permute-start | bytes 786440 | tf_op jit(solution)/shard_map/ppermute | solution.py:339
  140.7 7.5 %collective-permute-start.41 = (f32[2,4,64,128]{3,2,1,0:T(8,128)S(1)}, f32[2,4,64,128]{3,2,1,0:T(8,128)S(1)}, u32[]{:S(2)}, u32[]{:S(2)}) collective-permute-start(f32[2,4,64,128]{3,2,1,0:T(8,128)S(1)} %add.12), channel_id=1, source_target_pairs={{0,16},{16,0},{1,17},{17,1},{2,18},{18,2},{3,19},{19,3},{4,20},{20... | collective-permute-start | bytes 786440 | tf_op jit(solution)/shard_map/ppermute | solution.py:339
  141.0 12.8 %collective-permute-start.43 = (f32[2,4,64,128]{3,2,1,0:T(8,128)S(1)}, f32[2,4,64,128]{3,2,1,0:T(8,128)S(1)}, u32[]{:S(2)}, u32[]{:S(2)}) collective-permute-start(f32[2,4,64,128]{3,2,1,0:T(8,128)S(1)} %add.13), channel_id=1, source_target_pairs={{0,16},{16,0},{1,17},{17,1},{2,18},{18,2},{3,19},{19,3},{4,20},{20... | collective-permute-start | bytes 786440 | tf_op jit(solution)/shard_map/ppermute | solution.py:339
  (30 other events, 665.0 us)

commit v2 on v1

v2 whole, which is shorter than its diff:
```python
import functools

import jax
import jax.numpy as jnp
import ml_dtypes
import numpy as np
from jax import lax
from jax.experimental import pallas as pl
from jax.experimental.pallas import tpu as pltpu
from jax.sharding import PartitionSpec as P

STRAIN_WEIGHT = 0.05
EDGE_WEIGHT = 0.05
PIECES = (8, 8)
F32 = jnp.float32
BF16 = jnp.bfloat16


def split_table(table):
    high = table.astype(ml_dtypes.bfloat16)
    low = (table - high.astype(np.float64)).astype(ml_dtypes.bfloat16)
    return high, low


def forward_table(freqs, places, length):
    angle = 2.0 * np.pi / length * (freqs[:, None] * places[None, :] % length)
    cosine = np.cos(angle) * length ** (-0.5)
    sine = np.sin(angle) * length ** (-0.5)
    return np.block([[cosine, sine], [-sine, cosine]])


def turn_fits():
    nodes = np.cos(np.pi * (np.arange(400) + 0.5) / 400)
    t = (nodes + 1.0) / 8.0
    r = np.sqrt(t)
    fits = []
    for values, degree in ((np.cos(2 * np.pi * r), 8), (np.sin(2 * np.pi * r) / r, 8)):
        cheb = np.polynomial.chebyshev.Chebyshev.fit(t, values, degree, domain=[0.0, 0.25])
        fits.append([float(c) for c in cheb.convert(kind=np.polynomial.Polynomial).coef])
    return fits


COS_FIT, SIN_FIT = turn_fits()


def series(coefs, t):
    total = jnp.full_like(t, coefs[-1])
    for coef in coefs[-2::-1]:
        total = total * t + coef
    return total


def halves(x):
    high = x.astype(BF16)
    return high, (x - high.astype(F32)).astype(BF16)


def dot(a, b):
    return jnp.dot(a, b, preferred_element_type=F32)


def dot_pairs(a, b):
    return dot(a[0], b[0]) + (dot(a[0], b[1]) + dot(a[1], b[0]))


SMEM = pl.BlockSpec(memory_space=pltpu.SMEM)


def whole(shape):
    return pl.BlockSpec(tuple(shape), lambda step, rank=len(shape): (0,) * rank)


def call(kernel, outs, scalars, operands, scratch, flops, name, blocks=None, first=(), vmem=48):
    blocks = blocks or {}
    inputs = len(scalars) + len(operands)
    specs = [SMEM] * len(scalars)
    moved = 4 * sum(int(np.prod(shape)) for shape in outs)
    for at, operand in enumerate(operands):
        if at in blocks and blocks[at] is None:
            shape = (0,)
            specs.append(pl.BlockSpec(memory_space=pl.ANY))
        elif at in blocks:
            shape, index = blocks[at]
            specs.append(pl.BlockSpec(shape, lambda step, index=index: index))
        else:
            shape = operand.shape
            specs.append(whole(shape))
        moved += int(np.prod(shape)) * operand.dtype.itemsize
    specs += [pl.BlockSpec(memory_space=pl.ANY)] * len(first)

    def run(*refs):
        kernel(*refs[:inputs], *refs[inputs + len(first) :])

    return pl.pallas_call(
        run,
        grid=(1,),
        out_shape=[jax.ShapeDtypeStruct(shape, F32) for shape in outs],
        in_specs=specs,
        out_specs=[whole(shape) for shape in outs],
        scratch_shapes=scratch,
        compiler_params=pltpu.CompilerParams(vmem_limit_bytes=vmem * 1024 * 1024),
        cost_estimate=pl.CostEstimate(flops=int(flops), bytes_accessed=int(moved), transcendentals=0),
        name=name,
    )(*scalars, *operands, *first)


def field_of(place, amp, disp, sup, f, p):
    if f > 0:
        return disp[f - 1, p]
    rows = amp.shape[1]
    return sup[p, pl.ds(pl.multiple_of(place[2] * rows, rows), rows), :].astype(F32) * amp[p]


def edges_kernel(place, amp, disp, sup, x_mate, x_out):
    planes = amp.shape[0]
    core = place[1]
    for f in range(4):
        x_mate[f] = field_of(place, amp, disp, sup, f, (1 - core) * (planes - 1))
        x_out[f] = field_of(place, amp, disp, sup, f, core * (planes - 1))


def pack_kernel(edged, place, a, b, amp, disp, sup, out):
    portion, rows, depth = a.shape[1:]
    planes = amp.shape[0]
    for c in range(2):
        for p in range(portion):
            at = (c * portion + p) * rows
            out[at : at + rows, :] = a[c, p] + b[c, p]
    if edged:
        for f in range(4):
            for p in range(planes):
                value = field_of(place, amp, disp, sup, f, p)
                at = 2 * portion * rows + f * planes + p
                out[at : at + 1, :] = value[:1]
                at += 4 * planes
                out[at : at + 1, :] = value[rows - 1 :]


def laplace_kernel(refls, place, amp, disp, sup, x_mate, x_out, *refs):
    planes, rows, depth = amp.shape
    packs, out = refs[:-1], refs[-1]
    refl = place[2]
    low_core = place[1] == 0
    row = lax.broadcasted_iota(jnp.int32, (rows, depth), 0)
    lane = lax.broadcasted_iota(jnp.int32, (rows, depth), 1)
    for f in range(4):
        for p in range(planes):
            centre = field_of(place, amp, disp, sup, f, p)
            before, behind = jnp.zeros((1, depth), F32), jnp.zeros((1, depth), F32)
            for k in range(1, refls):
                at = packs[k - 1].shape[0] - 8 * planes + f * planes + p
                behind = jnp.where((refl ^ k) - refl == 1, packs[k - 1][at : at + 1, :], behind)
                at += 4 * planes
                before = jnp.where(refl - (refl ^ k) == 1, packs[k - 1][at : at + 1, :], before)
            if p == 0:
                beside = jnp.where(low_core, x_out[f], x_mate[f])
            else:
                beside = field_of(place, amp, disp, sup, f, p - 1)
            if p == planes - 1:
                beside = beside + jnp.where(low_core, x_mate[f], x_out[f])
            else:
                beside = beside + field_of(place, amp, disp, sup, f, p + 1)
            beside = beside + jnp.where(row == 0, before, pltpu.roll(centre, 1, 0))
            beside = beside + jnp.where(row == rows - 1, behind, pltpu.roll(centre, rows - 1, 0))
            beside = beside + jnp.where(lane == 0, 0.0, pltpu.roll(centre, 1, 1))
            beside = beside + jnp.where(lane == depth - 1, 0.0, pltpu.roll(centre, depth - 1, 1))
            out[f, p] = 6.0 * centre - beside


def object_kernel(which, grid, place, params, amp, disp, sup, *outs):
    planes, rows, depth = amp.shape
    first = pl.multiple_of(place[2] * rows, rows)
    zed = lax.broadcasted_iota(jnp.int32, (rows, depth), 1).astype(F32) * (1.0 / grid)
    each = len(outs) // len(which)
    portion = planes // (each - 1)

    for part in range(each - 1):

        def plane(i, carry, part=part):
            p = part * portion + i
            weight = sup[p, pl.ds(first, rows), :].astype(F32) * amp[p]
            parts = [disp[0, p], disp[1, p], disp[2, p]]
            for at, k in enumerate(which):
                phase = params[4 * k] * parts[0] + params[4 * k + 1] * parts[1] + params[4 * k + 2] * parts[2]
                shifted = params[4 * k + 3] * zed
                turns = phase * (0.5 / np.pi) + (shifted - jnp.floor(shifted))
                turns = turns - jnp.floor(turns + 0.5)
                square = turns * turns
                cosine = series(COS_FIT, square)
                sine = series(SIN_FIT, square) * turns
                outs[each * at][0, p] = cosine
                outs[each * at][1, p] = sine
                outs[each * at + 1 + part][0, i] = weight * cosine
                outs[each * at + 1 + part][1, i] = weight * sine
            return carry

        lax.fori_loop(0, portion, plane, 0)


def y_forward_kernel(refls, chips, splits, targets, place, *refs):
    count = 2 * refls * splits
    parts, tables, outs = refs[:count], refs[count], refs[count + 1 : -2]
    hold_high, hold_low = refs[-2:]
    chip, core, refl = place[0], place[1], place[2]
    portion, rows, depth = parts[0].shape[1:]
    planes = portion * splits
    length = rows * refls
    share = tables.shape[2] // chips

    def order(which):
        return jnp.concatenate(
            [tables[core, which, pl.ds(pl.multiple_of((chip ^ k) * share, share), share), :] for k in targets],
            axis=0,
        )

    table = (order(0), order(1))
    for src in range(2):
        for p in range(planes):
            lane = (src * planes + p) * depth
            for c in range(2):
                for k in range(refls):
                    part = parts[(src * refls + k) * splits + p // portion]
                    one, two = halves(part[c, p % portion])
                    at = pl.ds(pl.multiple_of(c * length + (refl ^ k) * rows, rows), rows)
                    hold_high[at, lane : lane + depth] = one
                    hold_low[at, lane : lane + depth] = two
    for src in range(2):
        for p in range(0, planes, 2):
            lane = (src * planes + p) * depth
            operand = (hold_high[:, lane : lane + 2 * depth], hold_low[:, lane : lane + 2 * depth])
            result = dot_pairs(table, operand)
            base = (core if src == 0 else 1 - core) * planes + p
            for i in range(len(targets)):
                for j in range(2):
                    outs[i][base + j] = result[i * share : (i + 1) * share, j * depth : (j + 1) * depth]


def middle_kernel(chips, first, place, *refs):
    got, intensity = refs[:chips], refs[chips]
    fwd = (refs[chips + 1][...], refs[chips + 2][...])
    bwd = (refs[chips + 3][...], refs[chips + 4][...])
    outs = refs[chips + 5 : -4]
    gather, scatter, measured, arrived = refs[-4:]
    chip = place[0]
    group, width, depth = got[0].shape
    rows = width // 2
    edge = group * chips
    grid = 2 * edge
    batch = gather.shape[1] // depth
    load = pltpu.make_async_copy(intensity.at[0, :, first : first + rows, :], measured, arrived)
    load.start()

    def place_of(c, k):
        return pl.ds(pl.multiple_of(c * edge + (chip ^ k) * group, group), group)

    for key in range(0, rows, batch):
        for k in range(chips):
            for c in range(2):
                for j in range(batch):
                    gather[place_of(c, k), j * depth : (j + 1) * depth] = got[k][:, (key + j) * 2 + c, :]
        one = dot_pairs(fwd, halves(gather[...]))
        if key == 0:
            load.wait()
        back = []
        for j in range(batch):
            lines = [one[c * grid : (c + 1) * grid, j * depth : (j + 1) * depth] for c in range(2)]
            spectrum = dot_pairs(halves(jnp.concatenate(lines, axis=1)), bwd)
            real, imag = spectrum[:, :grid], spectrum[:, grid:]
            excess = 4.0 * (real * real + imag * imag - measured[:, key + j, :])
            back.append(dot_pairs(halves(jnp.concatenate([excess * real, excess * imag], axis=1)), fwd))
        lines = [jnp.concatenate([b[:, c * depth : (c + 1) * depth] for b in back], axis=1) for c in range(2)]
        scatter[...] = dot_pairs(bwd, halves(jnp.concatenate(lines, axis=0)))
        for k in range(chips):
            for c in range(2):
                for j in range(batch):
                    outs[k][:, (key + j) * 2 + c, :] = scatter[place_of(c, k), j * depth : (j + 1) * depth]


def y_adjoint_kernel(refls, chips, jobs, place, *refs):
    got, tables = refs[:chips], refs[chips]
    total = refls * len(jobs)
    adds, outs = refs[chips + 1 : -2 - total], refs[-2 - total : -2]
    done, hold = refs[-2:]
    done[...] = jnp.zeros_like(done)
    chip, core, refl = place[0], place[1], place[2]
    planes, rows, depth = outs[0].shape[1:]
    width = got[0].shape[1]

    def order(which):
        pieces = []
        for q in range(refls):
            for c in range(2):
                at = pl.multiple_of(((refl ^ q) * 2 + c) * rows, rows)
                pieces.append(tables[core, which, pl.ds(at, rows), :])
        return jnp.concatenate(pieces, axis=0)

    table = (order(0), order(1))
    for job, (mate, first) in enumerate(jobs):
        base = (1 - core if mate else core) * (got[0].shape[0] // 2) + first
        for p in range(planes):
            lane = (job * planes + p) * depth
            for k in range(chips):
                at = pl.ds(pl.multiple_of((chip ^ k) * width, width), width)
                hold[at, lane : lane + depth] = got[k][base + p]
    for job in range(len(jobs)):
        for p in range(0, planes, 2):
            lane = (job * planes + p) * depth
            result = dot_pairs(table, halves(hold[:, lane : lane + 2 * depth]))
            for k in range(refls):
                for c in range(2):
                    at = (k * 2 + c) * rows
                    for j in range(2):
                        value = result[at : at + rows, j * depth : (j + 1) * depth]
                        if adds:
                            value = value + adds[job * refls + k][c, p + j]
                        outs[job * refls + k][c, p + j] = value


def final_kernel(refls, splits, place, params, *refs):
    amp, sup, lapped = refs[:3]
    own, mate = refs[3 : 3 + splits], refs[3 + splits : 3 + 2 * splits]
    others = refs[3 + 2 * splits : 3 + (1 + refls) * splits]
    phases = refs[3 + (1 + refls) * splits : -2]
    out_amp, out_disp = refs[-2:]
    planes, rows, depth = amp.shape
    first = pl.multiple_of(place[2] * rows, rows)
    portion = planes // splits

    for part in range(splits):

        def plane(i, carry, part=part):
            p = part * portion + i
            mask = sup[p, pl.ds(first, rows), :].astype(F32)
            weight = mask * amp[p]
            total = jnp.zeros((rows, depth), F32)
            moved = [jnp.zeros((rows, depth), F32) for _ in range(3)]
            for k in range(refls):
                if k == 0:
                    real, imag = [own[part][c, i] + mate[part][c, i] for c in range(2)]
                else:
                    at = [pl.ds(pl.multiple_of((c * portion + i) * rows, rows), rows) for c in range(2)]
                    real, imag = [others[(k - 1) * splits + part][at[c], :] for c in range(2)]
                cosine, sine = phases[k][0, p], phases[k][1, p]
                total = total + (real * cosine + imag * sine)
                across = weight * (imag * cosine - real * sine)
                moved = [m + params[4 * k + c] * across for c, m in enumerate(moved)]
            out_amp[p] = mask * total + (2.0 * EDGE_WEIGHT) * (mask * lapped[0, p])
            for c in range(3):
                out_disp[c, p] = moved[c] + (2.0 * STRAIN_WEIGHT) * lapped[c + 1, p]
            return carry

        lax.fori_loop(0, portion, plane, 0)


def swap(x, axis, bits):
    count = lax.axis_size(axis)
    return lax.ppermute(x, axis, [(i, i ^ bits) for i in range(count)])


def swap_outward(x, axis):
    count = lax.axis_size(axis)
    return lax.ppermute(x, axis, [pair for i in range(1, count - 1, 2) for pair in ((i, i + 1), (i + 1, i))])


def body(amplitude, displacement, support, miller, shift_kz, intensity):
    refls = lax.axis_size("refl")
    slabs = lax.axis_size("slab")
    chips = slabs // 2
    planes, rows, depth = amplitude.shape
    edge = planes * slabs
    grid = 2 * edge
    keys = grid // slabs
    pieces = PIECES if sum(PIECES) == keys else (keys,)
    splits = 2 if planes % 8 == 0 else 1
    portion = planes // splits
    group = 2 * planes
    refl = lax.axis_index("refl")
    slab = lax.axis_index("slab")
    place = jnp.stack([slab // 2, slab % 2, refl]).astype(jnp.int32)
    cells = planes * rows * depth
    part_shape = (2, portion, rows, depth)

    every, inner = np.arange(grid), np.arange(edge)
    table = forward_table(every, inner, grid)
    constants = [jnp.asarray(t) for one in (table, table.T) for t in split_table(one)]
    by_key = table.reshape(2, chips, 2, keys, 2 * edge).transpose(2, 1, 3, 0, 4)

    def y_tables(at):
        first, count = sum(pieces[:at]), pieces[at]
        some = by_key[:, :, first : first + count].reshape(2, chips * count * 2, 2 * edge)
        fwd = jnp.asarray(np.stack(split_table(some), axis=1))
        some = some.reshape(2, chips * count * 2, 2, refls, rows)
        some = some.transpose(0, 3, 2, 4, 1).reshape(2, 2 * edge, chips * count * 2)
        return fwd, jnp.asarray(np.stack(split_table(some), axis=1))

    own_params = jnp.concatenate([miller[0].astype(F32), shift_kz.astype(F32)])
    fields = (amplitude, displacement, support)
    def make(params, which, parts, vmem=48):
        made = call(
            functools.partial(object_kernel, which, grid),
            ([(2, planes, rows, depth)] + [(2, planes // parts, rows, depth)] * parts) * len(which),
            [place, params],
            fields,
            [],
            50 * len(which) * cells,
            "object",
            vmem=vmem,
        )
        return [made[i * (parts + 1) : (i + 1) * (parts + 1)] for i in range(len(which))]

    ((own_phase, *own_parts),) = make(own_params, [0], splits)
    params = jnp.concatenate([own_params] + [swap(own_params, "refl", k) for k in range(1, refls)])
    made = make(params, list(range(1, refls)), splits, vmem=60)
    phases = [own_phase] + [one[0] for one in made]
    own_mates = [swap(x, "slab", 1) for x in own_parts]
    held = [[swap(one[1], "refl", k + 1) for k, one in enumerate(made)]]
    for part in range(1, splits):
        held.append([swap(one[1 + part], "refl", k + 1) for k, one in enumerate(made)])

    held = [x for part in zip(*held) for x in part]
    mates = [swap(x, "slab", 1) for x in held]

    def y_forward(at, targets, first=()):
        made = call(
            functools.partial(y_forward_kernel, refls, chips, splits, targets),
            [(group, 2 * pieces[at], depth)] * len(targets),
            [place],
            (*own_parts, *held, *own_mates, *mates, y_tables(at)[0]),
            [pltpu.VMEM((2 * edge, group * depth), BF16)] * 2,
            6 * group * depth * 2 * edge * len(targets) * pieces[at] * 2,
            "y_forward",
            first=first,
        )
        return dict(zip(targets, made))

    def middle(at, got, first=()):
        count = pieces[at]
        return call(
            functools.partial(middle_kernel, chips, sum(pieces[:at])),
            [(group, 2 * count, depth)] * chips,
            [place],
            (*got, intensity, *constants),
            [pltpu.VMEM((2 * edge, min(count, 8) * depth), F32)] * 2
            + [pltpu.VMEM((grid, count, grid), F32), pltpu.SemaphoreType.DMA],
            6 * count * (2 * edge * 2 * grid * depth * 2 + grid * 2 * depth * 2 * grid * 2),
            "middle",
            {chips: None},
            first,
        )

    def y_adjoint(at, got, jobs, adds, first=()):
        count = pieces[at]
        made = call(
            functools.partial(y_adjoint_kernel, refls, chips, jobs),
            [part_shape] * (refls * len(jobs)) + [(8, 128)],
            [place],
            (*got, y_tables(at)[1], *[x for job in adds for x in job]),
            [pltpu.VMEM((chips * 2 * count, len(jobs) * portion * depth), F32)],
            6 * len(jobs) * portion * depth * 2 * edge * chips * 2 * count,
            "y_adjoint",
            first=first,
        )
        return [made[i * refls : (i + 1) * refls] for i in range(len(jobs))], made[-1]

    def cross(sends):
        return [sends[0]] + [swap(sends[k], "slab", 2 * k) for k in range(1, chips)]

    sends = [y_forward(at, list(range(chips))) for at in range(len(pieces))]
    jobs = [(mate, part * portion) for part in range(splits) for mate in (True, False)]
    adds = []
    for at in range(len(pieces)):
        backs = middle(at, cross(sends[at]))
        returned = cross(backs)
        if at + 1 < len(pieces):
            adds, unused = y_adjoint(at, returned, jobs, adds)
    sums = []
    own, mates, others = [], [], [[] for _ in range(1, refls)]
    mate_jobs = [job for job in range(len(jobs)) if jobs[job][0]]
    mine_jobs = [job for job in range(len(jobs)) if not jobs[job][0]]
    for_mate, first_done = y_adjoint(at, returned, [jobs[i] for i in mate_jobs], [adds[i] for i in mate_jobs if adds])
    mine, unused = y_adjoint(at, returned, [jobs[i] for i in mine_jobs], [adds[i] for i in mine_jobs if adds], (first_done,))
    for part in range(splits):
        from_mate = [swap(x, "slab", 1) for x in for_mate[part]]
        own.append(mine[part][0])
        mates.append(from_mate[0])
        for k in range(1, refls):
            shape = (2 * portion * rows + (8 * planes if part == 0 else 0), depth)
            (total,) = call(
                functools.partial(pack_kernel, part == 0),
                [shape],
                [place],
                (mine[part][k], from_mate[k], *fields),
                [],
                4 * cells,
                "pack",
            )
            sums.append(total)
            others[k - 1].append(swap(total, "refl", k))
    edges = call(edges_kernel, [(4, rows, depth)] * 2, [place], fields, [], cells, "edges", first=sums)
    halos = (swap(edges[0], "slab", 1), swap_outward(edges[1], "slab"), *[one[0] for one in others])
    (lapped,) = call(
        functools.partial(laplace_kernel, refls),
        [(4, planes, rows, depth)],
        [place],
        (*fields, *halos),
        [],
        30 * cells,
        "laplace",
    )
    others = [x for one in others for x in one]

    return tuple(
        call(
            functools.partial(final_kernel, refls, splits),
            [(planes, rows, depth), (3, planes, rows, depth)],
            [place, params],
            (amplitude, support, lapped, *own, *mates, *others, *phases),
            [],
            20 * refls * cells,
            "final",
        )
    )


def solution(mesh):
    placed = (
        P("slab", "refl", None),
        P(None, "slab", "refl", None),
        P("slab", None, None),
        P("refl", None),
        P("refl"),
        P("refl", None, "slab", None),
    )
    return jax.shard_map(
        body,
        mesh=mesh,
        in_specs=placed,
        out_specs=(P("slab", "refl", None), P(None, "slab", "refl", None)),
        check_vma=False,
    )
```

time: 157 us -> 147 us (0.936)
  waiting for transfers between devices: 66.1 us -> 50 us
  starting transfers between devices: 47.5 us -> 52.1 us
    ppermute x43 -> x42, waiting for transfers between devices: 63.9 us -> 45.4 us  [swap(): return lax.ppermute(x, axis, [(i, i ^ bits) for i in range(count)])]
    ppermute x43 -> x42, starting transfers between devices: 44.5 us -> 48.8 us  [swap(): return lax.ppermute(x, axis, [(i, i ^ bits) for i in range(count)])]
    ppermute x1, waiting for transfers between devices: 2.19 us -> 4.62 us  [swap_outward(): lax.ppermute(x, axis, [pair for i in range(1, count - 1, 2) for pair in (...]
    unnamed x36 -> x34, local copies, waits for them, and re-layouts: 3.2 us -> 4.72 us
  transfers between devices with their start and end apart: 44 -> 43, of which waited for: 16 -> 16; matrix products, arithmetic and copies ran while one was open for 0% -> 0% of each run, Pallas kernels for 20% -> 19%
where the time goes in v2:
time: 147 us; the launch traced here: 146 us
  starting transfers between devices  52.1 us (35%)
  waiting for transfers between devices  50 us (34%)
  Pallas kernels  35.6 us (24%)
  local copies, waits for them, and re-layouts  4.72 us (3%)
  other arithmetic  1.94 us (1%)
  between operations  1.66 us (1%)
    ppermute x42, starting transfers between devices, swap(): return lax.ppermute(x, axis, [(i, i ^ bits) for i in range(count)])  48.8 us
    ppermute x42, waiting for transfers between devices, swap(): return lax.ppermute(x, axis, [(i, i ^ bits) for i in range(count)])  45.4 us
    pallas_call x14, Pallas kernels, call(): pl.pallas_call(run, grid=(1,), out_shape=[jax.ShapeDtypeStruct(shape, F32...  35.6 us
    unnamed x34, local copies, waits for them, and re-layouts  4.72 us
    ppermute x1, waiting for transfers between devices, swap_outward(): lax.ppermute(x, axis, [pair for i in range(1, count - 1, 2) for pair in (...  4.62 us
    ppermute x1, starting transfers between devices, swap_outward(): lax.ppermute(x, axis, [pair for i in range(1, count - 1, 2) for pair in (...  3.34 us
  transfers between devices with their start and end apart: 43, of which 16 were waited for; matrix products, arithmetic and copies ran while one was open for 0% of the time, Pallas kernels for 19%

profile of v2, /device:TPU:13, one launch (start us, length us, event | category | flops | bytes accessed | tf_op | source)
XLA Modules:
  0.0 146.0 jit_solution(6888028748774139263)
XLA Ops:
  3.0 1.6 %collective-permute-done = f32[4]{0:T(128)S(1)} collective-permute-done((f32[4]{0:T(128)S(1)}, f32[4]{0:T(128)S(1)}, u32[]{:S(2)}, u32[]{:S(2)}) %collective-permute-start) | collective-permute-done | bytes 48 | tf_op jit(solution)/shard_map/ppermute | solution.py:357
  5.2 2.8 %object.3 = (f32[2,8,64,128]{3,2,1,0:T(8,128)}, f32[2,4,64,128]{3,2,1,0:T(8,128)}, f32[2,4,64,128]{3,2,1,0:T(8,128)}) custom-call(s32[3]{0:T(128)} %pad_add_fusion.refs_0_, f32[8]{0:T(128)} %pad_maximum_fusion.1.refs_1_, f32[8,64,128]{2,1,0:T(8,128)} %refs_2_.9, f32[3,8,64,128]{3,2,1,0:T(8,128)} %refs_2_.8, s32[8,128,128]{2,1,0:T(8,128)} %refs_3_.13), custom_call_target="tpu_custom_call" | custom-call | flops 3276800 | bytes 2621440 | tf_op jit(solution)/shard_map/object/pallas_call | solution.py:94
  14.2 2.5 %collective-permute-start.3 = (f32[2,4,64,128]{3,2,1,0:T(8,128)S(1)}, f32[2,4,64,128]{3,2,1,0:T(8,128)S(1)}, u32[]{:S(2)}, u32[]{:S(2)}) collective-permute-start(f32[2,4,64,128]{3,2,1,0:T(8,128)S(1)} %get-tuple-element.59.refs_1_), channel_id=1, source_target_pairs={{0,1},{1,0},{2,3},{3,2},{4,5},{5,4},{6,7},{7,6},{8,9},{9,8},{10,11... | collective-permute-start | bytes 786440 | tf_op jit(solution)/shard_map/ppermute | solution.py:357
  16.7 2.5 %collective-permute-start.5 = (f32[2,4,64,128]{3,2,1,0:T(8,128)S(1)}, f32[2,4,64,128]{3,2,1,0:T(8,128)S(1)}, u32[]{:S(2)}, u32[]{:S(2)}) collective-permute-start(f32[2,4,64,128]{3,2,1,0:T(8,128)S(1)} %collective-permute-done.1.refs_3_), channel_id=1, source_target_pairs={{0,1},{1,0},{2,3},{3,2},{4,5},{5,4},{6,7},{7,6},{8,9},{9,8},{10,11... | collective-permute-start | bytes 786440 | tf_op jit(solution)/shard_map/ppermute | solution.py:357
  19.8 2.7 %collective-permute-start.6 = (f32[2,4,64,128]{3,2,1,0:T(8,128)S(1)}, f32[2,4,64,128]{3,2,1,0:T(8,128)S(1)}, u32[]{:S(2)}, u32[]{:S(2)}) collective-permute-start(f32[2,4,64,128]{3,2,1,0:T(8,128)S(1)} %collective-permute-done.2.refs_4_), channel_id=1, source_target_pairs={{0,1},{1,0},{2,3},{3,2},{4,5},{5,4},{6,7},{7,6},{8,9},{9,8},{10,11... | collective-permute-start | bytes 786440 | tf_op jit(solution)/shard_map/ppermute | solution.py:357
  24.6 1.8 %y_forward.3 = (f32[16,16,128]{2,1,0:T(8,128)S(1)}, f32[16,16,128]{2,1,0:T(8,128)S(1)}, f32[16,16,128]{2,1,0:T(8,128)S(1)}, f32[16,16,128]{2,1,0:T(8,128)S(1)}, ...) custom-call(s32[3]{0:T(128)S(1)} %copy-done.10, ...), custom_call_target="tpu_custom_call" | custom-call | flops 402653184 | bytes 3407872 | tf_op jit(solution)/shard_map/y_forward/pallas_call | solution.py:94
  29.1 2.3 %collective-permute-start.24 = (f32[16,16,128]{2,1,0:T(8,128)S(1)}, f32[16,16,128]{2,1,0:T(8,128)S(1)}, u32[]{:S(2)}, u32[]{:S(2)}) collective-permute-start(f32[16,16,128]{2,1,0:T(8,128)S(1)} %get-tuple-element.83), channel_id=1, source_target_pairs={{0,8},{1,9},{2,10},{3,11},{4,12},{5,13},{6,14},{7,15},{8,0},{9,1},... | collective-permute-start | bytes 393224 | tf_op jit(solution)/shard_map/ppermute | solution.py:357
  32.4 1.7 %y_forward.2 = (f32[16,16,128]{2,1,0:T(8,128)S(1)}, f32[16,16,128]{2,1,0:T(8,128)S(1)}, f32[16,16,128]{2,1,0:T(8,128)S(1)}, f32[16,16,128]{2,1,0:T(8,128)S(1)}, ...) custom-call(s32[3]{0:T(128)S(1)} %copy-done.10, ...), custom_call_target="tpu_custom_call" | custom-call | flops 402653184 | bytes 3407872 | tf_op jit(solution)/shard_map/y_forward/pallas_call | solution.py:94
  34.2 1.4 collective-permute-start.26
  35.7 1.5 %collective-permute-done.23.refs_4_ = f32[16,16,128]{2,1,0:T(8,128)S(1)} collective-permute-done((f32[16,16,128]{2,1,0:T(8,128)S(1)}, f32[16,16,128]{2,1,0:T(8,128)S(1)}, u32[]{:S(2)}, u32[]{:S(2)}) %collective-permute-start.23) | collective-permute-done | bytes 131104 | tf_op jit(solution)/shard_map/ppermute | solution.py:357
  38.7 2.1 %collective-permute-start.8 = (f32[16,16,128]{2,1,0:T(8,128)S(1)}, f32[16,16,128]{2,1,0:T(8,128)S(1)}, u32[]{:S(2)}, u32[]{:S(2)}) collective-permute-start(f32[16,16,128]{2,1,0:T(8,128)S(1)} %get-tuple-element.65), channel_id=1, source_target_pairs={{0,4},{1,5},{2,6},{3,7},{4,0},{5,1},{6,2},{7,3},{8,12},{9,13},{10,... | collective-permute-start | bytes 393224 | tf_op jit(solution)/shard_map/ppermute | solution.py:357
  40.8 5.6 %collective-permute-done.25.refs_6_ = f32[16,16,128]{2,1,0:T(8,128)S(1)} collective-permute-done((f32[16,16,128]{2,1,0:T(8,128)S(1)}, f32[16,16,128]{2,1,0:T(8,128)S(1)}, u32[]{:S(2)}, u32[]{:S(2)}) %collective-permute-start.25) | collective-permute-done | bytes 131104 | tf_op jit(solution)/shard_map/ppermute | solution.py:357
  46.4 4.1 %collective-permute-done.26.refs_7_ = f32[16,16,128]{2,1,0:T(8,128)S(1)} collective-permute-done((f32[16,16,128]{2,1,0:T(8,128)S(1)}, f32[16,16,128]{2,1,0:T(8,128)S(1)}, u32[]{:S(2)}, u32[]{:S(2)}) %collective-permute-start.26) | collective-permute-done | bytes 131104 | tf_op jit(solution)/shard_map/ppermute | solution.py:357
  51.5 3.0 %collective-permute-done.27.refs_8_ = f32[16,16,128]{2,1,0:T(8,128)S(1)} collective-permute-done((f32[16,16,128]{2,1,0:T(8,128)S(1)}, f32[16,16,128]{2,1,0:T(8,128)S(1)}, u32[]{:S(2)}, u32[]{:S(2)}) %collective-permute-start.27) | collective-permute-done | bytes 131104 | tf_op jit(solution)/shard_map/ppermute | solution.py:357
  54.6 1.7 %collective-permute-start.12 = (f32[16,16,128]{2,1,0:T(8,128)S(1)}, f32[16,16,128]{2,1,0:T(8,128)S(1)}, u32[]{:S(2)}, u32[]{:S(2)}) collective-permute-start(f32[16,16,128]{2,1,0:T(8,128)S(1)} %get-tuple-element.69), channel_id=1, source_target_pairs={{0,12},{1,13},{2,14},{3,15},{4,8},{5,9},{6,10},{7,11},{8,4},{9,5},... | collective-permute-start | bytes 393224 | tf_op jit(solution)/shard_map/ppermute | solution.py:357
  56.3 9.2 %middle.3 = (f32[16,16,128]{2,1,0:T(8,128)S(1)}, f32[16,16,128]{2,1,0:T(8,128)S(1)}, f32[16,16,128]{2,1,0:T(8,128)S(1)}, f32[16,16,128]{2,1,0:T(8,128)S(1)}, f32...) custom-call(s32[3]{0:T(128)S(1)} %copy-done.10, ...), custom_call_target="tpu_custom_call" | custom-call | flops 4831838208 | bytes 3145728 | tf_op jit(solution)/shard_map/middle/pallas_call | solution.py:94
  65.5 1.3 collective-permute-start.28
  66.8 4.2 %collective-permute-start.29 = (f32[16,16,128]{2,1,0:T(8,128)S(1)}, f32[16,16,128]{2,1,0:T(8,128)S(1)}, u32[]{:S(2)}, u32[]{:S(2)}) collective-permute-start(f32[16,16,128]{2,1,0:T(8,128)S(1)} %get-tuple-element.89), channel_id=1, source_target_pairs={{0,4},{1,5},{2,6},{3,7},{4,0},{5,1},{6,2},{7,3},{8,12},{9,13},{10,... | collective-permute-start | bytes 393224 | tf_op jit(solution)/shard_map/ppermute | solution.py:357
  73.0 3.3 %collective-permute-done.13.refs_8_ = f32[16,16,128]{2,1,0:T(8,128)S(1)} collective-permute-done((f32[16,16,128]{2,1,0:T(8,128)S(1)}, f32[16,16,128]{2,1,0:T(8,128)S(1)}, u32[]{:S(2)}, u32[]{:S(2)}) %collective-permute-start.13) | collective-permute-done | bytes 131104 | tf_op jit(solution)/shard_map/ppermute | solution.py:357
  76.4 9.4 %middle.2 = (f32[16,16,128]{2,1,0:T(8,128)S(1)}, f32[16,16,128]{2,1,0:T(8,128)S(1)}, f32[16,16,128]{2,1,0:T(8,128)S(1)}, f32[16,16,128]{2,1,0:T(8,128)S(1)}, f32...) custom-call(s32[3]{0:T(128)S(1)} %copy-done.10, ...), custom_call_target="tpu_custom_call" | custom-call | flops 4831838208 | bytes 3145728 | tf_op jit(solution)/shard_map/middle/pallas_call | solution.py:94
  85.8 2.4 %collective-permute-start.33 = (f32[16,16,128]{2,1,0:T(8,128)S(1)}, f32[16,16,128]{2,1,0:T(8,128)S(1)}, u32[]{:S(2)}, u32[]{:S(2)}) collective-permute-start(f32[16,16,128]{2,1,0:T(8,128)S(1)} %get-tuple-element.93), channel_id=1, source_target_pairs={{0,12},{1,13},{2,14},{3,15},{4,8},{5,9},{6,10},{7,11},{8,4},{9,5},... | collective-permute-start | bytes 393224 | tf_op jit(solution)/shard_map/ppermute | solution.py:357
  89.5 4.1 %collective-permute-start.15 = (f32[16,16,128]{2,1,0:T(8,128)S(1)}, f32[16,16,128]{2,1,0:T(8,128)S(1)}, u32[]{:S(2)}, u32[]{:S(2)}) collective-permute-start(f32[16,16,128]{2,1,0:T(8,128)S(1)} %get-tuple-element.73), channel_id=1, source_target_pairs={{0,4},{1,5},{2,6},{3,7},{4,0},{5,1},{6,2},{7,3},{8,12},{9,13},{10,... | collective-permute-start | bytes 393224 | tf_op jit(solution)/shard_map/ppermute | solution.py:357
  95.2 2.7 %collective-permute-done.34.refs_8_ = f32[16,16,128]{2,1,0:T(8,128)S(1)} collective-permute-done((f32[16,16,128]{2,1,0:T(8,128)S(1)}, f32[16,16,128]{2,1,0:T(8,128)S(1)}, u32[]{:S(2)}, u32[]{:S(2)}) %collective-permute-start.34) | collective-permute-done | bytes 131104 | tf_op jit(solution)/shard_map/ppermute | solution.py:357
  100.1 2.0 %y_adjoint.3 = (f32[2,4,64,128]{3,2,1,0:T(8,128)S(1)}, f32[2,4,64,128]{3,2,1,0:T(8,128)S(1)}, f32[2,4,64,128]{3,2,1,0:T(8,128)S(1)}, f32[2,4,64,128]{3,2,1,0:T(8...) custom-call(s32[3]{0:T(128)S(1)} %copy-done.10, ...), custom_call_target="tpu_custom_call" | custom-call | flops 402653184 | bytes 3411968 | tf_op jit(solution)/shard_map/y_adjoint/pallas_call | solution.py:94
  102.2 6.5 %collective-permute-done.18.refs_6_ = f32[16,16,128]{2,1,0:T(8,128)S(1)} collective-permute-done((f32[16,16,128]{2,1,0:T(8,128)S(1)}, f32[16,16,128]{2,1,0:T(8,128)S(1)}, u32[]{:S(2)}, u32[]{:S(2)}) %collective-permute-start.18) | collective-permute-done | bytes 131104 | tf_op jit(solution)/shard_map/ppermute | solution.py:357
  108.7 7.8 %collective-permute-done.19.refs_7_ = f32[16,16,128]{2,1,0:T(8,128)S(1)} collective-permute-done((f32[16,16,128]{2,1,0:T(8,128)S(1)}, f32[16,16,128]{2,1,0:T(8,128)S(1)}, u32[]{:S(2)}, u32[]{:S(2)}) %collective-permute-start.19) | collective-permute-done | bytes 131104 | tf_op jit(solution)/shard_map/ppermute | solution.py:357
  116.5 5.4 %collective-permute-done.20.refs_8_ = f32[16,16,128]{2,1,0:T(8,128)S(1)} collective-permute-done((f32[16,16,128]{2,1,0:T(8,128)S(1)}, f32[16,16,128]{2,1,0:T(8,128)S(1)}, u32[]{:S(2)}, u32[]{:S(2)}) %collective-permute-start.20) | collective-permute-done | bytes 131104 | tf_op jit(solution)/shard_map/ppermute | solution.py:357
  123.1 4.9 %collective-permute-start.35 = (f32[2,4,64,128]{3,2,1,0:T(8,128)S(1)}, f32[2,4,64,128]{3,2,1,0:T(8,128)S(1)}, u32[]{:S(2)}, u32[]{:S(2)}) collective-permute-start(f32[2,4,64,128]{3,2,1,0:T(8,128)S(1)} %get-tuple-element.105), channel_id=1, source_target_pairs={{0,1},{1,0},{2,3},{3,2},{4,5},{5,4},{6,7},{7,6},{8,9},{9,8},{10,11... | collective-permute-start | bytes 786440 | tf_op jit(solution)/shard_map/ppermute | solution.py:357
  128.0 1.6 %y_adjoint.5 = (f32[2,4,64,128]{3,2,1,0:T(8,128)S(1)}, f32[2,4,64,128]{3,2,1,0:T(8,128)S(1)}, f32[2,4,64,128]{3,2,1,0:T(8,128)S(1)}, f32[2,4,64,128]{3,2,1,0:T(8,128)S(1)}, f32[8,128]{1,0:T(8,128)}) custom-call(s32[3]{0:T(128)S(1)} %copy-done.10, f32[16,16,128]{2,1,0:T(8,128)S(1)} %get-tuple-element.71.refs_1_, ...), custom_call_target="tpu_custom_call" | custom-call | flops 201326592 | bytes 3411968 | tf_op jit(solution)/shard_map/y_adjoint/pallas_call | solution.py:94
  134.2 3.3 %collective-permute-start.38 = (f32[4,64,128]{2,1,0:T(8,128)S(1)}, f32[4,64,128]{2,1,0:T(8,128)S(1)}, u32[]{:S(2)}, u32[]{:S(2)}) collective-permute-start(f32[4,64,128]{2,1,0:T(8,128)S(1)} %get-tuple-element.109), channel_id=1, source_target_pairs={{1,2},{2,1},{3,4},{4,3},{5,6},{6,5},{7,8},{8,7},{9,10},{10,9},{11,... | collective-permute-start | bytes 393224 | tf_op jit(solution)/shard_map/ppermute | solution.py:362
  137.6 4.6 %collective-permute-done.38.refs_5_ = f32[4,64,128]{2,1,0:T(8,128)S(1)} collective-permute-done((f32[4,64,128]{2,1,0:T(8,128)S(1)}, f32[4,64,128]{2,1,0:T(8,128)S(1)}, u32[]{:S(2)}, u32[]{:S(2)}) %collective-permute-start.38) | collective-permute-done | bytes 131104 | tf_op jit(solution)/shard_map/ppermute | solution.py:362
  144.1 1.9 %final.1 = (f32[8,64,128]{2,1,0:T(8,128)}, f32[3,8,64,128]{3,2,1,0:T(8,128)}) custom-call(s32[3]{0:T(128)S(1)} %copy-done.10, f32[8]{0:T(128)S(1)} %copy-done.11, f32[8,64,128]{2,1,0:T(8,128)S(1)} %copy-done.5, s32[8,128,128]{2,1,0:T(8,128)S(1)} %copy-done.3, f32[4,8,64,128]{3,2,1,0:T(8,128)S(1)} %laplace.1.refs_4_, ...), custom_call_target="tpu_custom_call" | custom-call | flops 2621440 | bytes 5537792 | tf_op jit(solution)/shard_map/final/pallas_call | solution.py:94
  (106 shorter events, 32.3 us)
Async XLA Ops:
  8.0 8.7 %collective-permute-start.1 = (f32[2,4,64,128]{3,2,1,0:T(8,128)}, f32[2,4,64,128]{3,2,1,0:T(8,128)S(1)}, u32[]{:S(2)}, u32[]{:S(2)}) collective-permute-start(f32[2,4,64,128]{3,2,1,0:T(8,128)} %get-tuple-element.61), channel_id=1, source_target_pairs={{0,16},{16,0},{1,17},{17,1},{2,18},{18,2},{3,19},{19,3},{4,20},{20... | collective-permute-start | bytes 786440 | tf_op jit(solution)/shard_map/ppermute | solution.py:357
  8.2 11.6 %collective-permute-start.2 = (f32[2,4,64,128]{3,2,1,0:T(8,128)}, f32[2,4,64,128]{3,2,1,0:T(8,128)S(1)}, u32[]{:S(2)}, u32[]{:S(2)}) collective-permute-start(f32[2,4,64,128]{3,2,1,0:T(8,128)} %get-tuple-element.62), channel_id=1, source_target_pairs={{0,16},{16,0},{1,17},{17,1},{2,18},{18,2},{3,19},{19,3},{4,20},{20... | collective-permute-start | bytes 786440 | tf_op jit(solution)/shard_map/ppermute | solution.py:357
  14.2 8.4 %collective-permute-start.3 = (f32[2,4,64,128]{3,2,1,0:T(8,128)S(1)}, f32[2,4,64,128]{3,2,1,0:T(8,128)S(1)}, u32[]{:S(2)}, u32[]{:S(2)}) collective-permute-start(f32[2,4,64,128]{3,2,1,0:T(8,128)S(1)} %get-tuple-element.59.refs_1_), channel_id=1, source_target_pairs={{0,1},{1,0},{2,3},{3,2},{4,5},{5,4},{6,7},{7,6},{8,9},{9,8},{10,11... | collective-permute-start | bytes 786440 | tf_op jit(solution)/shard_map/ppermute | solution.py:357
  27.8 9.4 %collective-permute-start.23 = (f32[16,16,128]{2,1,0:T(8,128)S(1)}, f32[16,16,128]{2,1,0:T(8,128)S(1)}, u32[]{:S(2)}, u32[]{:S(2)}) collective-permute-start(f32[16,16,128]{2,1,0:T(8,128)S(1)} %get-tuple-element.82), channel_id=1, source_target_pairs={{0,6},{1,7},{2,4},{3,5},{4,2},{5,3},{6,0},{7,1},{8,14},{9,15},{10,... | collective-permute-start | bytes 393224 | tf_op jit(solution)/shard_map/ppermute | solution.py:357
  29.1 9.6 %collective-permute-start.24 = (f32[16,16,128]{2,1,0:T(8,128)S(1)}, f32[16,16,128]{2,1,0:T(8,128)S(1)}, u32[]{:S(2)}, u32[]{:S(2)}) collective-permute-start(f32[16,16,128]{2,1,0:T(8,128)S(1)} %get-tuple-element.83), channel_id=1, source_target_pairs={{0,8},{1,9},{2,10},{3,11},{4,12},{5,13},{6,14},{7,15},{8,0},{9,1},... | collective-permute-start | bytes 393224 | tf_op jit(solution)/shard_map/ppermute | solution.py:357
  31.4 15.0 %collective-permute-start.25 = (f32[16,16,128]{2,1,0:T(8,128)S(1)}, f32[16,16,128]{2,1,0:T(8,128)S(1)}, u32[]{:S(2)}, u32[]{:S(2)}) collective-permute-start(f32[16,16,128]{2,1,0:T(8,128)S(1)} %get-tuple-element.84), channel_id=1, source_target_pairs={{0,10},{1,11},{2,8},{3,9},{4,14},{5,15},{6,12},{7,13},{8,2},{9,3},... | collective-permute-start | bytes 393224 | tf_op jit(solution)/shard_map/ppermute | solution.py:357
  34.2 16.3 %collective-permute-start.26 = (f32[16,16,128]{2,1,0:T(8,128)S(1)}, f32[16,16,128]{2,1,0:T(8,128)S(1)}, u32[]{:S(2)}, u32[]{:S(2)}) collective-permute-start(f32[16,16,128]{2,1,0:T(8,128)S(1)} %get-tuple-element.85), channel_id=1, source_target_pairs={{0,12},{1,13},{2,14},{3,15},{4,8},{5,9},{6,10},{7,11},{8,4},{9,5},... | collective-permute-start | bytes 393224 | tf_op jit(solution)/shard_map/ppermute | solution.py:357
  35.5 19.0 %collective-permute-start.27 = (f32[16,16,128]{2,1,0:T(8,128)S(1)}, f32[16,16,128]{2,1,0:T(8,128)S(1)}, u32[]{:S(2)}, u32[]{:S(2)}) collective-permute-start(f32[16,16,128]{2,1,0:T(8,128)S(1)} %get-tuple-element.86), channel_id=1, source_target_pairs={{0,14},{1,15},{2,12},{3,13},{4,10},{5,11},{6,8},{7,9},{8,6},{9,7},... | collective-permute-start | bytes 393224 | tf_op jit(solution)/shard_map/ppermute | solution.py:357
  37.2 17.4 %collective-permute-start.7 = (f32[16,16,128]{2,1,0:T(8,128)S(1)}, f32[16,16,128]{2,1,0:T(8,128)S(1)}, u32[]{:S(2)}, u32[]{:S(2)}) collective-permute-start(f32[16,16,128]{2,1,0:T(8,128)S(1)} %get-tuple-element.64), channel_id=1, source_target_pairs={{0,2},{1,3},{2,0},{3,1},{4,6},{5,7},{6,4},{7,5},{8,10},{9,11},{10,... | collective-permute-start | bytes 393224 | tf_op jit(solution)/shard_map/ppermute | solution.py:357
  38.7 17.6 %collective-permute-start.8 = (f32[16,16,128]{2,1,0:T(8,128)S(1)}, f32[16,16,128]{2,1,0:T(8,128)S(1)}, u32[]{:S(2)}, u32[]{:S(2)}) collective-permute-start(f32[16,16,128]{2,1,0:T(8,128)S(1)} %get-tuple-element.65), channel_id=1, source_target_pairs={{0,4},{1,5},{2,6},{3,7},{4,0},{5,1},{6,2},{7,3},{8,12},{9,13},{10,... | collective-permute-start | bytes 393224 | tf_op jit(solution)/shard_map/ppermute | solution.py:357
  46.4 19.1 %collective-permute-start.9 = (f32[16,16,128]{2,1,0:T(8,128)S(1)}, f32[16,16,128]{2,1,0:T(8,128)S(1)}, u32[]{:S(2)}, u32[]{:S(2)}) collective-permute-start(f32[16,16,128]{2,1,0:T(8,128)S(1)} %get-tuple-element.66), channel_id=1, source_target_pairs={{0,6},{1,7},{2,4},{3,5},{4,2},{5,3},{6,0},{7,1},{8,14},{9,15},{10,... | collective-permute-start | bytes 393224 | tf_op jit(solution)/shard_map/ppermute | solution.py:357
  50.5 16.3 %collective-permute-start.10 = (f32[16,16,128]{2,1,0:T(8,128)S(1)}, f32[16,16,128]{2,1,0:T(8,128)S(1)}, u32[]{:S(2)}, u32[]{:S(2)}) collective-permute-start(f32[16,16,128]{2,1,0:T(8,128)S(1)} %get-tuple-element.67), channel_id=1, source_target_pairs={{0,8},{1,9},{2,10},{3,11},{4,12},{5,13},{6,14},{7,15},{8,0},{9,1},... | collective-permute-start | bytes 393224 | tf_op jit(solution)/shard_map/ppermute | solution.py:357
  54.6 16.4 %collective-permute-start.11 = (f32[16,16,128]{2,1,0:T(8,128)S(1)}, f32[16,16,128]{2,1,0:T(8,128)S(1)}, u32[]{:S(2)}, u32[]{:S(2)}) collective-permute-start(f32[16,16,128]{2,1,0:T(8,128)S(1)} %get-tuple-element.68), channel_id=1, source_target_pairs={{0,10},{1,11},{2,8},{3,9},{4,14},{5,15},{6,12},{7,13},{8,2},{9,3},... | collective-permute-start | bytes 393224 | tf_op jit(solution)/shard_map/ppermute | solution.py:357
  54.6 17.9 %collective-permute-start.12 = (f32[16,16,128]{2,1,0:T(8,128)S(1)}, f32[16,16,128]{2,1,0:T(8,128)S(1)}, u32[]{:S(2)}, u32[]{:S(2)}) collective-permute-start(f32[16,16,128]{2,1,0:T(8,128)S(1)} %get-tuple-element.69), channel_id=1, source_target_pairs={{0,12},{1,13},{2,14},{3,15},{4,8},{5,9},{6,10},{7,11},{8,4},{9,5},... | collective-permute-start | bytes 393224 | tf_op jit(solution)/shard_map/ppermute | solution.py:357
  56.2 20.1 %collective-permute-start.13 = (f32[16,16,128]{2,1,0:T(8,128)S(1)}, f32[16,16,128]{2,1,0:T(8,128)S(1)}, u32[]{:S(2)}, u32[]{:S(2)}) collective-permute-start(f32[16,16,128]{2,1,0:T(8,128)S(1)} %get-tuple-element.70), channel_id=1, source_target_pairs={{0,14},{1,15},{2,12},{3,13},{4,10},{5,11},{6,8},{7,9},{8,6},{9,7},... | collective-permute-start | bytes 393224 | tf_op jit(solution)/shard_map/ppermute | solution.py:357
  65.5 20.4 %collective-permute-start.28 = (f32[16,16,128]{2,1,0:T(8,128)S(1)}, f32[16,16,128]{2,1,0:T(8,128)S(1)}, u32[]{:S(2)}, u32[]{:S(2)}) collective-permute-start(f32[16,16,128]{2,1,0:T(8,128)S(1)} %get-tuple-element.88), channel_id=1, source_target_pairs={{0,2},{1,3},{2,0},{3,1},{4,6},{5,7},{6,4},{7,5},{8,10},{9,11},{10,... | collective-permute-start | bytes 393224 | tf_op jit(solution)/shard_map/ppermute | solution.py:357
  66.8 21.5 %collective-permute-start.29 = (f32[16,16,128]{2,1,0:T(8,128)S(1)}, f32[16,16,128]{2,1,0:T(8,128)S(1)}, u32[]{:S(2)}, u32[]{:S(2)}) collective-permute-start(f32[16,16,128]{2,1,0:T(8,128)S(1)} %get-tuple-element.89), channel_id=1, source_target_pairs={{0,4},{1,5},{2,6},{3,7},{4,0},{5,1},{6,2},{7,3},{8,12},{9,13},{10,... | collective-permute-start | bytes 393224 | tf_op jit(solution)/shard_map/ppermute | solution.py:357
  70.9 17.3 %collective-permute-start.30 = (f32[16,16,128]{2,1,0:T(8,128)S(1)}, f32[16,16,128]{2,1,0:T(8,128)S(1)}, u32[]{:S(2)}, u32[]{:S(2)}) collective-permute-start(f32[16,16,128]{2,1,0:T(8,128)S(1)} %get-tuple-element.90), channel_id=1, source_target_pairs={{0,6},{1,7},{2,4},{3,5},{4,2},{5,3},{6,0},{7,1},{8,14},{9,15},{10,... | collective-permute-start | bytes 393224 | tf_op jit(solution)/shard_map/ppermute | solution.py:357
  72.4 17.1 %collective-permute-start.31 = (f32[16,16,128]{2,1,0:T(8,128)S(1)}, f32[16,16,128]{2,1,0:T(8,128)S(1)}, u32[]{:S(2)}, u32[]{:S(2)}) collective-permute-start(f32[16,16,128]{2,1,0:T(8,128)S(1)} %get-tuple-element.91), channel_id=1, source_target_pairs={{0,8},{1,9},{2,10},{3,11},{4,12},{5,13},{6,14},{7,15},{8,0},{9,1},... | collective-permute-start | bytes 393224 | tf_op jit(solution)/shard_map/ppermute | solution.py:357
  76.3 17.3 %collective-permute-start.32 = (f32[16,16,128]{2,1,0:T(8,128)S(1)}, f32[16,16,128]{2,1,0:T(8,128)S(1)}, u32[]{:S(2)}, u32[]{:S(2)}) collective-permute-start(f32[16,16,128]{2,1,0:T(8,128)S(1)} %get-tuple-element.92), channel_id=1, source_target_pairs={{0,10},{1,11},{2,8},{3,9},{4,14},{5,15},{6,12},{7,13},{8,2},{9,3},... | collective-permute-start | bytes 393224 | tf_op jit(solution)/shard_map/ppermute | solution.py:357
  85.8 9.0 %collective-permute-start.33 = (f32[16,16,128]{2,1,0:T(8,128)S(1)}, f32[16,16,128]{2,1,0:T(8,128)S(1)}, u32[]{:S(2)}, u32[]{:S(2)}) collective-permute-start(f32[16,16,128]{2,1,0:T(8,128)S(1)} %get-tuple-element.93), channel_id=1, source_target_pairs={{0,12},{1,13},{2,14},{3,15},{4,8},{5,9},{6,10},{7,11},{8,4},{9,5},... | collective-permute-start | bytes 393224 | tf_op jit(solution)/shard_map/ppermute | solution.py:357
  88.3 9.6 %collective-permute-start.34 = (f32[16,16,128]{2,1,0:T(8,128)S(1)}, f32[16,16,128]{2,1,0:T(8,128)S(1)}, u32[]{:S(2)}, u32[]{:S(2)}) collective-permute-start(f32[16,16,128]{2,1,0:T(8,128)S(1)} %get-tuple-element.94), channel_id=1, source_target_pairs={{0,14},{1,15},{2,12},{3,13},{4,10},{5,11},{6,8},{7,9},{8,6},{9,7},... | collective-permute-start | bytes 393224 | tf_op jit(solution)/shard_map/ppermute | solution.py:357
  88.3 10.8 %collective-permute-start.14 = (f32[16,16,128]{2,1,0:T(8,128)S(1)}, f32[16,16,128]{2,1,0:T(8,128)S(1)}, u32[]{:S(2)}, u32[]{:S(2)}) collective-permute-start(f32[16,16,128]{2,1,0:T(8,128)S(1)} %get-tuple-element.72), channel_id=1, source_target_pairs={{0,2},{1,3},{2,0},{3,1},{4,6},{5,7},{6,4},{7,5},{8,10},{9,11},{10,... | collective-permute-start | bytes 393224 | tf_op jit(solution)/shard_map/ppermute | solution.py:357
  89.5 9.5 %collective-permute-start.15 = (f32[16,16,128]{2,1,0:T(8,128)S(1)}, f32[16,16,128]{2,1,0:T(8,128)S(1)}, u32[]{:S(2)}, u32[]{:S(2)}) collective-permute-start(f32[16,16,128]{2,1,0:T(8,128)S(1)} %get-tuple-element.73), channel_id=1, source_target_pairs={{0,4},{1,5},{2,6},{3,7},{4,0},{5,1},{6,2},{7,3},{8,12},{9,13},{10,... | collective-permute-start | bytes 393224 | tf_op jit(solution)/shard_map/ppermute | solution.py:357
  93.7 8.5 %collective-permute-start.16 = (f32[16,16,128]{2,1,0:T(8,128)S(1)}, f32[16,16,128]{2,1,0:T(8,128)S(1)}, u32[]{:S(2)}, u32[]{:S(2)}) collective-permute-start(f32[16,16,128]{2,1,0:T(8,128)S(1)} %get-tuple-element.74), channel_id=1, source_target_pairs={{0,6},{1,7},{2,4},{3,5},{4,2},{5,3},{6,0},{7,1},{8,14},{9,15},{10,... | collective-permute-start | bytes 393224 | tf_op jit(solution)/shard_map/ppermute | solution.py:357
  97.8 10.9 %collective-permute-start.18 = (f32[16,16,128]{2,1,0:T(8,128)S(1)}, f32[16,16,128]{2,1,0:T(8,128)S(1)}, u32[]{:S(2)}, u32[]{:S(2)}) collective-permute-start(f32[16,16,128]{2,1,0:T(8,128)S(1)} %get-tuple-element.76), channel_id=1, source_target_pairs={{0,10},{1,11},{2,8},{3,9},{4,14},{5,15},{6,12},{7,13},{8,2},{9,3},... | collective-permute-start | bytes 393224 | tf_op jit(solution)/shard_map/ppermute | solution.py:357
  99.0 17.5 %collective-permute-start.19 = (f32[16,16,128]{2,1,0:T(8,128)S(1)}, f32[16,16,128]{2,1,0:T(8,128)S(1)}, u32[]{:S(2)}, u32[]{:S(2)}) collective-permute-start(f32[16,16,128]{2,1,0:T(8,128)S(1)} %get-tuple-element.77), channel_id=1, source_target_pairs={{0,12},{1,13},{2,14},{3,15},{4,8},{5,9},{6,10},{7,11},{8,4},{9,5},... | collective-permute-start | bytes 393224 | tf_op jit(solution)/shard_map/ppermute | solution.py:357
  99.0 22.9 %collective-permute-start.20 = (f32[16,16,128]{2,1,0:T(8,128)S(1)}, f32[16,16,128]{2,1,0:T(8,128)S(1)}, u32[]{:S(2)}, u32[]{:S(2)}) collective-permute-start(f32[16,16,128]{2,1,0:T(8,128)S(1)} %get-tuple-element.78), channel_id=1, source_target_pairs={{0,14},{1,15},{2,12},{3,13},{4,10},{5,11},{6,8},{7,9},{8,6},{9,7},... | collective-permute-start | bytes 393224 | tf_op jit(solution)/shard_map/ppermute | solution.py:357
  130.2 12.0 %collective-permute-start.39 = (f32[576,128]{1,0:T(8,128)S(1)}, f32[576,128]{1,0:T(8,128)S(1)}, u32[]{:S(2)}, u32[]{:S(2)}) collective-permute-start(f32[576,128]{1,0:T(8,128)S(1)} %pack.2.refs_4_), channel_id=1, source_target_pairs={{0,16},{16,0},{1,17},{17,1},{2,18},{18,2},{3,19},{19,3},{4,20},{20... | collective-permute-start | bytes 884744 | tf_op jit(solution)/shard_map/ppermute | solution.py:357
  132.5 11.0 %collective-permute-start.40 = (f32[2,4,64,128]{3,2,1,0:T(8,128)S(1)}, f32[2,4,64,128]{3,2,1,0:T(8,128)S(1)}, u32[]{:S(2)}, u32[]{:S(2)}) collective-permute-start(f32[2,4,64,128]{3,2,1,0:T(8,128)S(1)} %get-tuple-element.112), channel_id=1, source_target_pairs={{0,1},{1,0},{2,3},{3,2},{4,5},{5,4},{6,7},{7,6},{8,9},{9,8},{10,11... | collective-permute-start | bytes 786440 | tf_op jit(solution)/shard_map/ppermute | solution.py:357
  132.5 10.9 %collective-permute-start.41 = (f32[2,4,64,128]{3,2,1,0:T(8,128)S(1)}, f32[2,4,64,128]{3,2,1,0:T(8,128)S(1)}, u32[]{:S(2)}, u32[]{:S(2)}) collective-permute-start(f32[2,4,64,128]{3,2,1,0:T(8,128)S(1)} %get-tuple-element.113), channel_id=1, source_target_pairs={{0,1},{1,0},{2,3},{3,2},{4,5},{5,4},{6,7},{7,6},{8,9},{9,8},{10,11... | collective-permute-start | bytes 786440 | tf_op jit(solution)/shard_map/ppermute | solution.py:357
  133.0 11.1 %collective-permute-start.42 = (f32[512,128]{1,0:T(8,128)S(1)}, f32[512,128]{1,0:T(8,128)S(1)}, u32[]{:S(2)}, u32[]{:S(2)}) collective-permute-start(f32[512,128]{1,0:T(8,128)S(1)} %pack.3.refs_5_), channel_id=1, source_target_pairs={{0,16},{16,0},{1,17},{17,1},{2,18},{18,2},{3,19},{19,3},{4,20},{20... | collective-permute-start | bytes 786440 | tf_op jit(solution)/shard_map/ppermute | solution.py:357
  (28 other events, 547.7 us)

commit v3 on v2

--- a/solution.py
+++ b/solution.py
@@ -70,7 +70,7 @@
     return pl.BlockSpec(tuple(shape), lambda step, rank=len(shape): (0,) * rank)
 
 
-def call(kernel, outs, scalars, operands, scratch, flops, name, blocks=None, first=(), vmem=48):
+def call(kernel, outs, scalars, operands, scratch, flops, name, blocks=None, first=(), vmem=48, out_blocks=None, carried=()):
     blocks = blocks or {}
     inputs = len(scalars) + len(operands)
     specs = [SMEM] * len(scalars)
@@ -86,7 +86,9 @@
             shape = operand.shape
             specs.append(whole(shape))
         moved += int(np.prod(shape)) * operand.dtype.itemsize
+    first = (*first, *carried)
     specs += [pl.BlockSpec(memory_space=pl.ANY)] * len(first)
+    aliases = {len(specs) - len(carried) + i: i for i in range(len(carried))}
 
     def run(*refs):
         kernel(*refs[:inputs], *refs[inputs + len(first) :])
@@ -96,7 +98,11 @@
         grid=(1,),
         out_shape=[jax.ShapeDtypeStruct(shape, F32) for shape in outs],
         in_specs=specs,
-        out_specs=[whole(shape) for shape in outs],
+        out_specs=[
+            pl.BlockSpec(shape, lambda step, index=index: index)
+            for shape, index in out_blocks or [(shape, (0,) * len(shape)) for shape in outs]
+        ],
+        input_output_aliases=aliases,
         scratch_shapes=scratch,
         compiler_params=pltpu.CompilerParams(vmem_limit_bytes=vmem * 1024 * 1024),
         cost_estimate=pl.CostEstimate(flops=int(flops), bytes_accessed=int(moved), transcendentals=0),
@@ -167,34 +173,30 @@
             out[f, p] = 6.0 * centre - beside
 
 
-def object_kernel(which, grid, place, params, amp, disp, sup, *outs):
+def object_kernel(which, grid, place, *refs):
+    params, (amp, disp, sup), outs = refs[: len(which)], refs[len(which) : len(which) + 3], refs[len(which) + 3 :]
     planes, rows, depth = amp.shape
     first = pl.multiple_of(place[2] * rows, rows)
     zed = lax.broadcasted_iota(jnp.int32, (rows, depth), 1).astype(F32) * (1.0 / grid)
-    each = len(outs) // len(which)
-    portion = planes // (each - 1)
-
-    for part in range(each - 1):
-
-        def plane(i, carry, part=part):
-            p = part * portion + i
-            weight = sup[p, pl.ds(first, rows), :].astype(F32) * amp[p]
-            parts = [disp[0, p], disp[1, p], disp[2, p]]
-            for at, k in enumerate(which):
-                phase = params[4 * k] * parts[0] + params[4 * k + 1] * parts[1] + params[4 * k + 2] * parts[2]
-                shifted = params[4 * k + 3] * zed
-                turns = phase * (0.5 / np.pi) + (shifted - jnp.floor(shifted))
-                turns = turns - jnp.floor(turns + 0.5)
-                square = turns * turns
-                cosine = series(COS_FIT, square)
-                sine = series(SIN_FIT, square) * turns
-                outs[each * at][0, p] = cosine
-                outs[each * at][1, p] = sine
-                outs[each * at + 1 + part][0, i] = weight * cosine
-                outs[each * at + 1 + part][1, i] = weight * sine
-            return carry
-
-        lax.fori_loop(0, portion, plane, 0)
+
+    def plane(p, carry):
+        weight = sup[p, pl.ds(first, rows), :].astype(F32) * amp[p]
+        parts = [disp[0, p], disp[1, p], disp[2, p]]
+        for at, param in enumerate(params):
+            phase = param[0] * parts[0] + param[1] * parts[1] + param[2] * parts[2]
+            shifted = param[3] * zed
+            turns = phase * (0.5 / np.pi) + (shifted - jnp.floor(shifted))
+            turns = turns - jnp.floor(turns + 0.5)
+            square = turns * turns
+            cosine = series(COS_FIT, square)
+            sine = series(SIN_FIT, square) * turns
+            outs[2 * at][0, p] = cosine
+            outs[2 * at][1, p] = sine
+            outs[2 * at + 1][0, p] = weight * cosine
+            outs[2 * at + 1][1, p] = weight * sine
+        return carry
+
+    lax.fori_loop(0, planes, plane, 0)
 
 
 def y_forward_kernel(refls, chips, splits, targets, place, *refs):
@@ -247,7 +249,8 @@
     edge = group * chips
     grid = 2 * edge
     batch = gather.shape[1] // depth
-    load = pltpu.make_async_copy(intensity.at[0, :, first : first + rows, :], measured, arrived)
+    held = first // 8 * 8
+    load = pltpu.make_async_copy(intensity.at[0, :, held : held + measured.shape[1], :], measured, arrived)
     load.start()
 
     def place_of(c, k):
@@ -266,7 +269,7 @@
             lines = [one[c * grid : (c + 1) * grid, j * depth : (j + 1) * depth] for c in range(2)]
             spectrum = dot_pairs(halves(jnp.concatenate(lines, axis=1)), bwd)
             real, imag = spectrum[:, :grid], spectrum[:, grid:]
-            excess = 4.0 * (real * real + imag * imag - measured[:, key + j, :])
+            excess = 4.0 * (real * real + imag * imag - measured[:, first - held + key + j, :])
             back.append(dot_pairs(halves(jnp.concatenate([excess * real, excess * imag], axis=1)), fwd))
         lines = [jnp.concatenate([b[:, c * depth : (c + 1) * depth] for b in back], axis=1) for c in range(2)]
         scatter[...] = dot_pairs(bwd, halves(jnp.concatenate(lines, axis=0)))
@@ -276,9 +279,9 @@
                     outs[k][:, (key + j) * 2 + c, :] = scatter[place_of(c, k), j * depth : (j + 1) * depth]
 
 
-def y_adjoint_kernel(refls, chips, jobs, place, *refs):
+def y_adjoint_kernel(chips, jobs, parts, place, *refs):
     got, tables = refs[:chips], refs[chips]
-    total = refls * len(jobs)
+    total = len(parts) * len(jobs)
     adds, outs = refs[chips + 1 : -2 - total], refs[-2 - total : -2]
     done, hold = refs[-2:]
     done[...] = jnp.zeros_like(done)
@@ -288,7 +291,7 @@
 
     def order(which):
         pieces = []
-        for q in range(refls):
+        for q in parts:
             for c in range(2):
                 at = pl.multiple_of(((refl ^ q) * 2 + c) * rows, rows)
                 pieces.append(tables[core, which, pl.ds(at, rows), :])
@@ -306,50 +309,45 @@
         for p in range(0, planes, 2):
             lane = (job * planes + p) * depth
             result = dot_pairs(table, halves(hold[:, lane : lane + 2 * depth]))
-            for k in range(refls):
+            for i in range(len(parts)):
                 for c in range(2):
-                    at = (k * 2 + c) * rows
+                    at = (i * 2 + c) * rows
                     for j in range(2):
                         value = result[at : at + rows, j * depth : (j + 1) * depth]
                         if adds:
-                            value = value + adds[job * refls + k][c, p + j]
-                        outs[job * refls + k][c, p + j] = value
-
-
-def final_kernel(refls, splits, place, params, *refs):
-    amp, sup, lapped = refs[:3]
-    own, mate = refs[3 : 3 + splits], refs[3 + splits : 3 + 2 * splits]
-    others = refs[3 + 2 * splits : 3 + (1 + refls) * splits]
-    phases = refs[3 + (1 + refls) * splits : -2]
+                            value = value + adds[job * len(parts) + i][c, p + j]
+                        outs[job * len(parts) + i][c, p + j] = value
+
+
+def final_kernel(refls, place, *refs):
+    params = refs[:refls]
+    amp, sup, lapped, own, mate = refs[refls : refls + 5]
+    others, phases = refs[refls + 5 : 2 * refls + 4], refs[2 * refls + 4 : -2]
     out_amp, out_disp = refs[-2:]
     planes, rows, depth = amp.shape
     first = pl.multiple_of(place[2] * rows, rows)
-    portion = planes // splits
-
-    for part in range(splits):
-
-        def plane(i, carry, part=part):
-            p = part * portion + i
-            mask = sup[p, pl.ds(first, rows), :].astype(F32)
-            weight = mask * amp[p]
-            total = jnp.zeros((rows, depth), F32)
-            moved = [jnp.zeros((rows, depth), F32) for _ in range(3)]
-            for k in range(refls):
-                if k == 0:
-                    real, imag = [own[part][c, i] + mate[part][c, i] for c in range(2)]
-                else:
-                    at = [pl.ds(pl.multiple_of((c * portion + i) * rows, rows), rows) for c in range(2)]
-                    real, imag = [others[(k - 1) * splits + part][at[c], :] for c in range(2)]
-                cosine, sine = phases[k][0, p], phases[k][1, p]
-                total = total + (real * cosine + imag * sine)
-                across = weight * (imag * cosine - real * sine)
-                moved = [m + params[4 * k + c] * across for c, m in enumerate(moved)]
-            out_amp[p] = mask * total + (2.0 * EDGE_WEIGHT) * (mask * lapped[0, p])
-            for c in range(3):
-                out_disp[c, p] = moved[c] + (2.0 * STRAIN_WEIGHT) * lapped[c + 1, p]
-            return carry
-
-        lax.fori_loop(0, portion, plane, 0)
+
+    def plane(p, carry):
+        mask = sup[p, pl.ds(first, rows), :].astype(F32)
+        weight = mask * amp[p]
+        total = jnp.zeros((rows, depth), F32)
+        moved = [jnp.zeros((rows, depth), F32) for _ in range(3)]
+        for k in range(refls):
+            if k == 0:
+                real, imag = [own[c, p] + mate[c, p] for c in range(2)]
+            else:
+                at = [pl.ds(pl.multiple_of((c * planes + p) * rows, rows), rows) for c in range(2)]
+                real, imag = [others[k - 1][at[c], :] for c in range(2)]
+            cosine, sine = phases[k][0, p], phases[k][1, p]
+            total = total + (real * cosine + imag * sine)
+            across = weight * (imag * cosine - real * sine)
+            moved = [m + params[k][c] * across for c, m in enumerate(moved)]
+        out_amp[p] = mask * total + (2.0 * EDGE_WEIGHT) * (mask * lapped[0, p])
+        for c in range(3):
+            out_disp[c, p] = moved[c] + (2.0 * STRAIN_WEIGHT) * lapped[c + 1, p]
+        return carry
+
+    lax.fori_loop(0, planes, plane, 0)
 
 
 def swap(x, axis, bits):
@@ -395,29 +393,36 @@
 
     own_params = jnp.concatenate([miller[0].astype(F32), shift_kz.astype(F32)])
     fields = (amplitude, displacement, support)
-    def make(params, which, parts, vmem=48):
+    def part_blocks(part, start=0):
+        return {
+            start: ((portion, rows, depth), (part, 0, 0)),
+            start + 1: ((3, portion, rows, depth), (0, part, 0, 0)),
+            start + 2: ((portion, rows * refls, depth), (part, 0, 0)),
+        }
+
+    def make(part, which, vmem=48, first=()):
         made = call(
             functools.partial(object_kernel, which, grid),
-            ([(2, planes, rows, depth)] + [(2, planes // parts, rows, depth)] * parts) * len(which),
-            [place, params],
+            [part_shape] * (2 * len(which)),
+            [place, *[params[k] for k in which]],
             fields,
             [],
-            50 * len(which) * cells,
+            50 * len(which) * cells // splits,
             "object",
-            vmem=vmem,
+            part_blocks(part),
+            first,
+            vmem,
         )
-        return [made[i * (parts + 1) : (i + 1) * (parts + 1)] for i in range(len(which))]
-
-    ((own_phase, *own_parts),) = make(own_params, [0], splits)
-    params = jnp.concatenate([own_params] + [swap(own_params, "refl", k) for k in range(1, refls)])
-    made = make(params, list(range(1, refls)), splits, vmem=60)
-    phases = [own_phase] + [one[0] for one in made]
+        return {k: made[2 * i : 2 * i + 2] for i, k in enumerate(which)}
+
+    params = [own_params] + [swap(own_params, "refl", k) for k in range(1, refls)]
+    made = [make(0, list(range(1, refls)), 60)]
+    made += [make(part, list(range(1, refls)), 60, [made[0][1][1]]) for part in range(1, splits)]
+    held = [swap(made[part][k][1], "refl", k) for k in range(1, refls) for part in range(splits)]
+    for part in range(splits):
+        made[part].update(make(part, [0]))
+    own_parts = [made[part][0][1] for part in range(splits)]
     own_mates = [swap(x, "slab", 1) for x in own_parts]
-    held = [[swap(one[1], "refl", k + 1) for k, one in enumerate(made)]]
-    for part in range(1, splits):
-        held.append([swap(one[1 + part], "refl", k + 1) for k, one in enumerate(made)])
-
-    held = [x for part in zip(*held) for x in part]
     mates = [swap(x, "slab", 1) for x in held]
 
     def y_forward(at, targets, first=()):
@@ -433,69 +438,71 @@
         )
         return dict(zip(targets, made))
 
-    def middle(at, got, first=()):
-        count = pieces[at]
+    def middle(at, got):
+        first, count = sum(pieces[:at]), pieces[at]
+        held = -(-(first + count) // 8) * 8 - first // 8 * 8
         return call(
-            functools.partial(middle_kernel, chips, sum(pieces[:at])),
+            functools.partial(middle_kernel, chips, first),
             [(group, 2 * count, depth)] * chips,
             [place],
             (*got, intensity, *constants),
-            [pltpu.VMEM((2 * edge, min(count, 8) * depth), F32)] * 2
-            + [pltpu.VMEM((grid, count, grid), F32), pltpu.SemaphoreType.DMA],
+            [pltpu.VMEM((2 * edge, (count if count < 8 else count // 2 if count > 8 else 8) * depth), F32)] * 2
+            + [pltpu.VMEM((grid, held, grid), F32), pltpu.SemaphoreType.DMA],
             6 * count * (2 * edge * 2 * grid * depth * 2 + grid * 2 * depth * 2 * grid * 2),
             "middle",
             {chips: None},
-            first,
         )
 
-    def y_adjoint(at, got, jobs, adds, first=()):
+    def y_adjoint(at, got, jobs, parts, adds=None, first=()):
         count = pieces[at]
         made = call(
-            functools.partial(y_adjoint_kernel, refls, chips, jobs),
-            [part_shape] * (refls * len(jobs)) + [(8, 128)],
+            functools.partial(y_adjoint_kernel, chips, jobs, parts),
+            [part_shape] * (len(parts) * len(jobs)) + [(8, 128)],
             [place],
-            (*got, y_tables(at)[1], *[x for job in adds for x in job]),
+            (*got, y_tables(at)[1], *([adds[job][k] for job in jobs for k in parts] if adds else [])),
             [pltpu.VMEM((chips * 2 * count, len(jobs) * portion * depth), F32)],
-            6 * len(jobs) * portion * depth * 2 * edge * chips * 2 * count,
+            6 * len(jobs) * portion * depth * len(parts) * 2 * rows * chips * 2 * count,
             "y_adjoint",
             first=first,
         )
-        return [made[i * refls : (i + 1) * refls] for i in range(len(jobs))], made[-1]
+        each = len(parts)
+        return {job: dict(zip(parts, made[i * each : (i + 1) * each])) for i, job in enumerate(jobs)}, made[-1]
 
     def cross(sends):
         return [sends[0]] + [swap(sends[k], "slab", 2 * k) for k in range(1, chips)]
 
     sends = [y_forward(at, list(range(chips))) for at in range(len(pieces))]
-    jobs = [(mate, part * portion) for part in range(splits) for mate in (True, False)]
-    adds = []
+    jobs = {mate: [(mate, part * portion) for part in range(splits)] for mate in (True, False)}
+    everyone = list(range(refls))
+    adds = None
     for at in range(len(pieces)):
         backs = middle(at, cross(sends[at]))
         returned = cross(backs)
         if at + 1 < len(pieces):
-            adds, unused = y_adjoint(at, returned, jobs, adds)
-    sums = []
-    own, mates, others = [], [], [[] for _ in range(1, refls)]
-    mate_jobs = [job for job in range(len(jobs)) if jobs[job][0]]
-    mine_jobs = [job for job in range(len(jobs)) if not jobs[job][0]]
-    for_mate, first_done = y_adjoint(at, returned, [jobs[i] for i in mate_jobs], [adds[i] for i in mate_jobs if adds])
-    mine, unused = y_adjoint(at, returned, [jobs[i] for i in mine_jobs], [adds[i] for i in mine_jobs if adds], (first_done,))
+            adds, unused = y_adjoint(at, returned, jobs[True] + jobs[False], everyone, adds)
+
+    for_mate, done = y_adjoint(at, returned, jobs[True], everyone[1:], adds)
+    mine, unused = y_adjoint(at, returned, jobs[False], everyone[1:], adds, (done,))
+    sums, others = [], [[] for _ in range(1, refls)]
     for part in range(splits):
-        from_mate = [swap(x, "slab", 1) for x in for_mate[part]]
-        own.append(mine[part][0])
-        mates.append(from_mate[0])
         for k in range(1, refls):
             shape = (2 * portion * rows + (8 * planes if part == 0 else 0), depth)
+            from_mate = swap(for_mate[jobs[True][part]][k], "slab", 1)
             (total,) = call(
                 functools.partial(pack_kernel, part == 0),
                 [shape],
                 [place],
-                (mine[part][k], from_mate[k], *fields),
+                (mine[jobs[False][part]][k], from_mate, *fields),
                 [],
                 4 * cells,
                 "pack",
             )
             sums.append(total)
             others[k - 1].append(swap(total, "refl", k))
+    for_mate, unused = y_adjoint(at, returned, jobs[True], everyone[:1], adds, sums)
+    mine, unused = y_adjoint(at, returned, jobs[False], everyone[:1], adds, sums)
+    mates = [swap(for_mate[job][0], "slab", 1) for job in jobs[True]]
+    own = [mine[job][0] for job in jobs[False]]
     edges = call(edges_kernel, [(4, rows, depth)] * 2, [place], fields, [], cells, "edges", first=sums)
     halos = (swap(edges[0], "slab", 1), swap_outward(edges[1], "slab"), *[one[0] for one in others])
     (lapped,) = call(
@@ -507,19 +514,33 @@
         30 * cells,
         "laplace",
     )
-    others = [x for one in others for x in one]
-
-    return tuple(
-        call(
-            functools.partial(final_kernel, refls, splits),
+    result = ()
+    for part in range(splits):
+        result = call(
+            functools.partial(final_kernel, refls),
             [(planes, rows, depth), (3, planes, rows, depth)],
-            [place, params],
-            (amplitude, support, lapped, *own, *mates, *others, *phases),
+            [place, *params],
+            (
+                amplitude,
+                support,
+                lapped,
+                own[part],
+                mates[part],
+                *[one[part] for one in others],
+                *[made[part][k][0] for k in range(refls)],
+            ),
             [],
-            20 * refls * cells,
+            20 * refls * cells // splits,
             "final",
+            {
+                0: ((portion, rows, depth), (part, 0, 0)),
+                1: ((portion, rows * refls, depth), (part, 0, 0)),
+                2: ((4, portion, rows, depth), (0, part, 0, 0)),
+            },
+            out_blocks=[((portion, rows, depth), (part, 0, 0)), ((3, portion, rows, depth), (0, part, 0, 0))],
+            carried=result,
         )
-    )
+    return tuple(result)
 
 
 def solution(mesh):

time: 147 us -> 146 us (level)
  Pallas kernels: 35.6 us -> 41.5 us
  waiting for transfers between devices: 50 us -> 47.4 us
  starting transfers between devices: 52.1 us -> 49.6 us
    pallas_call x14 -> x19, Pallas kernels: 35.6 us -> 41.5 us  [call(): pl.pallas_call(run, grid=(1,), out_shape=[jax.ShapeDtypeStruct(shape, F32...]
    ppermute x42, starting transfers between devices: 48.8 us -> 46.3 us  [swap(): return lax.ppermute(x, axis, [(i, i ^ bits) for i in range(count)])]
    unnamed x34 -> x38, local copies, waits for them, and re-layouts: 4.72 us -> 4.42 us
  transfers between devices with their start and end apart: 43 -> 43, of which waited for: 16 -> 14; matrix products, arithmetic and copies ran while one was open for 0% -> 0% of each run, Pallas kernels for 19% -> 24%
where the time goes in v3:
time: 146 us
  starting transfers between devices  49.6 us (34%)
  waiting for transfers between devices  47.4 us (32%)
  Pallas kernels  41.5 us (28%)
  local copies, waits for them, and re-layouts  4.42 us (3%)
  between operations  1.61 us (1%)
    ppermute x42, starting transfers between devices, swap(): return lax.ppermute(x, axis, [(i, i ^ bits) for i in range(count)])  46.3 us
    ppermute x42, waiting for transfers between devices, swap(): return lax.ppermute(x, axis, [(i, i ^ bits) for i in range(count)])  44.3 us
    pallas_call x19, Pallas kernels, call(): pl.pallas_call(run, grid=(1,), out_shape=[jax.ShapeDtypeStruct(shape, F32...  41.5 us
    unnamed x38, local copies, waits for them, and re-layouts  4.42 us
    ppermute x1, starting transfers between devices, swap_outward(): lax.ppermute(x, axis, [pair for i in range(1, count - 1, 2) for pair in (...  3.32 us
    ppermute x1, waiting for transfers between devices, swap_outward(): lax.ppermute(x, axis, [pair for i in range(1, count - 1, 2) for pair in (...  3.19 us
  transfers between devices with their start and end apart: 43, of which 14 were waited for; matrix products, arithmetic and copies ran while one was open for 0% of the time, Pallas kernels for 24%

profile of v3, /device:TPU:13, one launch (start us, length us, event | category | flops | bytes accessed | tf_op | source)
XLA Modules:
  0.0 146.0 jit_solution(2893762389174626660)
XLA Ops:
  2.9 1.5 %collective-permute-done.refs_1_.refs_2_ = f32[4]{0:T(128)S(1)} collective-permute-done((f32[4]{0:T(128)S(1)}, f32[4]{0:T(128)S(1)}, u32[]{:S(2)}, u32[]{:S(2)}) %collective-permute-start) | collective-permute-done | bytes 48 | tf_op jit(solution)/shard_map/ppermute | solution.py:355
  5.1 2.2 %object.6 = (f32[2,4,64,128]{3,2,1,0:T(8,128)}, f32[2,4,64,128]{3,2,1,0:T(8,128)}) custom-call(s32[3]{0:T(128)} %pad_add_fusion.refs_0_, f32[4]{0:T(128)} %copy-done.12, f32[8,64,128]{2,1,0:T(8,128)} %refs_3_.19, f32[3,8,64,128]{3,2,1,0:T(8,128)} %refs_2_.11, s32[8,128,128]{2,1,0:T(8,128)} %refs_4_.15), custom_call_target="tpu_custom_call" | custom-call | flops 1638400 | bytes 1310720 | tf_op jit(solution)/shard_map/object/pallas_call | solution.py:96
  7.5 2.3 %object.7 = (f32[2,4,64,128]{3,2,1,0:T(8,128)}, f32[2,4,64,128]{3,2,1,0:T(8,128)}) custom-call(s32[3]{0:T(128)} %pad_add_fusion.refs_0_, f32[4]{0:T(128)} %copy-done.12, f32[8,64,128]{2,1,0:T(8,128)} %refs_3_.19, f32[3,8,64,128]{3,2,1,0:T(8,128)} %refs_2_.11, s32[8,128,128]{2,1,0:T(8,128)} %refs_4_.15, f32[2,4,64,128]{3,2,1,0:T(8,128)} %get-tuple-element.65.refs_5_), custom_call_target="tpu_custom_call" | custom-call | flops 1638400 | bytes 1310720 | tf_op jit(solution)/shard_map/object/pallas_call | solution.py:96
  15.6 2.5 %collective-permute-start.4 = (f32[2,4,64,128]{3,2,1,0:T(8,128)S(1)}, f32[2,4,64,128]{3,2,1,0:T(8,128)S(1)}, u32[]{:S(2)}, u32[]{:S(2)}) collective-permute-start(f32[2,4,64,128]{3,2,1,0:T(8,128)S(1)} %get-tuple-element.64.refs_2_), channel_id=1, source_target_pairs={{0,1},{1,0},{2,3},{3,2},{4,5},{5,4},{6,7},{7,6},{8,9},{9,8},{10,11... | collective-permute-start | bytes 786440 | tf_op jit(solution)/shard_map/ppermute | solution.py:355
  19.4 2.4 %collective-permute-start.6 = (f32[2,4,64,128]{3,2,1,0:T(8,128)S(1)}, f32[2,4,64,128]{3,2,1,0:T(8,128)S(1)}, u32[]{:S(2)}, u32[]{:S(2)}) collective-permute-start(f32[2,4,64,128]{3,2,1,0:T(8,128)S(1)} %collective-permute-done.2.refs_4_), channel_id=1, source_target_pairs={{0,1},{1,0},{2,3},{3,2},{4,5},{5,4},{6,7},{7,6},{8,9},{9,8},{10,11... | collective-permute-start | bytes 786440 | tf_op jit(solution)/shard_map/ppermute | solution.py:355
  23.0 1.7 %y_forward.3 = (f32[16,16,128]{2,1,0:T(8,128)S(1)}, f32[16,16,128]{2,1,0:T(8,128)S(1)}, f32[16,16,128]{2,1,0:T(8,128)S(1)}, f32[16,16,128]{2,1,0:T(8,128)S(1)}, ...) custom-call(s32[3]{0:T(128)S(1)} %copy-done.11, ...), custom_call_target="tpu_custom_call" | custom-call | flops 402653184 | bytes 3407872 | tf_op jit(solution)/shard_map/y_forward/pallas_call | solution.py:96
  27.4 2.3 %collective-permute-start.24 = (f32[16,16,128]{2,1,0:T(8,128)S(1)}, f32[16,16,128]{2,1,0:T(8,128)S(1)}, u32[]{:S(2)}, u32[]{:S(2)}) collective-permute-start(f32[16,16,128]{2,1,0:T(8,128)S(1)} %get-tuple-element.87), channel_id=1, source_target_pairs={{0,8},{1,9},{2,10},{3,11},{4,12},{5,13},{6,14},{7,15},{8,0},{9,1},... | collective-permute-start | bytes 393224 | tf_op jit(solution)/shard_map/ppermute | solution.py:355
  30.7 1.7 %y_forward.2 = (f32[16,16,128]{2,1,0:T(8,128)S(1)}, f32[16,16,128]{2,1,0:T(8,128)S(1)}, f32[16,16,128]{2,1,0:T(8,128)S(1)}, f32[16,16,128]{2,1,0:T(8,128)S(1)}, ...) custom-call(s32[3]{0:T(128)S(1)} %copy-done.11, ...), custom_call_target="tpu_custom_call" | custom-call | flops 402653184 | bytes 3407872 | tf_op jit(solution)/shard_map/y_forward/pallas_call | solution.py:96
  34.0 1.5 %collective-permute-done.23.refs_4_ = f32[16,16,128]{2,1,0:T(8,128)S(1)} collective-permute-done((f32[16,16,128]{2,1,0:T(8,128)S(1)}, f32[16,16,128]{2,1,0:T(8,128)S(1)}, u32[]{:S(2)}, u32[]{:S(2)}) %collective-permute-start.23) | collective-permute-done | bytes 131104 | tf_op jit(solution)/shard_map/ppermute | solution.py:355
  37.0 2.1 %collective-permute-start.8 = (f32[16,16,128]{2,1,0:T(8,128)S(1)}, f32[16,16,128]{2,1,0:T(8,128)S(1)}, u32[]{:S(2)}, u32[]{:S(2)}) collective-permute-start(f32[16,16,128]{2,1,0:T(8,128)S(1)} %get-tuple-element.69), channel_id=1, source_target_pairs={{0,4},{1,5},{2,6},{3,7},{4,0},{5,1},{6,2},{7,3},{8,12},{9,13},{10,... | collective-permute-start | bytes 393224 | tf_op jit(solution)/shard_map/ppermute | solution.py:355
  39.1 5.6 %collective-permute-done.25.refs_6_ = f32[16,16,128]{2,1,0:T(8,128)S(1)} collective-permute-done((f32[16,16,128]{2,1,0:T(8,128)S(1)}, f32[16,16,128]{2,1,0:T(8,128)S(1)}, u32[]{:S(2)}, u32[]{:S(2)}) %collective-permute-start.25) | collective-permute-done | bytes 131104 | tf_op jit(solution)/shard_map/ppermute | solution.py:355
  44.7 4.1 %collective-permute-done.26.refs_7_ = f32[16,16,128]{2,1,0:T(8,128)S(1)} collective-permute-done((f32[16,16,128]{2,1,0:T(8,128)S(1)}, f32[16,16,128]{2,1,0:T(8,128)S(1)}, u32[]{:S(2)}, u32[]{:S(2)}) %collective-permute-start.26) | collective-permute-done | bytes 131104 | tf_op jit(solution)/shard_map/ppermute | solution.py:355
  49.8 3.0 %collective-permute-done.27.refs_8_ = f32[16,16,128]{2,1,0:T(8,128)S(1)} collective-permute-done((f32[16,16,128]{2,1,0:T(8,128)S(1)}, f32[16,16,128]{2,1,0:T(8,128)S(1)}, u32[]{:S(2)}, u32[]{:S(2)}) %collective-permute-start.27) | collective-permute-done | bytes 131104 | tf_op jit(solution)/shard_map/ppermute | solution.py:355
  52.9 1.7 %collective-permute-start.12 = (f32[16,16,128]{2,1,0:T(8,128)S(1)}, f32[16,16,128]{2,1,0:T(8,128)S(1)}, u32[]{:S(2)}, u32[]{:S(2)}) collective-permute-start(f32[16,16,128]{2,1,0:T(8,128)S(1)} %get-tuple-element.73), channel_id=1, source_target_pairs={{0,12},{1,13},{2,14},{3,15},{4,8},{5,9},{6,10},{7,11},{8,4},{9,5},... | collective-permute-start | bytes 393224 | tf_op jit(solution)/shard_map/ppermute | solution.py:355
  54.6 9.2 %middle.3 = (f32[16,16,128]{2,1,0:T(8,128)S(1)}, f32[16,16,128]{2,1,0:T(8,128)S(1)}, f32[16,16,128]{2,1,0:T(8,128)S(1)}, f32[16,16,128]{2,1,0:T(8,128)S(1)}, f32...) custom-call(s32[3]{0:T(128)S(1)} %copy-done.11, ...), custom_call_target="tpu_custom_call" | custom-call | flops 4831838208 | bytes 3145728 | tf_op jit(solution)/shard_map/middle/pallas_call | solution.py:96
  65.1 4.2 %collective-permute-start.29 = (f32[16,16,128]{2,1,0:T(8,128)S(1)}, f32[16,16,128]{2,1,0:T(8,128)S(1)}, u32[]{:S(2)}, u32[]{:S(2)}) collective-permute-start(f32[16,16,128]{2,1,0:T(8,128)S(1)} %get-tuple-element.93), channel_id=1, source_target_pairs={{0,4},{1,5},{2,6},{3,7},{4,0},{5,1},{6,2},{7,3},{8,12},{9,13},{10,... | collective-permute-start | bytes 393224 | tf_op jit(solution)/shard_map/ppermute | solution.py:355
  71.3 3.3 %collective-permute-done.13.refs_8_ = f32[16,16,128]{2,1,0:T(8,128)S(1)} collective-permute-done((f32[16,16,128]{2,1,0:T(8,128)S(1)}, f32[16,16,128]{2,1,0:T(8,128)S(1)}, u32[]{:S(2)}, u32[]{:S(2)}) %collective-permute-start.13) | collective-permute-done | bytes 131104 | tf_op jit(solution)/shard_map/ppermute | solution.py:355
  74.7 9.4 %middle.2 = (f32[16,16,128]{2,1,0:T(8,128)S(1)}, f32[16,16,128]{2,1,0:T(8,128)S(1)}, f32[16,16,128]{2,1,0:T(8,128)S(1)}, f32[16,16,128]{2,1,0:T(8,128)S(1)}, f32...) custom-call(s32[3]{0:T(128)S(1)} %copy-done.11, ...), custom_call_target="tpu_custom_call" | custom-call | flops 4831838208 | bytes 3145728 | tf_op jit(solution)/shard_map/middle/pallas_call | solution.py:96
  84.2 2.4 %collective-permute-start.33 = (f32[16,16,128]{2,1,0:T(8,128)S(1)}, f32[16,16,128]{2,1,0:T(8,128)S(1)}, u32[]{:S(2)}, u32[]{:S(2)}) collective-permute-start(f32[16,16,128]{2,1,0:T(8,128)S(1)} %get-tuple-element.97), channel_id=1, source_target_pairs={{0,12},{1,13},{2,14},{3,15},{4,8},{5,9},{6,10},{7,11},{8,4},{9,5},... | collective-permute-start | bytes 393224 | tf_op jit(solution)/shard_map/ppermute | solution.py:355
  87.8 4.1 %collective-permute-start.15 = (f32[16,16,128]{2,1,0:T(8,128)S(1)}, f32[16,16,128]{2,1,0:T(8,128)S(1)}, u32[]{:S(2)}, u32[]{:S(2)}) collective-permute-start(f32[16,16,128]{2,1,0:T(8,128)S(1)} %get-tuple-element.77), channel_id=1, source_target_pairs={{0,4},{1,5},{2,6},{3,7},{4,0},{5,1},{6,2},{7,3},{8,12},{9,13},{10,... | collective-permute-start | bytes 393224 | tf_op jit(solution)/shard_map/ppermute | solution.py:355
  93.5 2.7 %collective-permute-done.34.refs_8_ = f32[16,16,128]{2,1,0:T(8,128)S(1)} collective-permute-done((f32[16,16,128]{2,1,0:T(8,128)S(1)}, f32[16,16,128]{2,1,0:T(8,128)S(1)}, u32[]{:S(2)}, u32[]{:S(2)}) %collective-permute-start.34) | collective-permute-done | bytes 131104 | tf_op jit(solution)/shard_map/ppermute | solution.py:355
  98.4 2.0 %y_adjoint.5 = (f32[2,4,64,128]{3,2,1,0:T(8,128)S(1)}, f32[2,4,64,128]{3,2,1,0:T(8,128)S(1)}, f32[2,4,64,128]{3,2,1,0:T(8,128)S(1)}, f32[2,4,64,128]{3,2,1,0:T(8...) custom-call(s32[3]{0:T(128)S(1)} %copy-done.11, ...), custom_call_target="tpu_custom_call" | custom-call | flops 402653184 | bytes 3411968 | tf_op jit(solution)/shard_map/y_adjoint/pallas_call | solution.py:96
  100.5 6.5 %collective-permute-done.18.refs_6_ = f32[16,16,128]{2,1,0:T(8,128)S(1)} collective-permute-done((f32[16,16,128]{2,1,0:T(8,128)S(1)}, f32[16,16,128]{2,1,0:T(8,128)S(1)}, u32[]{:S(2)}, u32[]{:S(2)}) %collective-permute-start.18) | collective-permute-done | bytes 131104 | tf_op jit(solution)/shard_map/ppermute | solution.py:355
  107.0 7.8 %collective-permute-done.19.refs_7_ = f32[16,16,128]{2,1,0:T(8,128)S(1)} collective-permute-done((f32[16,16,128]{2,1,0:T(8,128)S(1)}, f32[16,16,128]{2,1,0:T(8,128)S(1)}, u32[]{:S(2)}, u32[]{:S(2)}) %collective-permute-start.19) | collective-permute-done | bytes 131104 | tf_op jit(solution)/shard_map/ppermute | solution.py:355
  114.8 5.4 %collective-permute-done.20.refs_8_ = f32[16,16,128]{2,1,0:T(8,128)S(1)} collective-permute-done((f32[16,16,128]{2,1,0:T(8,128)S(1)}, f32[16,16,128]{2,1,0:T(8,128)S(1)}, u32[]{:S(2)}, u32[]{:S(2)}) %collective-permute-start.20) | collective-permute-done | bytes 131104 | tf_op jit(solution)/shard_map/ppermute | solution.py:355
  121.2 4.9 %collective-permute-start.35 = (f32[2,4,64,128]{3,2,1,0:T(8,128)S(1)}, f32[2,4,64,128]{3,2,1,0:T(8,128)S(1)}, u32[]{:S(2)}, u32[]{:S(2)}) collective-permute-start(f32[2,4,64,128]{3,2,1,0:T(8,128)S(1)} %get-tuple-element.105), channel_id=1, source_target_pairs={{0,1},{1,0},{2,3},{3,2},{4,5},{5,4},{6,7},{7,6},{8,9},{9,8},{10,11... | collective-permute-start | bytes 786440 | tf_op jit(solution)/shard_map/ppermute | solution.py:355
  126.1 1.4 y_adjoint.7
  133.6 3.3 %collective-permute-start.38 = (f32[4,64,128]{2,1,0:T(8,128)S(1)}, f32[4,64,128]{2,1,0:T(8,128)S(1)}, u32[]{:S(2)}, u32[]{:S(2)}) collective-permute-start(f32[4,64,128]{2,1,0:T(8,128)S(1)} %get-tuple-element.109), channel_id=1, source_target_pairs={{1,2},{2,1},{3,4},{4,3},{5,6},{6,5},{7,8},{8,7},{9,10},{10,9},{11,... | collective-permute-start | bytes 393224 | tf_op jit(solution)/shard_map/ppermute | solution.py:360
  137.0 1.4 y_adjoint.8
  138.4 3.2 %collective-permute-done.38.refs_5_ = f32[4,64,128]{2,1,0:T(8,128)S(1)} collective-permute-done((f32[4,64,128]{2,1,0:T(8,128)S(1)}, f32[4,64,128]{2,1,0:T(8,128)S(1)}, u32[]{:S(2)}, u32[]{:S(2)}) %collective-permute-start.38) | collective-permute-done | bytes 131104 | tf_op jit(solution)/shard_map/ppermute | solution.py:360
  142.9 1.6 %final.2 = (f32[8,64,128]{2,1,0:T(8,128)}, f32[3,8,64,128]{3,2,1,0:T(8,128)}) custom-call(s32[3]{0:T(128)S(1)} %copy-done.11, f32[4]{0:T(128)S(1)} %pad_maximum_fusion.refs_1_, f32[4]{0:T(128)S(1)} %copy-done.13, f32[8,64,128]{2,1,0:T(8,128)S(1)} %copy-done.5, s32[8,128,128]{2,1,0:T(8,128)S(1)} %copy-done.1, f32[4,8,64,128]{3,2,1,0:T(8,128)S(1)} %laplace.1.refs_5_, ...), custom_call_target="tpu_custom_call" | custom-call | flops 1310720 | bytes 3309568 | tf_op jit(solution)/shard_map/final/pallas_call | solution.py:96
  144.5 1.5 %final.3 = (f32[8,64,128]{2,1,0:T(8,128)}, f32[3,8,64,128]{3,2,1,0:T(8,128)}) custom-call(s32[3]{0:T(128)S(1)} %copy-done.11, f32[4]{0:T(128)S(1)} %pad_maximum_fusion.refs_1_, f32[4]{0:T(128)S(1)} %copy-done.13, f32[8,64,128]{2,1,0:T(8,128)S(1)} %copy-done.5, s32[8,128,128]{2,1,0:T(8,128)S(1)} %copy-done.1, ...), custom_call_target="tpu_custom_call", output_to_operand_aliasing={{0}: (11, {}), {1}: (12, {})} | custom-call | flops 1310720 | bytes 3276800 | tf_op jit(solution)/shard_map/final/pallas_call | solution.py:96
  (114 shorter events, 35.2 us)
Async XLA Ops:
  7.2 11.7 %collective-permute-start.1 = (f32[2,4,64,128]{3,2,1,0:T(8,128)}, f32[2,4,64,128]{3,2,1,0:T(8,128)S(1)}, u32[]{:S(2)}, u32[]{:S(2)}) collective-permute-start(f32[2,4,64,128]{3,2,1,0:T(8,128)} %get-tuple-element.65.refs_5_), channel_id=1, source_target_pairs={{0,16},{16,0},{1,17},{17,1},{2,18},{18,2},{3,19},{19,3},{4,20},{20... | collective-permute-start | bytes 786440 | tf_op jit(solution)/shard_map/ppermute | solution.py:355
  9.8 9.6 %collective-permute-start.2 = (f32[2,4,64,128]{3,2,1,0:T(8,128)}, f32[2,4,64,128]{3,2,1,0:T(8,128)S(1)}, u32[]{:S(2)}, u32[]{:S(2)}) collective-permute-start(f32[2,4,64,128]{3,2,1,0:T(8,128)} %get-tuple-element.66), channel_id=1, source_target_pairs={{0,16},{16,0},{1,17},{17,1},{2,18},{18,2},{3,19},{19,3},{4,20},{20... | collective-permute-start | bytes 786440 | tf_op jit(solution)/shard_map/ppermute | solution.py:355
  26.2 9.4 %collective-permute-start.23 = (f32[16,16,128]{2,1,0:T(8,128)S(1)}, f32[16,16,128]{2,1,0:T(8,128)S(1)}, u32[]{:S(2)}, u32[]{:S(2)}) collective-permute-start(f32[16,16,128]{2,1,0:T(8,128)S(1)} %get-tuple-element.86), channel_id=1, source_target_pairs={{0,6},{1,7},{2,4},{3,5},{4,2},{5,3},{6,0},{7,1},{8,14},{9,15},{10,... | collective-permute-start | bytes 393224 | tf_op jit(solution)/shard_map/ppermute | solution.py:355
  27.4 9.6 %collective-permute-start.24 = (f32[16,16,128]{2,1,0:T(8,128)S(1)}, f32[16,16,128]{2,1,0:T(8,128)S(1)}, u32[]{:S(2)}, u32[]{:S(2)}) collective-permute-start(f32[16,16,128]{2,1,0:T(8,128)S(1)} %get-tuple-element.87), channel_id=1, source_target_pairs={{0,8},{1,9},{2,10},{3,11},{4,12},{5,13},{6,14},{7,15},{8,0},{9,1},... | collective-permute-start | bytes 393224 | tf_op jit(solution)/shard_map/ppermute | solution.py:355
  29.7 15.0 %collective-permute-start.25 = (f32[16,16,128]{2,1,0:T(8,128)S(1)}, f32[16,16,128]{2,1,0:T(8,128)S(1)}, u32[]{:S(2)}, u32[]{:S(2)}) collective-permute-start(f32[16,16,128]{2,1,0:T(8,128)S(1)} %get-tuple-element.88), channel_id=1, source_target_pairs={{0,10},{1,11},{2,8},{3,9},{4,14},{5,15},{6,12},{7,13},{8,2},{9,3},... | collective-permute-start | bytes 393224 | tf_op jit(solution)/shard_map/ppermute | solution.py:355
  32.5 16.3 %collective-permute-start.26 = (f32[16,16,128]{2,1,0:T(8,128)S(1)}, f32[16,16,128]{2,1,0:T(8,128)S(1)}, u32[]{:S(2)}, u32[]{:S(2)}) collective-permute-start(f32[16,16,128]{2,1,0:T(8,128)S(1)} %get-tuple-element.89), channel_id=1, source_target_pairs={{0,12},{1,13},{2,14},{3,15},{4,8},{5,9},{6,10},{7,11},{8,4},{9,5},... | collective-permute-start | bytes 393224 | tf_op jit(solution)/shard_map/ppermute | solution.py:355
  33.8 19.0 %collective-permute-start.27 = (f32[16,16,128]{2,1,0:T(8,128)S(1)}, f32[16,16,128]{2,1,0:T(8,128)S(1)}, u32[]{:S(2)}, u32[]{:S(2)}) collective-permute-start(f32[16,16,128]{2,1,0:T(8,128)S(1)} %get-tuple-element.90), channel_id=1, source_target_pairs={{0,14},{1,15},{2,12},{3,13},{4,10},{5,11},{6,8},{7,9},{8,6},{9,7},... | collective-permute-start | bytes 393224 | tf_op jit(solution)/shard_map/ppermute | solution.py:355
  35.5 17.4 %collective-permute-start.7 = (f32[16,16,128]{2,1,0:T(8,128)S(1)}, f32[16,16,128]{2,1,0:T(8,128)S(1)}, u32[]{:S(2)}, u32[]{:S(2)}) collective-permute-start(f32[16,16,128]{2,1,0:T(8,128)S(1)} %get-tuple-element.68), channel_id=1, source_target_pairs={{0,2},{1,3},{2,0},{3,1},{4,6},{5,7},{6,4},{7,5},{8,10},{9,11},{10,... | collective-permute-start | bytes 393224 | tf_op jit(solution)/shard_map/ppermute | solution.py:355
  37.0 17.5 %collective-permute-start.8 = (f32[16,16,128]{2,1,0:T(8,128)S(1)}, f32[16,16,128]{2,1,0:T(8,128)S(1)}, u32[]{:S(2)}, u32[]{:S(2)}) collective-permute-start(f32[16,16,128]{2,1,0:T(8,128)S(1)} %get-tuple-element.69), channel_id=1, source_target_pairs={{0,4},{1,5},{2,6},{3,7},{4,0},{5,1},{6,2},{7,3},{8,12},{9,13},{10,... | collective-permute-start | bytes 393224 | tf_op jit(solution)/shard_map/ppermute | solution.py:355
  44.7 19.0 %collective-permute-start.9 = (f32[16,16,128]{2,1,0:T(8,128)S(1)}, f32[16,16,128]{2,1,0:T(8,128)S(1)}, u32[]{:S(2)}, u32[]{:S(2)}) collective-permute-start(f32[16,16,128]{2,1,0:T(8,128)S(1)} %get-tuple-element.70), channel_id=1, source_target_pairs={{0,6},{1,7},{2,4},{3,5},{4,2},{5,3},{6,0},{7,1},{8,14},{9,15},{10,... | collective-permute-start | bytes 393224 | tf_op jit(solution)/shard_map/ppermute | solution.py:355
  48.8 16.3 %collective-permute-start.10 = (f32[16,16,128]{2,1,0:T(8,128)S(1)}, f32[16,16,128]{2,1,0:T(8,128)S(1)}, u32[]{:S(2)}, u32[]{:S(2)}) collective-permute-start(f32[16,16,128]{2,1,0:T(8,128)S(1)} %get-tuple-element.71), channel_id=1, source_target_pairs={{0,8},{1,9},{2,10},{3,11},{4,12},{5,13},{6,14},{7,15},{8,0},{9,1},... | collective-permute-start | bytes 393224 | tf_op jit(solution)/shard_map/ppermute | solution.py:355
  52.9 16.4 %collective-permute-start.11 = (f32[16,16,128]{2,1,0:T(8,128)S(1)}, f32[16,16,128]{2,1,0:T(8,128)S(1)}, u32[]{:S(2)}, u32[]{:S(2)}) collective-permute-start(f32[16,16,128]{2,1,0:T(8,128)S(1)} %get-tuple-element.72), channel_id=1, source_target_pairs={{0,10},{1,11},{2,8},{3,9},{4,14},{5,15},{6,12},{7,13},{8,2},{9,3},... | collective-permute-start | bytes 393224 | tf_op jit(solution)/shard_map/ppermute | solution.py:355
  52.9 17.9 %collective-permute-start.12 = (f32[16,16,128]{2,1,0:T(8,128)S(1)}, f32[16,16,128]{2,1,0:T(8,128)S(1)}, u32[]{:S(2)}, u32[]{:S(2)}) collective-permute-start(f32[16,16,128]{2,1,0:T(8,128)S(1)} %get-tuple-element.73), channel_id=1, source_target_pairs={{0,12},{1,13},{2,14},{3,15},{4,8},{5,9},{6,10},{7,11},{8,4},{9,5},... | collective-permute-start | bytes 393224 | tf_op jit(solution)/shard_map/ppermute | solution.py:355
  54.5 20.1 %collective-permute-start.13 = (f32[16,16,128]{2,1,0:T(8,128)S(1)}, f32[16,16,128]{2,1,0:T(8,128)S(1)}, u32[]{:S(2)}, u32[]{:S(2)}) collective-permute-start(f32[16,16,128]{2,1,0:T(8,128)S(1)} %get-tuple-element.74), channel_id=1, source_target_pairs={{0,14},{1,15},{2,12},{3,13},{4,10},{5,11},{6,8},{7,9},{8,6},{9,7},... | collective-permute-start | bytes 393224 | tf_op jit(solution)/shard_map/ppermute | solution.py:355
  63.8 20.4 %collective-permute-start.28 = (f32[16,16,128]{2,1,0:T(8,128)S(1)}, f32[16,16,128]{2,1,0:T(8,128)S(1)}, u32[]{:S(2)}, u32[]{:S(2)}) collective-permute-start(f32[16,16,128]{2,1,0:T(8,128)S(1)} %get-tuple-element.92), channel_id=1, source_target_pairs={{0,2},{1,3},{2,0},{3,1},{4,6},{5,7},{6,4},{7,5},{8,10},{9,11},{10,... | collective-permute-start | bytes 393224 | tf_op jit(solution)/shard_map/ppermute | solution.py:355
  65.1 21.5 %collective-permute-start.29 = (f32[16,16,128]{2,1,0:T(8,128)S(1)}, f32[16,16,128]{2,1,0:T(8,128)S(1)}, u32[]{:S(2)}, u32[]{:S(2)}) collective-permute-start(f32[16,16,128]{2,1,0:T(8,128)S(1)} %get-tuple-element.93), channel_id=1, source_target_pairs={{0,4},{1,5},{2,6},{3,7},{4,0},{5,1},{6,2},{7,3},{8,12},{9,13},{10,... | collective-permute-start | bytes 393224 | tf_op jit(solution)/shard_map/ppermute | solution.py:355
  69.2 17.3 %collective-permute-start.30 = (f32[16,16,128]{2,1,0:T(8,128)S(1)}, f32[16,16,128]{2,1,0:T(8,128)S(1)}, u32[]{:S(2)}, u32[]{:S(2)}) collective-permute-start(f32[16,16,128]{2,1,0:T(8,128)S(1)} %get-tuple-element.94), channel_id=1, source_target_pairs={{0,6},{1,7},{2,4},{3,5},{4,2},{5,3},{6,0},{7,1},{8,14},{9,15},{10,... | collective-permute-start | bytes 393224 | tf_op jit(solution)/shard_map/ppermute | solution.py:355
  70.8 17.1 %collective-permute-start.31 = (f32[16,16,128]{2,1,0:T(8,128)S(1)}, f32[16,16,128]{2,1,0:T(8,128)S(1)}, u32[]{:S(2)}, u32[]{:S(2)}) collective-permute-start(f32[16,16,128]{2,1,0:T(8,128)S(1)} %get-tuple-element.95), channel_id=1, source_target_pairs={{0,8},{1,9},{2,10},{3,11},{4,12},{5,13},{6,14},{7,15},{8,0},{9,1},... | collective-permute-start | bytes 393224 | tf_op jit(solution)/shard_map/ppermute | solution.py:355
  74.7 17.3 %collective-permute-start.32 = (f32[16,16,128]{2,1,0:T(8,128)S(1)}, f32[16,16,128]{2,1,0:T(8,128)S(1)}, u32[]{:S(2)}, u32[]{:S(2)}) collective-permute-start(f32[16,16,128]{2,1,0:T(8,128)S(1)} %get-tuple-element.96), channel_id=1, source_target_pairs={{0,10},{1,11},{2,8},{3,9},{4,14},{5,15},{6,12},{7,13},{8,2},{9,3},... | collective-permute-start | bytes 393224 | tf_op jit(solution)/shard_map/ppermute | solution.py:355
  84.2 9.0 %collective-permute-start.33 = (f32[16,16,128]{2,1,0:T(8,128)S(1)}, f32[16,16,128]{2,1,0:T(8,128)S(1)}, u32[]{:S(2)}, u32[]{:S(2)}) collective-permute-start(f32[16,16,128]{2,1,0:T(8,128)S(1)} %get-tuple-element.97), channel_id=1, source_target_pairs={{0,12},{1,13},{2,14},{3,15},{4,8},{5,9},{6,10},{7,11},{8,4},{9,5},... | collective-permute-start | bytes 393224 | tf_op jit(solution)/shard_map/ppermute | solution.py:355
  86.6 9.6 %collective-permute-start.34 = (f32[16,16,128]{2,1,0:T(8,128)S(1)}, f32[16,16,128]{2,1,0:T(8,128)S(1)}, u32[]{:S(2)}, u32[]{:S(2)}) collective-permute-start(f32[16,16,128]{2,1,0:T(8,128)S(1)} %get-tuple-element.98), channel_id=1, source_target_pairs={{0,14},{1,15},{2,12},{3,13},{4,10},{5,11},{6,8},{7,9},{8,6},{9,7},... | collective-permute-start | bytes 393224 | tf_op jit(solution)/shard_map/ppermute | solution.py:355
  86.6 10.8 %collective-permute-start.14 = (f32[16,16,128]{2,1,0:T(8,128)S(1)}, f32[16,16,128]{2,1,0:T(8,128)S(1)}, u32[]{:S(2)}, u32[]{:S(2)}) collective-permute-start(f32[16,16,128]{2,1,0:T(8,128)S(1)} %get-tuple-element.76), channel_id=1, source_target_pairs={{0,2},{1,3},{2,0},{3,1},{4,6},{5,7},{6,4},{7,5},{8,10},{9,11},{10,... | collective-permute-start | bytes 393224 | tf_op jit(solution)/shard_map/ppermute | solution.py:355
  87.8 9.5 %collective-permute-start.15 = (f32[16,16,128]{2,1,0:T(8,128)S(1)}, f32[16,16,128]{2,1,0:T(8,128)S(1)}, u32[]{:S(2)}, u32[]{:S(2)}) collective-permute-start(f32[16,16,128]{2,1,0:T(8,128)S(1)} %get-tuple-element.77), channel_id=1, source_target_pairs={{0,4},{1,5},{2,6},{3,7},{4,0},{5,1},{6,2},{7,3},{8,12},{9,13},{10,... | collective-permute-start | bytes 393224 | tf_op jit(solution)/shard_map/ppermute | solution.py:355
  92.0 8.5 %collective-permute-start.16 = (f32[16,16,128]{2,1,0:T(8,128)S(1)}, f32[16,16,128]{2,1,0:T(8,128)S(1)}, u32[]{:S(2)}, u32[]{:S(2)}) collective-permute-start(f32[16,16,128]{2,1,0:T(8,128)S(1)} %get-tuple-element.78), channel_id=1, source_target_pairs={{0,6},{1,7},{2,4},{3,5},{4,2},{5,3},{6,0},{7,1},{8,14},{9,15},{10,... | collective-permute-start | bytes 393224 | tf_op jit(solution)/shard_map/ppermute | solution.py:355
  96.2 10.9 %collective-permute-start.18 = (f32[16,16,128]{2,1,0:T(8,128)S(1)}, f32[16,16,128]{2,1,0:T(8,128)S(1)}, u32[]{:S(2)}, u32[]{:S(2)}) collective-permute-start(f32[16,16,128]{2,1,0:T(8,128)S(1)} %get-tuple-element.80), channel_id=1, source_target_pairs={{0,10},{1,11},{2,8},{3,9},{4,14},{5,15},{6,12},{7,13},{8,2},{9,3},... | collective-permute-start | bytes 393224 | tf_op jit(solution)/shard_map/ppermute | solution.py:355
  97.3 17.5 %collective-permute-start.19 = (f32[16,16,128]{2,1,0:T(8,128)S(1)}, f32[16,16,128]{2,1,0:T(8,128)S(1)}, u32[]{:S(2)}, u32[]{:S(2)}) collective-permute-start(f32[16,16,128]{2,1,0:T(8,128)S(1)} %get-tuple-element.81), channel_id=1, source_target_pairs={{0,12},{1,13},{2,14},{3,15},{4,8},{5,9},{6,10},{7,11},{8,4},{9,5},... | collective-permute-start | bytes 393224 | tf_op jit(solution)/shard_map/ppermute | solution.py:355
  97.4 22.8 %collective-permute-start.20 = (f32[16,16,128]{2,1,0:T(8,128)S(1)}, f32[16,16,128]{2,1,0:T(8,128)S(1)}, u32[]{:S(2)}, u32[]{:S(2)}) collective-permute-start(f32[16,16,128]{2,1,0:T(8,128)S(1)} %get-tuple-element.82), channel_id=1, source_target_pairs={{0,14},{1,15},{2,12},{3,13},{4,10},{5,11},{6,8},{7,9},{8,6},{9,7},... | collective-permute-start | bytes 393224 | tf_op jit(solution)/shard_map/ppermute | solution.py:355
  128.2 13.4 %collective-permute-start.39 = (f32[576,128]{1,0:T(8,128)S(1)}, f32[576,128]{1,0:T(8,128)S(1)}, u32[]{:S(2)}, u32[]{:S(2)}) collective-permute-start(f32[576,128]{1,0:T(8,128)S(1)} %pack.2.refs_4_.refs_12_), channel_id=1, source_target_pairs={{0,16},{16,0},{1,17},{17,1},{2,18},{18,2},{3,19},{19,3},{4,20},{20... | collective-permute-start | bytes 884744 | tf_op jit(solution)/shard_map/ppermute | solution.py:355
  131.9 11.0 %collective-permute-start.42 = (f32[2,4,64,128]{3,2,1,0:T(8,128)S(1)}, f32[2,4,64,128]{3,2,1,0:T(8,128)S(1)}, u32[]{:S(2)}, u32[]{:S(2)}) collective-permute-start(f32[2,4,64,128]{3,2,1,0:T(8,128)S(1)} %get-tuple-element.119), channel_id=1, source_target_pairs={{0,1},{1,0},{2,3},{3,2},{4,5},{5,4},{6,7},{7,6},{8,9},{9,8},{10,11... | collective-permute-start | bytes 786440 | tf_op jit(solution)/shard_map/ppermute | solution.py:355
  131.9 12.5 %collective-permute-start.40 = (f32[2,4,64,128]{3,2,1,0:T(8,128)S(1)}, f32[2,4,64,128]{3,2,1,0:T(8,128)S(1)}, u32[]{:S(2)}, u32[]{:S(2)}) collective-permute-start(f32[2,4,64,128]{3,2,1,0:T(8,128)S(1)} %get-tuple-element.115), channel_id=1, source_target_pairs={{0,1},{1,0},{2,3},{3,2},{4,5},{5,4},{6,7},{7,6},{8,9},{9,8},{10,11... | collective-permute-start | bytes 786440 | tf_op jit(solution)/shard_map/ppermute | solution.py:355
  132.4 12.1 %collective-permute-start.41 = (f32[512,128]{1,0:T(8,128)S(1)}, f32[512,128]{1,0:T(8,128)S(1)}, u32[]{:S(2)}, u32[]{:S(2)}) collective-permute-start(f32[512,128]{1,0:T(8,128)S(1)} %pack.3.refs_5_.refs_13_), channel_id=1, source_target_pairs={{0,16},{16,0},{1,17},{17,1},{2,18},{18,2},{3,19},{19,3},{4,20},{20... | collective-permute-start | bytes 786440 | tf_op jit(solution)/shard_map/ppermute | solution.py:355
  133.6 8.0 %collective-permute-start.38 = (f32[4,64,128]{2,1,0:T(8,128)S(1)}, f32[4,64,128]{2,1,0:T(8,128)S(1)}, u32[]{:S(2)}, u32[]{:S(2)}) collective-permute-start(f32[4,64,128]{2,1,0:T(8,128)S(1)} %get-tuple-element.109), channel_id=1, source_target_pairs={{1,2},{2,1},{3,4},{4,3},{5,6},{6,5},{7,8},{8,7},{9,10},{10,9},{11,... | collective-permute-start | bytes 393224 | tf_op jit(solution)/shard_map/ppermute | solution.py:360
  (30 other events, 530.2 us)

commit v4 on v3

--- a/solution.py
+++ b/solution.py
@@ -471,12 +471,15 @@
     def cross(sends):
         return [sends[0]] + [swap(sends[k], "slab", 2 * k) for k in range(1, chips)]
 
-    sends = [y_forward(at, list(range(chips))) for at in range(len(pieces))]
+    arrived, first = [], ()
+    for at in range(len(pieces)):
+        arrived.append(cross(y_forward(at, list(range(chips)), first)))
+        first = [arrived[at][chips // 2]]
     jobs = {mate: [(mate, part * portion) for part in range(splits)] for mate in (True, False)}
     everyone = list(range(refls))
     adds = None
     for at in range(len(pieces)):
-        backs = middle(at, cross(sends[at]))
+        backs = middle(at, arrived[at])
         returned = cross(backs)
         if at + 1 < len(pieces):
             adds, unused = y_adjoint(at, returned, jobs[True] + jobs[False], everyone, adds)

time: 146 us -> 143 us (0.979)
  waiting for transfers between devices: 47.4 us -> 44.9 us
    ppermute x42, waiting for transfers between devices: 44.3 us -> 40.8 us  [swap(): return lax.ppermute(x, axis, [(i, i ^ bits) for i in range(count)])]
  transfers between devices with their start and end apart: 43 -> 43, of which waited for: 14 -> 14; matrix products, arithmetic and copies ran while one was open for 0% -> 0% of each run, Pallas kernels for 24% -> 25%
where the time goes in v4:
time: 143 us
  starting transfers between devices  49 us (34%)
  waiting for transfers between devices  44.9 us (31%)
  Pallas kernels  41.5 us (29%)
  local copies, waits for them, and re-layouts  4.42 us (3%)
  between operations  1.61 us (1%)
    ppermute x42, starting transfers between devices, swap(): return lax.ppermute(x, axis, [(i, i ^ bits) for i in range(count)])  46.6 us
    pallas_call x19, Pallas kernels, call(): pl.pallas_call(run, grid=(1,), out_shape=[jax.ShapeDtypeStruct(shape, F32...  41.5 us
    ppermute x42, waiting for transfers between devices, swap(): return lax.ppermute(x, axis, [(i, i ^ bits) for i in range(count)])  40.8 us
    unnamed x38, local copies, waits for them, and re-layouts  4.42 us
    ppermute x1, waiting for transfers between devices, swap_outward(): lax.ppermute(x, axis, [pair for i in range(1, count - 1, 2) for pair in (...  4.1 us
  transfers between devices with their start and end apart: 43, of which 14 were waited for; matrix products, arithmetic and copies ran while one was open for 0% of the time, Pallas kernels for 25%

profile of v4, /device:TPU:13, one launch (start us, length us, event | category | flops | bytes accessed | tf_op | source)
XLA Modules:
  0.0 142.8 jit_solution(4204277936323069414)
XLA Ops:
  2.9 1.5 %collective-permute-done.refs_1_.refs_2_ = f32[4]{0:T(128)S(1)} collective-permute-done((f32[4]{0:T(128)S(1)}, f32[4]{0:T(128)S(1)}, u32[]{:S(2)}, u32[]{:S(2)}) %collective-permute-start) | collective-permute-done | bytes 48 | tf_op jit(solution)/shard_map/ppermute | solution.py:355
  5.1 2.2 %object.6 = (f32[2,4,64,128]{3,2,1,0:T(8,128)}, f32[2,4,64,128]{3,2,1,0:T(8,128)}) custom-call(s32[3]{0:T(128)} %pad_add_fusion.refs_0_, f32[4]{0:T(128)} %copy-done.12, f32[8,64,128]{2,1,0:T(8,128)} %refs_3_.19, f32[3,8,64,128]{3,2,1,0:T(8,128)} %refs_2_.11, s32[8,128,128]{2,1,0:T(8,128)} %refs_4_.15), custom_call_target="tpu_custom_call" | custom-call | flops 1638400 | bytes 1310720 | tf_op jit(solution)/shard_map/object/pallas_call | solution.py:96
  7.5 2.3 %object.7 = (f32[2,4,64,128]{3,2,1,0:T(8,128)}, f32[2,4,64,128]{3,2,1,0:T(8,128)}) custom-call(s32[3]{0:T(128)} %pad_add_fusion.refs_0_, f32[4]{0:T(128)} %copy-done.12, f32[8,64,128]{2,1,0:T(8,128)} %refs_3_.19, f32[3,8,64,128]{3,2,1,0:T(8,128)} %refs_2_.11, s32[8,128,128]{2,1,0:T(8,128)} %refs_4_.15, f32[2,4,64,128]{3,2,1,0:T(8,128)} %get-tuple-element.65.refs_5_), custom_call_target="tpu_custom_call" | custom-call | flops 1638400 | bytes 1310720 | tf_op jit(solution)/shard_map/object/pallas_call | solution.py:96
  15.6 2.5 %collective-permute-start.4 = (f32[2,4,64,128]{3,2,1,0:T(8,128)S(1)}, f32[2,4,64,128]{3,2,1,0:T(8,128)S(1)}, u32[]{:S(2)}, u32[]{:S(2)}) collective-permute-start(f32[2,4,64,128]{3,2,1,0:T(8,128)S(1)} %get-tuple-element.64.refs_2_), channel_id=1, source_target_pairs={{0,1},{1,0},{2,3},{3,2},{4,5},{5,4},{6,7},{7,6},{8,9},{9,8},{10,11... | collective-permute-start | bytes 786440 | tf_op jit(solution)/shard_map/ppermute | solution.py:355
  19.4 2.4 %collective-permute-start.6 = (f32[2,4,64,128]{3,2,1,0:T(8,128)S(1)}, f32[2,4,64,128]{3,2,1,0:T(8,128)S(1)}, u32[]{:S(2)}, u32[]{:S(2)}) collective-permute-start(f32[2,4,64,128]{3,2,1,0:T(8,128)S(1)} %collective-permute-done.2.refs_4_), channel_id=1, source_target_pairs={{0,1},{1,0},{2,3},{3,2},{4,5},{5,4},{6,7},{7,6},{8,9},{9,8},{10,11... | collective-permute-start | bytes 786440 | tf_op jit(solution)/shard_map/ppermute | solution.py:355
  23.0 1.7 %y_forward.2 = (f32[16,16,128]{2,1,0:T(8,128)S(1)}, f32[16,16,128]{2,1,0:T(8,128)S(1)}, f32[16,16,128]{2,1,0:T(8,128)S(1)}, f32[16,16,128]{2,1,0:T(8,128)S(1)}, ...) custom-call(s32[3]{0:T(128)S(1)} %copy-done.11, ...), custom_call_target="tpu_custom_call" | custom-call | flops 402653184 | bytes 3407872 | tf_op jit(solution)/shard_map/y_forward/pallas_call | solution.py:96
  24.7 2.4 %collective-permute-start.7 = (f32[16,16,128]{2,1,0:T(8,128)S(1)}, f32[16,16,128]{2,1,0:T(8,128)S(1)}, u32[]{:S(2)}, u32[]{:S(2)}) collective-permute-start(f32[16,16,128]{2,1,0:T(8,128)S(1)} %get-tuple-element.67), channel_id=1, source_target_pairs={{0,8},{1,9},{2,10},{3,11},{4,12},{5,13},{6,14},{7,15},{8,0},{9,1},... | collective-permute-start | bytes 393224 | tf_op jit(solution)/shard_map/ppermute | solution.py:355
  30.7 2.3 %collective-permute-done.7.refs_10_.refs_5_ = f32[16,16,128]{2,1,0:T(8,128)S(1)} collective-permute-done((f32[16,16,128]{2,1,0:T(8,128)S(1)}, f32[16,16,128]{2,1,0:T(8,128)S(1)}, u32[]{:S(2)}, u32[]{:S(2)}) %collective-permute-start.7) | collective-permute-done | bytes 131104 | tf_op jit(solution)/shard_map/ppermute | solution.py:355
  33.1 1.7 %y_forward.3 = (f32[16,16,128]{2,1,0:T(8,128)S(1)}, f32[16,16,128]{2,1,0:T(8,128)S(1)}, f32[16,16,128]{2,1,0:T(8,128)S(1)}, f32[16,16,128]{2,1,0:T(8,128)S(1)}, ...) custom-call(s32[3]{0:T(128)S(1)} %copy-done.11, ...), custom_call_target="tpu_custom_call" | custom-call | flops 402653184 | bytes 3407872 | tf_op jit(solution)/shard_map/y_forward/pallas_call | solution.py:96
  34.8 2.5 %collective-permute-start.27 = (f32[16,16,128]{2,1,0:T(8,128)S(1)}, f32[16,16,128]{2,1,0:T(8,128)S(1)}, u32[]{:S(2)}, u32[]{:S(2)}) collective-permute-start(f32[16,16,128]{2,1,0:T(8,128)S(1)} %get-tuple-element.90), channel_id=1, source_target_pairs={{0,14},{1,15},{2,12},{3,13},{4,10},{5,11},{6,8},{7,9},{8,6},{9,7},... | collective-permute-start | bytes 393224 | tf_op jit(solution)/shard_map/ppermute | solution.py:355
  37.8 2.7 %collective-permute-start.9 = (f32[16,16,128]{2,1,0:T(8,128)S(1)}, f32[16,16,128]{2,1,0:T(8,128)S(1)}, u32[]{:S(2)}, u32[]{:S(2)}) collective-permute-start(f32[16,16,128]{2,1,0:T(8,128)S(1)} %get-tuple-element.70), channel_id=1, source_target_pairs={{0,4},{1,5},{2,6},{3,7},{4,0},{5,1},{6,2},{7,3},{8,12},{9,13},{10,... | collective-permute-start | bytes 393224 | tf_op jit(solution)/shard_map/ppermute | solution.py:355
  41.4 5.7 %collective-permute-done.26.refs_7_ = f32[16,16,128]{2,1,0:T(8,128)S(1)} collective-permute-done((f32[16,16,128]{2,1,0:T(8,128)S(1)}, f32[16,16,128]{2,1,0:T(8,128)S(1)}, u32[]{:S(2)}, u32[]{:S(2)}) %collective-permute-start.26) | collective-permute-done | bytes 131104 | tf_op jit(solution)/shard_map/ppermute | solution.py:355
  47.1 4.1 %collective-permute-done.27.refs_8_ = f32[16,16,128]{2,1,0:T(8,128)S(1)} collective-permute-done((f32[16,16,128]{2,1,0:T(8,128)S(1)}, f32[16,16,128]{2,1,0:T(8,128)S(1)}, u32[]{:S(2)}, u32[]{:S(2)}) %collective-permute-start.27) | collective-permute-done | bytes 131104 | tf_op jit(solution)/shard_map/ppermute | solution.py:355
  51.2 2.3 %collective-permute-start.13 = (f32[16,16,128]{2,1,0:T(8,128)S(1)}, f32[16,16,128]{2,1,0:T(8,128)S(1)}, u32[]{:S(2)}, u32[]{:S(2)}) collective-permute-start(f32[16,16,128]{2,1,0:T(8,128)S(1)} %get-tuple-element.74), channel_id=1, source_target_pairs={{0,12},{1,13},{2,14},{3,15},{4,8},{5,9},{6,10},{7,11},{8,4},{9,5},... | collective-permute-start | bytes 393224 | tf_op jit(solution)/shard_map/ppermute | solution.py:355
  53.5 9.2 %middle.3 = (f32[16,16,128]{2,1,0:T(8,128)S(1)}, f32[16,16,128]{2,1,0:T(8,128)S(1)}, f32[16,16,128]{2,1,0:T(8,128)S(1)}, f32[16,16,128]{2,1,0:T(8,128)S(1)}, f32...) custom-call(s32[3]{0:T(128)S(1)} %copy-done.11, ...), custom_call_target="tpu_custom_call" | custom-call | flops 4831838208 | bytes 3145728 | tf_op jit(solution)/shard_map/middle/pallas_call | solution.py:96
  64.0 4.2 %collective-permute-start.29 = (f32[16,16,128]{2,1,0:T(8,128)S(1)}, f32[16,16,128]{2,1,0:T(8,128)S(1)}, u32[]{:S(2)}, u32[]{:S(2)}) collective-permute-start(f32[16,16,128]{2,1,0:T(8,128)S(1)} %get-tuple-element.93), channel_id=1, source_target_pairs={{0,4},{1,5},{2,6},{3,7},{4,0},{5,1},{6,2},{7,3},{8,12},{9,13},{10,... | collective-permute-start | bytes 393224 | tf_op jit(solution)/shard_map/ppermute | solution.py:355
  68.2 1.4 %collective-permute-start.30 = (f32[16,16,128]{2,1,0:T(8,128)S(1)}, f32[16,16,128]{2,1,0:T(8,128)S(1)}, u32[]{:S(2)}, u32[]{:S(2)}) collective-permute-start(f32[16,16,128]{2,1,0:T(8,128)S(1)} %get-tuple-element.94), channel_id=1, source_target_pairs={{0,6},{1,7},{2,4},{3,5},{4,2},{5,3},{6,0},{7,1},{8,14},{9,15},{10,... | collective-permute-start | bytes 393224 | tf_op jit(solution)/shard_map/ppermute | solution.py:355
  70.9 3.7 %collective-permute-done.14.refs_8_ = f32[16,16,128]{2,1,0:T(8,128)S(1)} collective-permute-done((f32[16,16,128]{2,1,0:T(8,128)S(1)}, f32[16,16,128]{2,1,0:T(8,128)S(1)}, u32[]{:S(2)}, u32[]{:S(2)}) %collective-permute-start.14) | collective-permute-done | bytes 131104 | tf_op jit(solution)/shard_map/ppermute | solution.py:355
  74.6 9.4 %middle.2 = (f32[16,16,128]{2,1,0:T(8,128)S(1)}, f32[16,16,128]{2,1,0:T(8,128)S(1)}, f32[16,16,128]{2,1,0:T(8,128)S(1)}, f32[16,16,128]{2,1,0:T(8,128)S(1)}, f32...) custom-call(s32[3]{0:T(128)S(1)} %copy-done.11, ...), custom_call_target="tpu_custom_call" | custom-call | flops 4831838208 | bytes 3145728 | tf_op jit(solution)/shard_map/middle/pallas_call | solution.py:96
  86.8 4.0 %collective-permute-start.16 = (f32[16,16,128]{2,1,0:T(8,128)S(1)}, f32[16,16,128]{2,1,0:T(8,128)S(1)}, u32[]{:S(2)}, u32[]{:S(2)}) collective-permute-start(f32[16,16,128]{2,1,0:T(8,128)S(1)} %get-tuple-element.78), channel_id=1, source_target_pairs={{0,4},{1,5},{2,6},{3,7},{4,0},{5,1},{6,2},{7,3},{8,12},{9,13},{10,... | collective-permute-start | bytes 393224 | tf_op jit(solution)/shard_map/ppermute | solution.py:355
  93.4 2.9 %collective-permute-done.34.refs_8_ = f32[16,16,128]{2,1,0:T(8,128)S(1)} collective-permute-done((f32[16,16,128]{2,1,0:T(8,128)S(1)}, f32[16,16,128]{2,1,0:T(8,128)S(1)}, u32[]{:S(2)}, u32[]{:S(2)}) %collective-permute-start.34) | collective-permute-done | bytes 131104 | tf_op jit(solution)/shard_map/ppermute | solution.py:355
  96.6 2.6 %collective-permute-start.21 = (f32[16,16,128]{2,1,0:T(8,128)S(1)}, f32[16,16,128]{2,1,0:T(8,128)S(1)}, u32[]{:S(2)}, u32[]{:S(2)}) collective-permute-start(f32[16,16,128]{2,1,0:T(8,128)S(1)} %get-tuple-element.83), channel_id=1, source_target_pairs={{0,14},{1,15},{2,12},{3,13},{4,10},{5,11},{6,8},{7,9},{8,6},{9,7},... | collective-permute-start | bytes 393224 | tf_op jit(solution)/shard_map/ppermute | solution.py:355
  99.2 2.0 %y_adjoint.5 = (f32[2,4,64,128]{3,2,1,0:T(8,128)S(1)}, f32[2,4,64,128]{3,2,1,0:T(8,128)S(1)}, f32[2,4,64,128]{3,2,1,0:T(8,128)S(1)}, f32[2,4,64,128]{3,2,1,0:T(8...) custom-call(s32[3]{0:T(128)S(1)} %copy-done.11, ...), custom_call_target="tpu_custom_call" | custom-call | flops 402653184 | bytes 3411968 | tf_op jit(solution)/shard_map/y_adjoint/pallas_call | solution.py:96
  102.2 10.7 %collective-permute-done.19.refs_6_ = f32[16,16,128]{2,1,0:T(8,128)S(1)} collective-permute-done((f32[16,16,128]{2,1,0:T(8,128)S(1)}, f32[16,16,128]{2,1,0:T(8,128)S(1)}, u32[]{:S(2)}, u32[]{:S(2)}) %collective-permute-start.19) | collective-permute-done | bytes 131104 | tf_op jit(solution)/shard_map/ppermute | solution.py:355
  112.9 2.8 %collective-permute-done.20.refs_7_ = f32[16,16,128]{2,1,0:T(8,128)S(1)} collective-permute-done((f32[16,16,128]{2,1,0:T(8,128)S(1)}, f32[16,16,128]{2,1,0:T(8,128)S(1)}, u32[]{:S(2)}, u32[]{:S(2)}) %collective-permute-start.20) | collective-permute-done | bytes 131104 | tf_op jit(solution)/shard_map/ppermute | solution.py:355
  115.7 3.9 %collective-permute-done.21.refs_8_ = f32[16,16,128]{2,1,0:T(8,128)S(1)} collective-permute-done((f32[16,16,128]{2,1,0:T(8,128)S(1)}, f32[16,16,128]{2,1,0:T(8,128)S(1)}, u32[]{:S(2)}, u32[]{:S(2)}) %collective-permute-start.21) | collective-permute-done | bytes 131104 | tf_op jit(solution)/shard_map/ppermute | solution.py:355
  120.5 2.3 %collective-permute-start.35 = (f32[2,4,64,128]{3,2,1,0:T(8,128)S(1)}, f32[2,4,64,128]{3,2,1,0:T(8,128)S(1)}, u32[]{:S(2)}, u32[]{:S(2)}) collective-permute-start(f32[2,4,64,128]{3,2,1,0:T(8,128)S(1)} %get-tuple-element.105), channel_id=1, source_target_pairs={{0,1},{1,0},{2,3},{3,2},{4,5},{5,4},{6,7},{7,6},{8,9},{9,8},{10,11... | collective-permute-start | bytes 786440 | tf_op jit(solution)/shard_map/ppermute | solution.py:355
  130.5 2.4 %collective-permute-start.38 = (f32[4,64,128]{2,1,0:T(8,128)S(1)}, f32[4,64,128]{2,1,0:T(8,128)S(1)}, u32[]{:S(2)}, u32[]{:S(2)}) collective-permute-start(f32[4,64,128]{2,1,0:T(8,128)S(1)} %get-tuple-element.109), channel_id=1, source_target_pairs={{1,2},{2,1},{3,4},{4,3},{5,6},{6,5},{7,8},{8,7},{9,10},{10,9},{11,... | collective-permute-start | bytes 393224 | tf_op jit(solution)/shard_map/ppermute | solution.py:360
  132.9 1.4 %y_adjoint.8 = (f32[2,4,64,128]{3,2,1,0:T(8,128)S(1)}, f32[2,4,64,128]{3,2,1,0:T(8,128)S(1)}, f32[8,128]{1,0:T(8,128)}) custom-call(s32[3]{0:T(128)S(1)} %copy-done.11, f32[16,16,128]{2,1,0:T(8,128)S(1)} %get-tuple-element.76.refs_1_, f32[16,16,128]{2,1,0:T(8,128)S(1)} %collective-permute-done.15.refs_2_, ...), custom_call_target="tpu_custom_call" | custom-call | flops 100663296 | bytes 2363392 | tf_op jit(solution)/shard_map/y_adjoint/pallas_call | solution.py:96
  134.3 4.1 %collective-permute-done.38.refs_5_ = f32[4,64,128]{2,1,0:T(8,128)S(1)} collective-permute-done((f32[4,64,128]{2,1,0:T(8,128)S(1)}, f32[4,64,128]{2,1,0:T(8,128)S(1)}, u32[]{:S(2)}, u32[]{:S(2)}) %collective-permute-start.38) | collective-permute-done | bytes 131104 | tf_op jit(solution)/shard_map/ppermute | solution.py:360
  139.7 1.6 %final.2 = (f32[8,64,128]{2,1,0:T(8,128)}, f32[3,8,64,128]{3,2,1,0:T(8,128)}) custom-call(s32[3]{0:T(128)S(1)} %copy-done.11, f32[4]{0:T(128)S(1)} %pad_maximum_fusion.refs_1_, f32[4]{0:T(128)S(1)} %copy-done.13, f32[8,64,128]{2,1,0:T(8,128)S(1)} %copy-done.5, s32[8,128,128]{2,1,0:T(8,128)S(1)} %copy-done.1, f32[4,8,64,128]{3,2,1,0:T(8,128)S(1)} %laplace.1.refs_5_, ...), custom_call_target="tpu_custom_call" | custom-call | flops 1310720 | bytes 3309568 | tf_op jit(solution)/shard_map/final/pallas_call | solution.py:96
  141.3 1.5 %final.3 = (f32[8,64,128]{2,1,0:T(8,128)}, f32[3,8,64,128]{3,2,1,0:T(8,128)}) custom-call(s32[3]{0:T(128)S(1)} %copy-done.11, f32[4]{0:T(128)S(1)} %pad_maximum_fusion.refs_1_, f32[4]{0:T(128)S(1)} %copy-done.13, f32[8,64,128]{2,1,0:T(8,128)S(1)} %copy-done.5, s32[8,128,128]{2,1,0:T(8,128)S(1)} %copy-done.1, ...), custom_call_target="tpu_custom_call", output_to_operand_aliasing={{0}: (11, {}), {1}: (12, {})} | custom-call | flops 1310720 | bytes 3276800 | tf_op jit(solution)/shard_map/final/pallas_call | solution.py:96
  (114 shorter events, 34.7 us)
Async XLA Ops:
  7.2 11.7 %collective-permute-start.1 = (f32[2,4,64,128]{3,2,1,0:T(8,128)}, f32[2,4,64,128]{3,2,1,0:T(8,128)S(1)}, u32[]{:S(2)}, u32[]{:S(2)}) collective-permute-start(f32[2,4,64,128]{3,2,1,0:T(8,128)} %get-tuple-element.65.refs_5_), channel_id=1, source_target_pairs={{0,16},{16,0},{1,17},{17,1},{2,18},{18,2},{3,19},{19,3},{4,20},{20... | collective-permute-start | bytes 786440 | tf_op jit(solution)/shard_map/ppermute | solution.py:355
  9.8 9.6 %collective-permute-start.2 = (f32[2,4,64,128]{3,2,1,0:T(8,128)}, f32[2,4,64,128]{3,2,1,0:T(8,128)S(1)}, u32[]{:S(2)}, u32[]{:S(2)}) collective-permute-start(f32[2,4,64,128]{3,2,1,0:T(8,128)} %get-tuple-element.66), channel_id=1, source_target_pairs={{0,16},{16,0},{1,17},{17,1},{2,18},{18,2},{3,19},{19,3},{4,20},{20... | collective-permute-start | bytes 786440 | tf_op jit(solution)/shard_map/ppermute | solution.py:355
  24.7 8.4 %collective-permute-start.7 = (f32[16,16,128]{2,1,0:T(8,128)S(1)}, f32[16,16,128]{2,1,0:T(8,128)S(1)}, u32[]{:S(2)}, u32[]{:S(2)}) collective-permute-start(f32[16,16,128]{2,1,0:T(8,128)S(1)} %get-tuple-element.67), channel_id=1, source_target_pairs={{0,8},{1,9},{2,10},{3,11},{4,12},{5,13},{6,14},{7,15},{8,0},{9,1},... | collective-permute-start | bytes 393224 | tf_op jit(solution)/shard_map/ppermute | solution.py:355
  28.3 9.0 %collective-permute-start.23 = (f32[16,16,128]{2,1,0:T(8,128)S(1)}, f32[16,16,128]{2,1,0:T(8,128)S(1)}, u32[]{:S(2)}, u32[]{:S(2)}) collective-permute-start(f32[16,16,128]{2,1,0:T(8,128)S(1)} %get-tuple-element.86), channel_id=1, source_target_pairs={{0,4},{1,5},{2,6},{3,7},{4,0},{5,1},{6,2},{7,3},{8,12},{9,13},{10,... | collective-permute-start | bytes 393224 | tf_op jit(solution)/shard_map/ppermute | solution.py:355
  28.5 9.3 %collective-permute-start.24 = (f32[16,16,128]{2,1,0:T(8,128)S(1)}, f32[16,16,128]{2,1,0:T(8,128)S(1)}, u32[]{:S(2)}, u32[]{:S(2)}) collective-permute-start(f32[16,16,128]{2,1,0:T(8,128)S(1)} %get-tuple-element.87), channel_id=1, source_target_pairs={{0,6},{1,7},{2,4},{3,5},{4,2},{5,3},{6,0},{7,1},{8,14},{9,15},{10,... | collective-permute-start | bytes 393224 | tf_op jit(solution)/shard_map/ppermute | solution.py:355
  29.7 10.7 %collective-permute-start.25 = (f32[16,16,128]{2,1,0:T(8,128)S(1)}, f32[16,16,128]{2,1,0:T(8,128)S(1)}, u32[]{:S(2)}, u32[]{:S(2)}) collective-permute-start(f32[16,16,128]{2,1,0:T(8,128)S(1)} %get-tuple-element.88), channel_id=1, source_target_pairs={{0,10},{1,11},{2,8},{3,9},{4,14},{5,15},{6,12},{7,13},{8,2},{9,3},... | collective-permute-start | bytes 393224 | tf_op jit(solution)/shard_map/ppermute | solution.py:355
  33.1 14.0 %collective-permute-start.26 = (f32[16,16,128]{2,1,0:T(8,128)S(1)}, f32[16,16,128]{2,1,0:T(8,128)S(1)}, u32[]{:S(2)}, u32[]{:S(2)}) collective-permute-start(f32[16,16,128]{2,1,0:T(8,128)S(1)} %get-tuple-element.89), channel_id=1, source_target_pairs={{0,12},{1,13},{2,14},{3,15},{4,8},{5,9},{6,10},{7,11},{8,4},{9,5},... | collective-permute-start | bytes 393224 | tf_op jit(solution)/shard_map/ppermute | solution.py:355
  34.8 16.3 %collective-permute-start.27 = (f32[16,16,128]{2,1,0:T(8,128)S(1)}, f32[16,16,128]{2,1,0:T(8,128)S(1)}, u32[]{:S(2)}, u32[]{:S(2)}) collective-permute-start(f32[16,16,128]{2,1,0:T(8,128)S(1)} %get-tuple-element.90), channel_id=1, source_target_pairs={{0,14},{1,15},{2,12},{3,13},{4,10},{5,11},{6,8},{7,9},{8,6},{9,7},... | collective-permute-start | bytes 393224 | tf_op jit(solution)/shard_map/ppermute | solution.py:355
  37.3 13.9 %collective-permute-start.8 = (f32[16,16,128]{2,1,0:T(8,128)S(1)}, f32[16,16,128]{2,1,0:T(8,128)S(1)}, u32[]{:S(2)}, u32[]{:S(2)}) collective-permute-start(f32[16,16,128]{2,1,0:T(8,128)S(1)} %get-tuple-element.69), channel_id=1, source_target_pairs={{0,2},{1,3},{2,0},{3,1},{4,6},{5,7},{6,4},{7,5},{8,10},{9,11},{10,... | collective-permute-start | bytes 393224 | tf_op jit(solution)/shard_map/ppermute | solution.py:355
  37.8 15.7 %collective-permute-start.9 = (f32[16,16,128]{2,1,0:T(8,128)S(1)}, f32[16,16,128]{2,1,0:T(8,128)S(1)}, u32[]{:S(2)}, u32[]{:S(2)}) collective-permute-start(f32[16,16,128]{2,1,0:T(8,128)S(1)} %get-tuple-element.70), channel_id=1, source_target_pairs={{0,4},{1,5},{2,6},{3,7},{4,0},{5,1},{6,2},{7,3},{8,12},{9,13},{10,... | collective-permute-start | bytes 393224 | tf_op jit(solution)/shard_map/ppermute | solution.py:355
  40.5 22.2 %collective-permute-start.10 = (f32[16,16,128]{2,1,0:T(8,128)S(1)}, f32[16,16,128]{2,1,0:T(8,128)S(1)}, u32[]{:S(2)}, u32[]{:S(2)}) collective-permute-start(f32[16,16,128]{2,1,0:T(8,128)S(1)} %get-tuple-element.71), channel_id=1, source_target_pairs={{0,6},{1,7},{2,4},{3,5},{4,2},{5,3},{6,0},{7,1},{8,14},{9,15},{10,... | collective-permute-start | bytes 393224 | tf_op jit(solution)/shard_map/ppermute | solution.py:355
  47.1 16.9 %collective-permute-start.11 = (f32[16,16,128]{2,1,0:T(8,128)S(1)}, f32[16,16,128]{2,1,0:T(8,128)S(1)}, u32[]{:S(2)}, u32[]{:S(2)}) collective-permute-start(f32[16,16,128]{2,1,0:T(8,128)S(1)} %get-tuple-element.72), channel_id=1, source_target_pairs={{0,8},{1,9},{2,10},{3,11},{4,12},{5,13},{6,14},{7,15},{8,0},{9,1},... | collective-permute-start | bytes 393224 | tf_op jit(solution)/shard_map/ppermute | solution.py:355
  51.2 17.0 %collective-permute-start.12 = (f32[16,16,128]{2,1,0:T(8,128)S(1)}, f32[16,16,128]{2,1,0:T(8,128)S(1)}, u32[]{:S(2)}, u32[]{:S(2)}) collective-permute-start(f32[16,16,128]{2,1,0:T(8,128)S(1)} %get-tuple-element.73), channel_id=1, source_target_pairs={{0,10},{1,11},{2,8},{3,9},{4,14},{5,15},{6,12},{7,13},{8,2},{9,3},... | collective-permute-start | bytes 393224 | tf_op jit(solution)/shard_map/ppermute | solution.py:355
  51.2 19.1 %collective-permute-start.13 = (f32[16,16,128]{2,1,0:T(8,128)S(1)}, f32[16,16,128]{2,1,0:T(8,128)S(1)}, u32[]{:S(2)}, u32[]{:S(2)}) collective-permute-start(f32[16,16,128]{2,1,0:T(8,128)S(1)} %get-tuple-element.74), channel_id=1, source_target_pairs={{0,12},{1,13},{2,14},{3,15},{4,8},{5,9},{6,10},{7,11},{8,4},{9,5},... | collective-permute-start | bytes 393224 | tf_op jit(solution)/shard_map/ppermute | solution.py:355
  53.5 21.2 %collective-permute-start.14 = (f32[16,16,128]{2,1,0:T(8,128)S(1)}, f32[16,16,128]{2,1,0:T(8,128)S(1)}, u32[]{:S(2)}, u32[]{:S(2)}) collective-permute-start(f32[16,16,128]{2,1,0:T(8,128)S(1)} %get-tuple-element.75), channel_id=1, source_target_pairs={{0,14},{1,15},{2,12},{3,13},{4,10},{5,11},{6,8},{7,9},{8,6},{9,7},... | collective-permute-start | bytes 393224 | tf_op jit(solution)/shard_map/ppermute | solution.py:355
  62.7 21.4 %collective-permute-start.28 = (f32[16,16,128]{2,1,0:T(8,128)S(1)}, f32[16,16,128]{2,1,0:T(8,128)S(1)}, u32[]{:S(2)}, u32[]{:S(2)}) collective-permute-start(f32[16,16,128]{2,1,0:T(8,128)S(1)} %get-tuple-element.92), channel_id=1, source_target_pairs={{0,2},{1,3},{2,0},{3,1},{4,6},{5,7},{6,4},{7,5},{8,10},{9,11},{10,... | collective-permute-start | bytes 393224 | tf_op jit(solution)/shard_map/ppermute | solution.py:355
  64.0 21.5 %collective-permute-start.29 = (f32[16,16,128]{2,1,0:T(8,128)S(1)}, f32[16,16,128]{2,1,0:T(8,128)S(1)}, u32[]{:S(2)}, u32[]{:S(2)}) collective-permute-start(f32[16,16,128]{2,1,0:T(8,128)S(1)} %get-tuple-element.93), channel_id=1, source_target_pairs={{0,4},{1,5},{2,6},{3,7},{4,0},{5,1},{6,2},{7,3},{8,12},{9,13},{10,... | collective-permute-start | bytes 393224 | tf_op jit(solution)/shard_map/ppermute | solution.py:355
  68.2 17.3 %collective-permute-start.30 = (f32[16,16,128]{2,1,0:T(8,128)S(1)}, f32[16,16,128]{2,1,0:T(8,128)S(1)}, u32[]{:S(2)}, u32[]{:S(2)}) collective-permute-start(f32[16,16,128]{2,1,0:T(8,128)S(1)} %get-tuple-element.94), channel_id=1, source_target_pairs={{0,6},{1,7},{2,4},{3,5},{4,2},{5,3},{6,0},{7,1},{8,14},{9,15},{10,... | collective-permute-start | bytes 393224 | tf_op jit(solution)/shard_map/ppermute | solution.py:355
  70.3 16.5 %collective-permute-start.31 = (f32[16,16,128]{2,1,0:T(8,128)S(1)}, f32[16,16,128]{2,1,0:T(8,128)S(1)}, u32[]{:S(2)}, u32[]{:S(2)}) collective-permute-start(f32[16,16,128]{2,1,0:T(8,128)S(1)} %get-tuple-element.95), channel_id=1, source_target_pairs={{0,8},{1,9},{2,10},{3,11},{4,12},{5,13},{6,14},{7,15},{8,0},{9,1},... | collective-permute-start | bytes 393224 | tf_op jit(solution)/shard_map/ppermute | solution.py:355
  74.6 16.3 %collective-permute-start.32 = (f32[16,16,128]{2,1,0:T(8,128)S(1)}, f32[16,16,128]{2,1,0:T(8,128)S(1)}, u32[]{:S(2)}, u32[]{:S(2)}) collective-permute-start(f32[16,16,128]{2,1,0:T(8,128)S(1)} %get-tuple-element.96), channel_id=1, source_target_pairs={{0,10},{1,11},{2,8},{3,9},{4,14},{5,15},{6,12},{7,13},{8,2},{9,3},... | collective-permute-start | bytes 393224 | tf_op jit(solution)/shard_map/ppermute | solution.py:355
  85.5 10.8 %collective-permute-start.34 = (f32[16,16,128]{2,1,0:T(8,128)S(1)}, f32[16,16,128]{2,1,0:T(8,128)S(1)}, u32[]{:S(2)}, u32[]{:S(2)}) collective-permute-start(f32[16,16,128]{2,1,0:T(8,128)S(1)} %get-tuple-element.98), channel_id=1, source_target_pairs={{0,14},{1,15},{2,12},{3,13},{4,10},{5,11},{6,8},{7,9},{8,6},{9,7},... | collective-permute-start | bytes 393224 | tf_op jit(solution)/shard_map/ppermute | solution.py:355
  85.5 11.1 %collective-permute-start.15 = (f32[16,16,128]{2,1,0:T(8,128)S(1)}, f32[16,16,128]{2,1,0:T(8,128)S(1)}, u32[]{:S(2)}, u32[]{:S(2)}) collective-permute-start(f32[16,16,128]{2,1,0:T(8,128)S(1)} %get-tuple-element.77), channel_id=1, source_target_pairs={{0,2},{1,3},{2,0},{3,1},{4,6},{5,7},{6,4},{7,5},{8,10},{9,11},{10,... | collective-permute-start | bytes 393224 | tf_op jit(solution)/shard_map/ppermute | solution.py:355
  86.8 9.8 %collective-permute-start.16 = (f32[16,16,128]{2,1,0:T(8,128)S(1)}, f32[16,16,128]{2,1,0:T(8,128)S(1)}, u32[]{:S(2)}, u32[]{:S(2)}) collective-permute-start(f32[16,16,128]{2,1,0:T(8,128)S(1)} %get-tuple-element.78), channel_id=1, source_target_pairs={{0,4},{1,5},{2,6},{3,7},{4,0},{5,1},{6,2},{7,3},{8,12},{9,13},{10,... | collective-permute-start | bytes 393224 | tf_op jit(solution)/shard_map/ppermute | solution.py:355
  90.9 11.3 %collective-permute-start.17 = (f32[16,16,128]{2,1,0:T(8,128)S(1)}, f32[16,16,128]{2,1,0:T(8,128)S(1)}, u32[]{:S(2)}, u32[]{:S(2)}) collective-permute-start(f32[16,16,128]{2,1,0:T(8,128)S(1)} %get-tuple-element.79), channel_id=1, source_target_pairs={{0,6},{1,7},{2,4},{3,5},{4,2},{5,3},{6,0},{7,1},{8,14},{9,15},{10,... | collective-permute-start | bytes 393224 | tf_op jit(solution)/shard_map/ppermute | solution.py:355
  92.1 10.1 %collective-permute-start.18 = (f32[16,16,128]{2,1,0:T(8,128)S(1)}, f32[16,16,128]{2,1,0:T(8,128)S(1)}, u32[]{:S(2)}, u32[]{:S(2)}) collective-permute-start(f32[16,16,128]{2,1,0:T(8,128)S(1)} %get-tuple-element.80), channel_id=1, source_target_pairs={{0,8},{1,9},{2,10},{3,11},{4,12},{5,13},{6,14},{7,15},{8,0},{9,1},... | collective-permute-start | bytes 393224 | tf_op jit(solution)/shard_map/ppermute | solution.py:355
  96.3 16.6 %collective-permute-start.19 = (f32[16,16,128]{2,1,0:T(8,128)S(1)}, f32[16,16,128]{2,1,0:T(8,128)S(1)}, u32[]{:S(2)}, u32[]{:S(2)}) collective-permute-start(f32[16,16,128]{2,1,0:T(8,128)S(1)} %get-tuple-element.81), channel_id=1, source_target_pairs={{0,10},{1,11},{2,8},{3,9},{4,14},{5,15},{6,12},{7,13},{8,2},{9,3},... | collective-permute-start | bytes 393224 | tf_op jit(solution)/shard_map/ppermute | solution.py:355
  96.6 19.1 %collective-permute-start.20 = (f32[16,16,128]{2,1,0:T(8,128)S(1)}, f32[16,16,128]{2,1,0:T(8,128)S(1)}, u32[]{:S(2)}, u32[]{:S(2)}) collective-permute-start(f32[16,16,128]{2,1,0:T(8,128)S(1)} %get-tuple-element.82), channel_id=1, source_target_pairs={{0,12},{1,13},{2,14},{3,15},{4,8},{5,9},{6,10},{7,11},{8,4},{9,5},... | collective-permute-start | bytes 393224 | tf_op jit(solution)/shard_map/ppermute | solution.py:355
  96.6 22.9 %collective-permute-start.21 = (f32[16,16,128]{2,1,0:T(8,128)S(1)}, f32[16,16,128]{2,1,0:T(8,128)S(1)}, u32[]{:S(2)}, u32[]{:S(2)}) collective-permute-start(f32[16,16,128]{2,1,0:T(8,128)S(1)} %get-tuple-element.83), channel_id=1, source_target_pairs={{0,14},{1,15},{2,12},{3,13},{4,10},{5,11},{6,8},{7,9},{8,6},{9,7},... | collective-permute-start | bytes 393224 | tf_op jit(solution)/shard_map/ppermute | solution.py:355
  125.0 13.4 %collective-permute-start.39 = (f32[576,128]{1,0:T(8,128)S(1)}, f32[576,128]{1,0:T(8,128)S(1)}, u32[]{:S(2)}, u32[]{:S(2)}) collective-permute-start(f32[576,128]{1,0:T(8,128)S(1)} %pack.2.refs_4_.refs_12_), channel_id=1, source_target_pairs={{0,16},{16,0},{1,17},{17,1},{2,18},{18,2},{3,19},{19,3},{4,20},{20... | collective-permute-start | bytes 884744 | tf_op jit(solution)/shard_map/ppermute | solution.py:355
  128.8 10.9 %collective-permute-start.42 = (f32[2,4,64,128]{3,2,1,0:T(8,128)S(1)}, f32[2,4,64,128]{3,2,1,0:T(8,128)S(1)}, u32[]{:S(2)}, u32[]{:S(2)}) collective-permute-start(f32[2,4,64,128]{3,2,1,0:T(8,128)S(1)} %get-tuple-element.119), channel_id=1, source_target_pairs={{0,1},{1,0},{2,3},{3,2},{4,5},{5,4},{6,7},{7,6},{8,9},{9,8},{10,11... | collective-permute-start | bytes 786440 | tf_op jit(solution)/shard_map/ppermute | solution.py:355
  128.8 12.5 %collective-permute-start.40 = (f32[2,4,64,128]{3,2,1,0:T(8,128)S(1)}, f32[2,4,64,128]{3,2,1,0:T(8,128)S(1)}, u32[]{:S(2)}, u32[]{:S(2)}) collective-permute-start(f32[2,4,64,128]{3,2,1,0:T(8,128)S(1)} %get-tuple-element.115), channel_id=1, source_target_pairs={{0,1},{1,0},{2,3},{3,2},{4,5},{5,4},{6,7},{7,6},{8,9},{9,8},{10,11... | collective-permute-start | bytes 786440 | tf_op jit(solution)/shard_map/ppermute | solution.py:355
  129.3 12.0 %collective-permute-start.41 = (f32[512,128]{1,0:T(8,128)S(1)}, f32[512,128]{1,0:T(8,128)S(1)}, u32[]{:S(2)}, u32[]{:S(2)}) collective-permute-start(f32[512,128]{1,0:T(8,128)S(1)} %pack.3.refs_5_.refs_13_), channel_id=1, source_target_pairs={{0,16},{16,0},{1,17},{17,1},{2,18},{18,2},{3,19},{19,3},{4,20},{20... | collective-permute-start | bytes 786440 | tf_op jit(solution)/shard_map/ppermute | solution.py:355
  (30 other events, 518.1 us)

commit v5 on v4

--- a/solution.py
+++ b/solution.py
@@ -474,7 +474,7 @@
     arrived, first = [], ()
     for at in range(len(pieces)):
         arrived.append(cross(y_forward(at, list(range(chips)), first)))
-        first = [arrived[at][chips // 2]]
+        first = [arrived[at][chips // 2 + 1]]
     jobs = {mate: [(mate, part * portion) for part in range(splits)] for mate in (True, False)}
     everyone = list(range(refls))
     adds = None
@@ -502,11 +502,10 @@
             )
             sums.append(total)
             others[k - 1].append(swap(total, "refl", k))
-    for_mate, unused = y_adjoint(at, returned, jobs[True], everyone[:1], adds, sums)
-    mine, unused = y_adjoint(at, returned, jobs[False], everyone[:1], adds, sums)
-    mates = [swap(for_mate[job][0], "slab", 1) for job in jobs[True]]
-    own = [mine[job][0] for job in jobs[False]]
-    edges = call(edges_kernel, [(4, rows, depth)] * 2, [place], fields, [], cells, "edges", first=sums)
+    kept, unused = y_adjoint(at, returned, jobs[True] + jobs[False], everyone[:1], adds, sums)
+    mates = [swap(kept[job][0], "slab", 1) for job in jobs[True]]
+    own = [kept[job][0] for job in jobs[False]]
+    edges = call(edges_kernel, [(4, rows, depth)] * 2, [place], fields, [], cells, "edges", first=sums[:1])
     halos = (swap(edges[0], "slab", 1), swap_outward(edges[1], "slab"), *[one[0] for one in others])
     (lapped,) = call(
         functools.partial(laplace_kernel, refls),

time: 143 us -> 143 us (level)
  waiting for transfers between devices: 44.9 us -> 46.5 us
    pallas_call x19 -> x18, Pallas kernels: 41.5 us -> 40.4 us  [call(): pl.pallas_call(run, grid=(1,), out_shape=[jax.ShapeDtypeStruct(shape, F32...]
  transfers between devices with their start and end apart: 43 -> 43, of which waited for: 14 -> 14; matrix products, arithmetic and copies ran while one was open for 0% -> 0% of each run, Pallas kernels for 25% -> 24%
where the time goes in v5:
time: 143 us
  starting transfers between devices  49 us (34%)
  waiting for transfers between devices  46.5 us (33%)
  Pallas kernels  40.4 us (28%)
  local copies, waits for them, and re-layouts  4.36 us (3%)
  between operations  1.59 us (1%)
    ppermute x42, starting transfers between devices, swap(): return lax.ppermute(x, axis, [(i, i ^ bits) for i in range(count)])  46.1 us
    ppermute x42, waiting for transfers between devices, swap(): return lax.ppermute(x, axis, [(i, i ^ bits) for i in range(count)])  41.4 us
    pallas_call x18, Pallas kernels, call(): pl.pallas_call(run, grid=(1,), out_shape=[jax.ShapeDtypeStruct(shape, F32...  40.4 us
    ppermute x1, waiting for transfers between devices, swap_outward(): lax.ppermute(x, axis, [pair for i in range(1, count - 1, 2) for pair in (...  5.06 us
    unnamed x38, local copies, waits for them, and re-layouts  4.36 us
    ppermute x1, starting transfers between devices, swap_outward(): lax.ppermute(x, axis, [pair for i in range(1, count - 1, 2) for pair in (...  2.91 us
  transfers between devices with their start and end apart: 43, of which 14 were waited for; matrix products, arithmetic and copies ran while one was open for 0% of the time, Pallas kernels for 24%

profile of v5, /device:TPU:13, one launch (start us, length us, event | category | flops | bytes accessed | tf_op | source)
XLA Modules:
  0.0 143.1 jit_solution(7012353765306035083)
XLA Ops:
  2.9 1.5 %collective-permute-done.refs_1_.refs_2_ = f32[4]{0:T(128)S(1)} collective-permute-done((f32[4]{0:T(128)S(1)}, f32[4]{0:T(128)S(1)}, u32[]{:S(2)}, u32[]{:S(2)}) %collective-permute-start) | collective-permute-done | bytes 48 | tf_op jit(solution)/shard_map/ppermute | solution.py:355
  5.0 2.2 %object.6 = (f32[2,4,64,128]{3,2,1,0:T(8,128)}, f32[2,4,64,128]{3,2,1,0:T(8,128)}) custom-call(s32[3]{0:T(128)} %pad_add_fusion.refs_0_, f32[4]{0:T(128)} %copy-done.12, f32[8,64,128]{2,1,0:T(8,128)} %refs_3_.19, f32[3,8,64,128]{3,2,1,0:T(8,128)} %refs_4_.13, s32[8,128,128]{2,1,0:T(8,128)} %refs_4_.15), custom_call_target="tpu_custom_call" | custom-call | flops 1638400 | bytes 1310720 | tf_op jit(solution)/shard_map/object/pallas_call | solution.py:96
  7.4 2.3 %object.7 = (f32[2,4,64,128]{3,2,1,0:T(8,128)}, f32[2,4,64,128]{3,2,1,0:T(8,128)}) custom-call(s32[3]{0:T(128)} %pad_add_fusion.refs_0_, f32[4]{0:T(128)} %copy-done.12, f32[8,64,128]{2,1,0:T(8,128)} %refs_3_.19, f32[3,8,64,128]{3,2,1,0:T(8,128)} %refs_4_.13, s32[8,128,128]{2,1,0:T(8,128)} %refs_4_.15, f32[2,4,64,128]{3,2,1,0:T(8,128)} %get-tuple-element.65.refs_5_), custom_call_target="tpu_custom_call" | custom-call | flops 1638400 | bytes 1310720 | tf_op jit(solution)/shard_map/object/pallas_call | solution.py:96
  15.5 2.5 %collective-permute-start.4 = (f32[2,4,64,128]{3,2,1,0:T(8,128)S(1)}, f32[2,4,64,128]{3,2,1,0:T(8,128)S(1)}, u32[]{:S(2)}, u32[]{:S(2)}) collective-permute-start(f32[2,4,64,128]{3,2,1,0:T(8,128)S(1)} %get-tuple-element.64.refs_2_), channel_id=1, source_target_pairs={{0,1},{1,0},{2,3},{3,2},{4,5},{5,4},{6,7},{7,6},{8,9},{9,8},{10,11... | collective-permute-start | bytes 786440 | tf_op jit(solution)/shard_map/ppermute | solution.py:355
  19.3 2.4 %collective-permute-start.6 = (f32[2,4,64,128]{3,2,1,0:T(8,128)S(1)}, f32[2,4,64,128]{3,2,1,0:T(8,128)S(1)}, u32[]{:S(2)}, u32[]{:S(2)}) collective-permute-start(f32[2,4,64,128]{3,2,1,0:T(8,128)S(1)} %collective-permute-done.2.refs_4_), channel_id=1, source_target_pairs={{0,1},{1,0},{2,3},{3,2},{4,5},{5,4},{6,7},{7,6},{8,9},{9,8},{10,11... | collective-permute-start | bytes 786440 | tf_op jit(solution)/shard_map/ppermute | solution.py:355
  22.9 1.7 %y_forward.2 = (f32[16,16,128]{2,1,0:T(8,128)S(1)}, f32[16,16,128]{2,1,0:T(8,128)S(1)}, f32[16,16,128]{2,1,0:T(8,128)S(1)}, f32[16,16,128]{2,1,0:T(8,128)S(1)}, ...) custom-call(s32[3]{0:T(128)S(1)} %copy-done.11, ...), custom_call_target="tpu_custom_call" | custom-call | flops 402653184 | bytes 3407872 | tf_op jit(solution)/shard_map/y_forward/pallas_call | solution.py:96
  24.6 3.3 %collective-permute-start.7 = (f32[16,16,128]{2,1,0:T(8,128)S(1)}, f32[16,16,128]{2,1,0:T(8,128)S(1)}, u32[]{:S(2)}, u32[]{:S(2)}) collective-permute-start(f32[16,16,128]{2,1,0:T(8,128)S(1)} %get-tuple-element.67), channel_id=1, source_target_pairs={{0,10},{1,11},{2,8},{3,9},{4,14},{5,15},{6,12},{7,13},{8,2},{9,3},... | collective-permute-start | bytes 393224 | tf_op jit(solution)/shard_map/ppermute | solution.py:355
  28.4 2.2 %collective-permute-start.24 = (f32[16,16,128]{2,1,0:T(8,128)S(1)}, f32[16,16,128]{2,1,0:T(8,128)S(1)}, u32[]{:S(2)}, u32[]{:S(2)}) collective-permute-start(f32[16,16,128]{2,1,0:T(8,128)S(1)} %get-tuple-element.87), channel_id=1, source_target_pairs={{0,6},{1,7},{2,4},{3,5},{4,2},{5,3},{6,0},{7,1},{8,14},{9,15},{10,... | collective-permute-start | bytes 393224 | tf_op jit(solution)/shard_map/ppermute | solution.py:355
  30.7 3.3 %collective-permute-done.7.refs_10_.refs_6_ = f32[16,16,128]{2,1,0:T(8,128)S(1)} collective-permute-done((f32[16,16,128]{2,1,0:T(8,128)S(1)}, f32[16,16,128]{2,1,0:T(8,128)S(1)}, u32[]{:S(2)}, u32[]{:S(2)}) %collective-permute-start.7) | collective-permute-done | bytes 131104 | tf_op jit(solution)/shard_map/ppermute | solution.py:355
  33.9 1.7 %y_forward.3 = (f32[16,16,128]{2,1,0:T(8,128)S(1)}, f32[16,16,128]{2,1,0:T(8,128)S(1)}, f32[16,16,128]{2,1,0:T(8,128)S(1)}, f32[16,16,128]{2,1,0:T(8,128)S(1)}, ...) custom-call(s32[3]{0:T(128)S(1)} %copy-done.11, ...), custom_call_target="tpu_custom_call" | custom-call | flops 402653184 | bytes 3407872 | tf_op jit(solution)/shard_map/y_forward/pallas_call | solution.py:96
  38.4 2.9 %collective-permute-start.9 = (f32[16,16,128]{2,1,0:T(8,128)S(1)}, f32[16,16,128]{2,1,0:T(8,128)S(1)}, u32[]{:S(2)}, u32[]{:S(2)}) collective-permute-start(f32[16,16,128]{2,1,0:T(8,128)S(1)} %get-tuple-element.70), channel_id=1, source_target_pairs={{0,4},{1,5},{2,6},{3,7},{4,0},{5,1},{6,2},{7,3},{8,12},{9,13},{10,... | collective-permute-start | bytes 393224 | tf_op jit(solution)/shard_map/ppermute | solution.py:355
  42.2 5.8 %collective-permute-done.26.refs_7_ = f32[16,16,128]{2,1,0:T(8,128)S(1)} collective-permute-done((f32[16,16,128]{2,1,0:T(8,128)S(1)}, f32[16,16,128]{2,1,0:T(8,128)S(1)}, u32[]{:S(2)}, u32[]{:S(2)}) %collective-permute-start.26) | collective-permute-done | bytes 131104 | tf_op jit(solution)/shard_map/ppermute | solution.py:355
  48.0 3.0 %collective-permute-done.27.refs_8_ = f32[16,16,128]{2,1,0:T(8,128)S(1)} collective-permute-done((f32[16,16,128]{2,1,0:T(8,128)S(1)}, f32[16,16,128]{2,1,0:T(8,128)S(1)}, u32[]{:S(2)}, u32[]{:S(2)}) %collective-permute-start.27) | collective-permute-done | bytes 131104 | tf_op jit(solution)/shard_map/ppermute | solution.py:355
  51.0 2.0 %collective-permute-start.13 = (f32[16,16,128]{2,1,0:T(8,128)S(1)}, f32[16,16,128]{2,1,0:T(8,128)S(1)}, u32[]{:S(2)}, u32[]{:S(2)}) collective-permute-start(f32[16,16,128]{2,1,0:T(8,128)S(1)} %get-tuple-element.74), channel_id=1, source_target_pairs={{0,12},{1,13},{2,14},{3,15},{4,8},{5,9},{6,10},{7,11},{8,4},{9,5},... | collective-permute-start | bytes 393224 | tf_op jit(solution)/shard_map/ppermute | solution.py:355
  54.0 9.2 %middle.3 = (f32[16,16,128]{2,1,0:T(8,128)S(1)}, f32[16,16,128]{2,1,0:T(8,128)S(1)}, f32[16,16,128]{2,1,0:T(8,128)S(1)}, f32[16,16,128]{2,1,0:T(8,128)S(1)}, f32...) custom-call(s32[3]{0:T(128)S(1)} %copy-done.11, ...), custom_call_target="tpu_custom_call" | custom-call | flops 4831838208 | bytes 3145728 | tf_op jit(solution)/shard_map/middle/pallas_call | solution.py:96
  64.8 4.0 %collective-permute-start.29 = (f32[16,16,128]{2,1,0:T(8,128)S(1)}, f32[16,16,128]{2,1,0:T(8,128)S(1)}, u32[]{:S(2)}, u32[]{:S(2)}) collective-permute-start(f32[16,16,128]{2,1,0:T(8,128)S(1)} %get-tuple-element.93), channel_id=1, source_target_pairs={{0,4},{1,5},{2,6},{3,7},{4,0},{5,1},{6,2},{7,3},{8,12},{9,13},{10,... | collective-permute-start | bytes 393224 | tf_op jit(solution)/shard_map/ppermute | solution.py:355
  70.7 3.3 %collective-permute-done.14.refs_8_ = f32[16,16,128]{2,1,0:T(8,128)S(1)} collective-permute-done((f32[16,16,128]{2,1,0:T(8,128)S(1)}, f32[16,16,128]{2,1,0:T(8,128)S(1)}, u32[]{:S(2)}, u32[]{:S(2)}) %collective-permute-start.14) | collective-permute-done | bytes 131104 | tf_op jit(solution)/shard_map/ppermute | solution.py:355
  74.0 9.4 %middle.2 = (f32[16,16,128]{2,1,0:T(8,128)S(1)}, f32[16,16,128]{2,1,0:T(8,128)S(1)}, f32[16,16,128]{2,1,0:T(8,128)S(1)}, f32[16,16,128]{2,1,0:T(8,128)S(1)}, f32...) custom-call(s32[3]{0:T(128)S(1)} %copy-done.11, ...), custom_call_target="tpu_custom_call" | custom-call | flops 4831838208 | bytes 3145728 | tf_op jit(solution)/shard_map/middle/pallas_call | solution.py:96
  83.6 2.9 %collective-permute-start.34 = (f32[16,16,128]{2,1,0:T(8,128)S(1)}, f32[16,16,128]{2,1,0:T(8,128)S(1)}, u32[]{:S(2)}, u32[]{:S(2)}) collective-permute-start(f32[16,16,128]{2,1,0:T(8,128)S(1)} %get-tuple-element.98), channel_id=1, source_target_pairs={{0,14},{1,15},{2,12},{3,13},{4,10},{5,11},{6,8},{7,9},{8,6},{9,7},... | collective-permute-start | bytes 393224 | tf_op jit(solution)/shard_map/ppermute | solution.py:355
  86.5 5.2 %collective-permute-start.16 = (f32[16,16,128]{2,1,0:T(8,128)S(1)}, f32[16,16,128]{2,1,0:T(8,128)S(1)}, u32[]{:S(2)}, u32[]{:S(2)}) collective-permute-start(f32[16,16,128]{2,1,0:T(8,128)S(1)} %get-tuple-element.78), channel_id=1, source_target_pairs={{0,4},{1,5},{2,6},{3,7},{4,0},{5,1},{6,2},{7,3},{8,12},{9,13},{10,... | collective-permute-start | bytes 393224 | tf_op jit(solution)/shard_map/ppermute | solution.py:355
  93.1 2.7 %collective-permute-done.34.refs_8_ = f32[16,16,128]{2,1,0:T(8,128)S(1)} collective-permute-done((f32[16,16,128]{2,1,0:T(8,128)S(1)}, f32[16,16,128]{2,1,0:T(8,128)S(1)}, u32[]{:S(2)}, u32[]{:S(2)}) %collective-permute-start.34) | collective-permute-done | bytes 131104 | tf_op jit(solution)/shard_map/ppermute | solution.py:355
  95.8 2.8 %collective-permute-start.20 = (f32[16,16,128]{2,1,0:T(8,128)S(1)}, f32[16,16,128]{2,1,0:T(8,128)S(1)}, u32[]{:S(2)}, u32[]{:S(2)}) collective-permute-start(f32[16,16,128]{2,1,0:T(8,128)S(1)} %get-tuple-element.82), channel_id=1, source_target_pairs={{0,12},{1,13},{2,14},{3,15},{4,8},{5,9},{6,10},{7,11},{8,4},{9,5},... | collective-permute-start | bytes 393224 | tf_op jit(solution)/shard_map/ppermute | solution.py:355
  98.8 2.0 %y_adjoint.4 = (f32[2,4,64,128]{3,2,1,0:T(8,128)S(1)}, f32[2,4,64,128]{3,2,1,0:T(8,128)S(1)}, f32[2,4,64,128]{3,2,1,0:T(8,128)S(1)}, f32[2,4,64,128]{3,2,1,0:T(8...) custom-call(s32[3]{0:T(128)S(1)} %copy-done.11, ...), custom_call_target="tpu_custom_call" | custom-call | flops 402653184 | bytes 3411968 | tf_op jit(solution)/shard_map/y_adjoint/pallas_call | solution.py:96
  100.9 2.7 %collective-permute-done.17.refs_4_ = f32[16,16,128]{2,1,0:T(8,128)S(1)} collective-permute-done((f32[16,16,128]{2,1,0:T(8,128)S(1)}, f32[16,16,128]{2,1,0:T(8,128)S(1)}, u32[]{:S(2)}, u32[]{:S(2)}) %collective-permute-start.17) | collective-permute-done | bytes 131104 | tf_op jit(solution)/shard_map/ppermute | solution.py:355
  103.5 8.7 %collective-permute-done.19.refs_6_ = f32[16,16,128]{2,1,0:T(8,128)S(1)} collective-permute-done((f32[16,16,128]{2,1,0:T(8,128)S(1)}, f32[16,16,128]{2,1,0:T(8,128)S(1)}, u32[]{:S(2)}, u32[]{:S(2)}) %collective-permute-start.19) | collective-permute-done | bytes 131104 | tf_op jit(solution)/shard_map/ppermute | solution.py:355
  112.3 4.0 %collective-permute-done.20.refs_7_ = f32[16,16,128]{2,1,0:T(8,128)S(1)} collective-permute-done((f32[16,16,128]{2,1,0:T(8,128)S(1)}, f32[16,16,128]{2,1,0:T(8,128)S(1)}, u32[]{:S(2)}, u32[]{:S(2)}) %collective-permute-start.20) | collective-permute-done | bytes 131104 | tf_op jit(solution)/shard_map/ppermute | solution.py:355
  116.3 3.1 %collective-permute-done.21.refs_8_ = f32[16,16,128]{2,1,0:T(8,128)S(1)} collective-permute-done((f32[16,16,128]{2,1,0:T(8,128)S(1)}, f32[16,16,128]{2,1,0:T(8,128)S(1)}, u32[]{:S(2)}, u32[]{:S(2)}) %collective-permute-start.21) | collective-permute-done | bytes 131104 | tf_op jit(solution)/shard_map/ppermute | solution.py:355
  120.3 2.5 %collective-permute-start.35 = (f32[2,4,64,128]{3,2,1,0:T(8,128)S(1)}, f32[2,4,64,128]{3,2,1,0:T(8,128)S(1)}, u32[]{:S(2)}, u32[]{:S(2)}) collective-permute-start(f32[2,4,64,128]{3,2,1,0:T(8,128)S(1)} %get-tuple-element.105), channel_id=1, source_target_pairs={{0,1},{1,0},{2,3},{3,2},{4,5},{5,4},{6,7},{7,6},{8,9},{9,8},{10,11... | collective-permute-start | bytes 786440 | tf_op jit(solution)/shard_map/ppermute | solution.py:355
  127.3 1.7 %y_adjoint.7 = (f32[2,4,64,128]{3,2,1,0:T(8,128)S(1)}, f32[2,4,64,128]{3,2,1,0:T(8,128)S(1)}, f32[2,4,64,128]{3,2,1,0:T(8,128)S(1)}, f32[2,4,64,128]{3,2,1,0:T(8,128)S(1)}, f32[8,128]{1,0:T(8,128)}) custom-call(s32[3]{0:T(128)S(1)} %copy-done.11, f32[16,16,128]{2,1,0:T(8,128)S(1)} %get-tuple-element.76.refs_1_, ...), custom_call_target="tpu_custom_call" | custom-call | flops 201326592 | bytes 3411968 | tf_op jit(solution)/shard_map/y_adjoint/pallas_call | solution.py:96
  130.8 2.9 %collective-permute-start.37 = (f32[4,64,128]{2,1,0:T(8,128)S(1)}, f32[4,64,128]{2,1,0:T(8,128)S(1)}, u32[]{:S(2)}, u32[]{:S(2)}) collective-permute-start(f32[4,64,128]{2,1,0:T(8,128)S(1)} %get-tuple-element.107), channel_id=1, source_target_pairs={{1,2},{2,1},{3,4},{4,3},{5,6},{6,5},{7,8},{8,7},{9,10},{10,9},{11,... | collective-permute-start | bytes 393224 | tf_op jit(solution)/shard_map/ppermute | solution.py:360
  133.7 5.1 %collective-permute-done.37.refs_5_ = f32[4,64,128]{2,1,0:T(8,128)S(1)} collective-permute-done((f32[4,64,128]{2,1,0:T(8,128)S(1)}, f32[4,64,128]{2,1,0:T(8,128)S(1)}, u32[]{:S(2)}, u32[]{:S(2)}) %collective-permute-start.37) | collective-permute-done | bytes 131104 | tf_op jit(solution)/shard_map/ppermute | solution.py:360
  140.0 1.5 %final.2 = (f32[8,64,128]{2,1,0:T(8,128)}, f32[3,8,64,128]{3,2,1,0:T(8,128)}) custom-call(s32[3]{0:T(128)S(1)} %copy-done.11, f32[4]{0:T(128)S(1)} %pad_maximum_fusion.refs_1_, f32[4]{0:T(128)S(1)} %copy-done.13, f32[8,64,128]{2,1,0:T(8,128)S(1)} %copy-done.5, s32[8,128,128]{2,1,0:T(8,128)S(1)} %copy-done.1, f32[4,8,64,128]{3,2,1,0:T(8,128)S(1)} %laplace.1.refs_5_, ...), custom_call_target="tpu_custom_call" | custom-call | flops 1310720 | bytes 3309568 | tf_op jit(solution)/shard_map/final/pallas_call | solution.py:96
  (113 shorter events, 30.8 us)
Async XLA Ops:
  7.2 11.6 %collective-permute-start.1 = (f32[2,4,64,128]{3,2,1,0:T(8,128)}, f32[2,4,64,128]{3,2,1,0:T(8,128)S(1)}, u32[]{:S(2)}, u32[]{:S(2)}) collective-permute-start(f32[2,4,64,128]{3,2,1,0:T(8,128)} %get-tuple-element.65.refs_5_), channel_id=1, source_target_pairs={{0,16},{16,0},{1,17},{17,1},{2,18},{18,2},{3,19},{19,3},{4,20},{20... | collective-permute-start | bytes 786440 | tf_op jit(solution)/shard_map/ppermute | solution.py:355
  9.7 9.6 %collective-permute-start.2 = (f32[2,4,64,128]{3,2,1,0:T(8,128)}, f32[2,4,64,128]{3,2,1,0:T(8,128)S(1)}, u32[]{:S(2)}, u32[]{:S(2)}) collective-permute-start(f32[2,4,64,128]{3,2,1,0:T(8,128)} %get-tuple-element.66), channel_id=1, source_target_pairs={{0,16},{16,0},{1,17},{17,1},{2,18},{18,2},{3,19},{19,3},{4,20},{20... | collective-permute-start | bytes 786440 | tf_op jit(solution)/shard_map/ppermute | solution.py:355
  24.6 9.3 %collective-permute-start.7 = (f32[16,16,128]{2,1,0:T(8,128)S(1)}, f32[16,16,128]{2,1,0:T(8,128)S(1)}, u32[]{:S(2)}, u32[]{:S(2)}) collective-permute-start(f32[16,16,128]{2,1,0:T(8,128)S(1)} %get-tuple-element.67), channel_id=1, source_target_pairs={{0,10},{1,11},{2,8},{3,9},{4,14},{5,15},{6,12},{7,13},{8,2},{9,3},... | collective-permute-start | bytes 393224 | tf_op jit(solution)/shard_map/ppermute | solution.py:355
  28.2 9.0 %collective-permute-start.23 = (f32[16,16,128]{2,1,0:T(8,128)S(1)}, f32[16,16,128]{2,1,0:T(8,128)S(1)}, u32[]{:S(2)}, u32[]{:S(2)}) collective-permute-start(f32[16,16,128]{2,1,0:T(8,128)S(1)} %get-tuple-element.86), channel_id=1, source_target_pairs={{0,4},{1,5},{2,6},{3,7},{4,0},{5,1},{6,2},{7,3},{8,12},{9,13},{10,... | collective-permute-start | bytes 393224 | tf_op jit(solution)/shard_map/ppermute | solution.py:355
  28.4 10.0 %collective-permute-start.24 = (f32[16,16,128]{2,1,0:T(8,128)S(1)}, f32[16,16,128]{2,1,0:T(8,128)S(1)}, u32[]{:S(2)}, u32[]{:S(2)}) collective-permute-start(f32[16,16,128]{2,1,0:T(8,128)S(1)} %get-tuple-element.87), channel_id=1, source_target_pairs={{0,6},{1,7},{2,4},{3,5},{4,2},{5,3},{6,0},{7,1},{8,14},{9,15},{10,... | collective-permute-start | bytes 393224 | tf_op jit(solution)/shard_map/ppermute | solution.py:355
  30.6 10.7 %collective-permute-start.25 = (f32[16,16,128]{2,1,0:T(8,128)S(1)}, f32[16,16,128]{2,1,0:T(8,128)S(1)}, u32[]{:S(2)}, u32[]{:S(2)}) collective-permute-start(f32[16,16,128]{2,1,0:T(8,128)S(1)} %get-tuple-element.88), channel_id=1, source_target_pairs={{0,8},{1,9},{2,10},{3,11},{4,12},{5,13},{6,14},{7,15},{8,0},{9,1},... | collective-permute-start | bytes 393224 | tf_op jit(solution)/shard_map/ppermute | solution.py:355
  33.9 14.0 %collective-permute-start.26 = (f32[16,16,128]{2,1,0:T(8,128)S(1)}, f32[16,16,128]{2,1,0:T(8,128)S(1)}, u32[]{:S(2)}, u32[]{:S(2)}) collective-permute-start(f32[16,16,128]{2,1,0:T(8,128)S(1)} %get-tuple-element.89), channel_id=1, source_target_pairs={{0,12},{1,13},{2,14},{3,15},{4,8},{5,9},{6,10},{7,11},{8,4},{9,5},... | collective-permute-start | bytes 393224 | tf_op jit(solution)/shard_map/ppermute | solution.py:355
  35.7 15.3 %collective-permute-start.27 = (f32[16,16,128]{2,1,0:T(8,128)S(1)}, f32[16,16,128]{2,1,0:T(8,128)S(1)}, u32[]{:S(2)}, u32[]{:S(2)}) collective-permute-start(f32[16,16,128]{2,1,0:T(8,128)S(1)} %get-tuple-element.90), channel_id=1, source_target_pairs={{0,14},{1,15},{2,12},{3,13},{4,10},{5,11},{6,8},{7,9},{8,6},{9,7},... | collective-permute-start | bytes 393224 | tf_op jit(solution)/shard_map/ppermute | solution.py:355
  37.2 13.8 %collective-permute-start.8 = (f32[16,16,128]{2,1,0:T(8,128)S(1)}, f32[16,16,128]{2,1,0:T(8,128)S(1)}, u32[]{:S(2)}, u32[]{:S(2)}) collective-permute-start(f32[16,16,128]{2,1,0:T(8,128)S(1)} %get-tuple-element.69), channel_id=1, source_target_pairs={{0,2},{1,3},{2,0},{3,1},{4,6},{5,7},{6,4},{7,5},{8,10},{9,11},{10,... | collective-permute-start | bytes 393224 | tf_op jit(solution)/shard_map/ppermute | solution.py:355
  38.4 14.6 %collective-permute-start.9 = (f32[16,16,128]{2,1,0:T(8,128)S(1)}, f32[16,16,128]{2,1,0:T(8,128)S(1)}, u32[]{:S(2)}, u32[]{:S(2)}) collective-permute-start(f32[16,16,128]{2,1,0:T(8,128)S(1)} %get-tuple-element.70), channel_id=1, source_target_pairs={{0,4},{1,5},{2,6},{3,7},{4,0},{5,1},{6,2},{7,3},{8,12},{9,13},{10,... | collective-permute-start | bytes 393224 | tf_op jit(solution)/shard_map/ppermute | solution.py:355
  41.3 21.9 %collective-permute-start.10 = (f32[16,16,128]{2,1,0:T(8,128)S(1)}, f32[16,16,128]{2,1,0:T(8,128)S(1)}, u32[]{:S(2)}, u32[]{:S(2)}) collective-permute-start(f32[16,16,128]{2,1,0:T(8,128)S(1)} %get-tuple-element.71), channel_id=1, source_target_pairs={{0,6},{1,7},{2,4},{3,5},{4,2},{5,3},{6,0},{7,1},{8,14},{9,15},{10,... | collective-permute-start | bytes 393224 | tf_op jit(solution)/shard_map/ppermute | solution.py:355
  48.0 16.9 %collective-permute-start.11 = (f32[16,16,128]{2,1,0:T(8,128)S(1)}, f32[16,16,128]{2,1,0:T(8,128)S(1)}, u32[]{:S(2)}, u32[]{:S(2)}) collective-permute-start(f32[16,16,128]{2,1,0:T(8,128)S(1)} %get-tuple-element.72), channel_id=1, source_target_pairs={{0,8},{1,9},{2,10},{3,11},{4,12},{5,13},{6,14},{7,15},{8,0},{9,1},... | collective-permute-start | bytes 393224 | tf_op jit(solution)/shard_map/ppermute | solution.py:355
  51.0 17.8 %collective-permute-start.12 = (f32[16,16,128]{2,1,0:T(8,128)S(1)}, f32[16,16,128]{2,1,0:T(8,128)S(1)}, u32[]{:S(2)}, u32[]{:S(2)}) collective-permute-start(f32[16,16,128]{2,1,0:T(8,128)S(1)} %get-tuple-element.73), channel_id=1, source_target_pairs={{0,10},{1,11},{2,8},{3,9},{4,14},{5,15},{6,12},{7,13},{8,2},{9,3},... | collective-permute-start | bytes 393224 | tf_op jit(solution)/shard_map/ppermute | solution.py:355
  51.0 19.6 %collective-permute-start.13 = (f32[16,16,128]{2,1,0:T(8,128)S(1)}, f32[16,16,128]{2,1,0:T(8,128)S(1)}, u32[]{:S(2)}, u32[]{:S(2)}) collective-permute-start(f32[16,16,128]{2,1,0:T(8,128)S(1)} %get-tuple-element.74), channel_id=1, source_target_pairs={{0,12},{1,13},{2,14},{3,15},{4,8},{5,9},{6,10},{7,11},{8,4},{9,5},... | collective-permute-start | bytes 393224 | tf_op jit(solution)/shard_map/ppermute | solution.py:355
  53.0 21.0 %collective-permute-start.14 = (f32[16,16,128]{2,1,0:T(8,128)S(1)}, f32[16,16,128]{2,1,0:T(8,128)S(1)}, u32[]{:S(2)}, u32[]{:S(2)}) collective-permute-start(f32[16,16,128]{2,1,0:T(8,128)S(1)} %get-tuple-element.75), channel_id=1, source_target_pairs={{0,14},{1,15},{2,12},{3,13},{4,10},{5,11},{6,8},{7,9},{8,6},{9,7},... | collective-permute-start | bytes 393224 | tf_op jit(solution)/shard_map/ppermute | solution.py:355
  63.2 20.3 %collective-permute-start.28 = (f32[16,16,128]{2,1,0:T(8,128)S(1)}, f32[16,16,128]{2,1,0:T(8,128)S(1)}, u32[]{:S(2)}, u32[]{:S(2)}) collective-permute-start(f32[16,16,128]{2,1,0:T(8,128)S(1)} %get-tuple-element.92), channel_id=1, source_target_pairs={{0,2},{1,3},{2,0},{3,1},{4,6},{5,7},{6,4},{7,5},{8,10},{9,11},{10,... | collective-permute-start | bytes 393224 | tf_op jit(solution)/shard_map/ppermute | solution.py:355
  64.8 18.7 %collective-permute-start.29 = (f32[16,16,128]{2,1,0:T(8,128)S(1)}, f32[16,16,128]{2,1,0:T(8,128)S(1)}, u32[]{:S(2)}, u32[]{:S(2)}) collective-permute-start(f32[16,16,128]{2,1,0:T(8,128)S(1)} %get-tuple-element.93), channel_id=1, source_target_pairs={{0,4},{1,5},{2,6},{3,7},{4,0},{5,1},{6,2},{7,3},{8,12},{9,13},{10,... | collective-permute-start | bytes 393224 | tf_op jit(solution)/shard_map/ppermute | solution.py:355
  68.8 17.7 %collective-permute-start.30 = (f32[16,16,128]{2,1,0:T(8,128)S(1)}, f32[16,16,128]{2,1,0:T(8,128)S(1)}, u32[]{:S(2)}, u32[]{:S(2)}) collective-permute-start(f32[16,16,128]{2,1,0:T(8,128)S(1)} %get-tuple-element.94), channel_id=1, source_target_pairs={{0,6},{1,7},{2,4},{3,5},{4,2},{5,3},{6,0},{7,1},{8,14},{9,15},{10,... | collective-permute-start | bytes 393224 | tf_op jit(solution)/shard_map/ppermute | solution.py:355
  70.7 15.8 %collective-permute-start.31 = (f32[16,16,128]{2,1,0:T(8,128)S(1)}, f32[16,16,128]{2,1,0:T(8,128)S(1)}, u32[]{:S(2)}, u32[]{:S(2)}) collective-permute-start(f32[16,16,128]{2,1,0:T(8,128)S(1)} %get-tuple-element.95), channel_id=1, source_target_pairs={{0,8},{1,9},{2,10},{3,11},{4,12},{5,13},{6,14},{7,15},{8,0},{9,1},... | collective-permute-start | bytes 393224 | tf_op jit(solution)/shard_map/ppermute | solution.py:355
  74.0 17.7 %collective-permute-start.32 = (f32[16,16,128]{2,1,0:T(8,128)S(1)}, f32[16,16,128]{2,1,0:T(8,128)S(1)}, u32[]{:S(2)}, u32[]{:S(2)}) collective-permute-start(f32[16,16,128]{2,1,0:T(8,128)S(1)} %get-tuple-element.96), channel_id=1, source_target_pairs={{0,10},{1,11},{2,8},{3,9},{4,14},{5,15},{6,12},{7,13},{8,2},{9,3},... | collective-permute-start | bytes 393224 | tf_op jit(solution)/shard_map/ppermute | solution.py:355
  83.6 12.2 %collective-permute-start.34 = (f32[16,16,128]{2,1,0:T(8,128)S(1)}, f32[16,16,128]{2,1,0:T(8,128)S(1)}, u32[]{:S(2)}, u32[]{:S(2)}) collective-permute-start(f32[16,16,128]{2,1,0:T(8,128)S(1)} %get-tuple-element.98), channel_id=1, source_target_pairs={{0,14},{1,15},{2,12},{3,13},{4,10},{5,11},{6,8},{7,9},{8,6},{9,7},... | collective-permute-start | bytes 393224 | tf_op jit(solution)/shard_map/ppermute | solution.py:355
  86.5 9.3 %collective-permute-start.15 = (f32[16,16,128]{2,1,0:T(8,128)S(1)}, f32[16,16,128]{2,1,0:T(8,128)S(1)}, u32[]{:S(2)}, u32[]{:S(2)}) collective-permute-start(f32[16,16,128]{2,1,0:T(8,128)S(1)} %get-tuple-element.77), channel_id=1, source_target_pairs={{0,2},{1,3},{2,0},{3,1},{4,6},{5,7},{6,4},{7,5},{8,10},{9,11},{10,... | collective-permute-start | bytes 393224 | tf_op jit(solution)/shard_map/ppermute | solution.py:355
  86.5 12.1 %collective-permute-start.16 = (f32[16,16,128]{2,1,0:T(8,128)S(1)}, f32[16,16,128]{2,1,0:T(8,128)S(1)}, u32[]{:S(2)}, u32[]{:S(2)}) collective-permute-start(f32[16,16,128]{2,1,0:T(8,128)S(1)} %get-tuple-element.78), channel_id=1, source_target_pairs={{0,4},{1,5},{2,6},{3,7},{4,0},{5,1},{6,2},{7,3},{8,12},{9,13},{10,... | collective-permute-start | bytes 393224 | tf_op jit(solution)/shard_map/ppermute | solution.py:355
  91.7 11.9 %collective-permute-start.17 = (f32[16,16,128]{2,1,0:T(8,128)S(1)}, f32[16,16,128]{2,1,0:T(8,128)S(1)}, u32[]{:S(2)}, u32[]{:S(2)}) collective-permute-start(f32[16,16,128]{2,1,0:T(8,128)S(1)} %get-tuple-element.79), channel_id=1, source_target_pairs={{0,6},{1,7},{2,4},{3,5},{4,2},{5,3},{6,0},{7,1},{8,14},{9,15},{10,... | collective-permute-start | bytes 393224 | tf_op jit(solution)/shard_map/ppermute | solution.py:355
  91.7 11.8 %collective-permute-start.18 = (f32[16,16,128]{2,1,0:T(8,128)S(1)}, f32[16,16,128]{2,1,0:T(8,128)S(1)}, u32[]{:S(2)}, u32[]{:S(2)}) collective-permute-start(f32[16,16,128]{2,1,0:T(8,128)S(1)} %get-tuple-element.80), channel_id=1, source_target_pairs={{0,8},{1,9},{2,10},{3,11},{4,12},{5,13},{6,14},{7,15},{8,0},{9,1},... | collective-permute-start | bytes 393224 | tf_op jit(solution)/shard_map/ppermute | solution.py:355
  95.8 16.4 %collective-permute-start.19 = (f32[16,16,128]{2,1,0:T(8,128)S(1)}, f32[16,16,128]{2,1,0:T(8,128)S(1)}, u32[]{:S(2)}, u32[]{:S(2)}) collective-permute-start(f32[16,16,128]{2,1,0:T(8,128)S(1)} %get-tuple-element.81), channel_id=1, source_target_pairs={{0,10},{1,11},{2,8},{3,9},{4,14},{5,15},{6,12},{7,13},{8,2},{9,3},... | collective-permute-start | bytes 393224 | tf_op jit(solution)/shard_map/ppermute | solution.py:355
  95.8 20.4 %collective-permute-start.20 = (f32[16,16,128]{2,1,0:T(8,128)S(1)}, f32[16,16,128]{2,1,0:T(8,128)S(1)}, u32[]{:S(2)}, u32[]{:S(2)}) collective-permute-start(f32[16,16,128]{2,1,0:T(8,128)S(1)} %get-tuple-element.82), channel_id=1, source_target_pairs={{0,12},{1,13},{2,14},{3,15},{4,8},{5,9},{6,10},{7,11},{8,4},{9,5},... | collective-permute-start | bytes 393224 | tf_op jit(solution)/shard_map/ppermute | solution.py:355
  98.6 20.7 %collective-permute-start.21 = (f32[16,16,128]{2,1,0:T(8,128)S(1)}, f32[16,16,128]{2,1,0:T(8,128)S(1)}, u32[]{:S(2)}, u32[]{:S(2)}) collective-permute-start(f32[16,16,128]{2,1,0:T(8,128)S(1)} %get-tuple-element.83), channel_id=1, source_target_pairs={{0,14},{1,15},{2,12},{3,13},{4,10},{5,11},{6,8},{7,9},{8,6},{9,7},... | collective-permute-start | bytes 393224 | tf_op jit(solution)/shard_map/ppermute | solution.py:355
  125.0 13.7 %collective-permute-start.38 = (f32[576,128]{1,0:T(8,128)S(1)}, f32[576,128]{1,0:T(8,128)S(1)}, u32[]{:S(2)}, u32[]{:S(2)}) collective-permute-start(f32[576,128]{1,0:T(8,128)S(1)} %pack.2.refs_4_.refs_14_), channel_id=1, source_target_pairs={{0,16},{16,0},{1,17},{17,1},{2,18},{18,2},{3,19},{19,3},{4,20},{20... | collective-permute-start | bytes 884744 | tf_op jit(solution)/shard_map/ppermute | solution.py:355
  129.0 11.0 %collective-permute-start.42 = (f32[2,4,64,128]{3,2,1,0:T(8,128)S(1)}, f32[2,4,64,128]{3,2,1,0:T(8,128)S(1)}, u32[]{:S(2)}, u32[]{:S(2)}) collective-permute-start(f32[2,4,64,128]{3,2,1,0:T(8,128)S(1)} %get-tuple-element.119), channel_id=1, source_target_pairs={{0,1},{1,0},{2,3},{3,2},{4,5},{5,4},{6,7},{7,6},{8,9},{9,8},{10,11... | collective-permute-start | bytes 786440 | tf_op jit(solution)/shard_map/ppermute | solution.py:355
  129.0 12.5 %collective-permute-start.40 = (f32[2,4,64,128]{3,2,1,0:T(8,128)S(1)}, f32[2,4,64,128]{3,2,1,0:T(8,128)S(1)}, u32[]{:S(2)}, u32[]{:S(2)}) collective-permute-start(f32[2,4,64,128]{3,2,1,0:T(8,128)S(1)} %get-tuple-element.115), channel_id=1, source_target_pairs={{0,1},{1,0},{2,3},{3,2},{4,5},{5,4},{6,7},{7,6},{8,9},{9,8},{10,11... | collective-permute-start | bytes 786440 | tf_op jit(solution)/shard_map/ppermute | solution.py:355
  129.5 12.1 %collective-permute-start.41 = (f32[512,128]{1,0:T(8,128)S(1)}, f32[512,128]{1,0:T(8,128)S(1)}, u32[]{:S(2)}, u32[]{:S(2)}) collective-permute-start(f32[512,128]{1,0:T(8,128)S(1)} %pack.3.refs_15_), channel_id=1, source_target_pairs={{0,16},{16,0},{1,17},{17,1},{2,18},{18,2},{3,19},{19,3},{4,20},{20... | collective-permute-start | bytes 786440 | tf_op jit(solution)/shard_map/ppermute | solution.py:355
  (30 other events, 532.6 us)

commit v6 on v4

--- a/solution.py
+++ b/solution.py
@@ -506,7 +506,7 @@
     mine, unused = y_adjoint(at, returned, jobs[False], everyone[:1], adds, sums)
     mates = [swap(for_mate[job][0], "slab", 1) for job in jobs[True]]
     own = [mine[job][0] for job in jobs[False]]
-    edges = call(edges_kernel, [(4, rows, depth)] * 2, [place], fields, [], cells, "edges", first=sums)
+    edges = call(edges_kernel, [(4, rows, depth)] * 2, [place], fields, [], cells, "edges", first=sums[:1])
     halos = (swap(edges[0], "slab", 1), swap_outward(edges[1], "slab"), *[one[0] for one in others])
     (lapped,) = call(
         functools.partial(laplace_kernel, refls),

time: 143 us -> 143 us (level)
  no operation moved by 1% of the time
where the time goes in v6:
time: 143 us
  starting transfers between devices  49 us (34%)
  waiting for transfers between devices  44.9 us (31%)
  Pallas kernels  41.5 us (29%)
  local copies, waits for them, and re-layouts  4.42 us (3%)
  between operations  1.62 us (1%)
    ppermute x42, starting transfers between devices, swap(): return lax.ppermute(x, axis, [(i, i ^ bits) for i in range(count)])  46.6 us
    pallas_call x19, Pallas kernels, call(): pl.pallas_call(run, grid=(1,), out_shape=[jax.ShapeDtypeStruct(shape, F32...  41.5 us
    ppermute x42, waiting for transfers between devices, swap(): return lax.ppermute(x, axis, [(i, i ^ bits) for i in range(count)])  40.8 us
    unnamed x38, local copies, waits for them, and re-layouts  4.42 us
    ppermute x1, waiting for transfers between devices, swap_outward(): lax.ppermute(x, axis, [pair for i in range(1, count - 1, 2) for pair in (...  4.1 us
  transfers between devices with their start and end apart: 43, of which 14 were waited for; matrix products, arithmetic and copies ran while one was open for 0% of the time, Pallas kernels for 25%

profile of v6, /device:TPU:13, one launch (start us, length us, event | category | flops | bytes accessed | tf_op | source)
XLA Modules:
  0.0 142.8 jit_solution(18138281009660178366)
XLA Ops:
  2.9 1.5 %collective-permute-done.refs_1_.refs_2_ = f32[4]{0:T(128)S(1)} collective-permute-done((f32[4]{0:T(128)S(1)}, f32[4]{0:T(128)S(1)}, u32[]{:S(2)}, u32[]{:S(2)}) %collective-permute-start) | collective-permute-done | bytes 48 | tf_op jit(solution)/shard_map/ppermute | solution.py:355
  5.1 2.2 %object.6 = (f32[2,4,64,128]{3,2,1,0:T(8,128)}, f32[2,4,64,128]{3,2,1,0:T(8,128)}) custom-call(s32[3]{0:T(128)} %pad_add_fusion.refs_0_, f32[4]{0:T(128)} %copy-done.12, f32[8,64,128]{2,1,0:T(8,128)} %refs_3_.19, f32[3,8,64,128]{3,2,1,0:T(8,128)} %refs_4_.13, s32[8,128,128]{2,1,0:T(8,128)} %refs_4_.15), custom_call_target="tpu_custom_call" | custom-call | flops 1638400 | bytes 1310720 | tf_op jit(solution)/shard_map/object/pallas_call | solution.py:96
  7.5 2.3 %object.7 = (f32[2,4,64,128]{3,2,1,0:T(8,128)}, f32[2,4,64,128]{3,2,1,0:T(8,128)}) custom-call(s32[3]{0:T(128)} %pad_add_fusion.refs_0_, f32[4]{0:T(128)} %copy-done.12, f32[8,64,128]{2,1,0:T(8,128)} %refs_3_.19, f32[3,8,64,128]{3,2,1,0:T(8,128)} %refs_4_.13, s32[8,128,128]{2,1,0:T(8,128)} %refs_4_.15, f32[2,4,64,128]{3,2,1,0:T(8,128)} %get-tuple-element.65.refs_5_), custom_call_target="tpu_custom_call" | custom-call | flops 1638400 | bytes 1310720 | tf_op jit(solution)/shard_map/object/pallas_call | solution.py:96
  15.6 2.5 %collective-permute-start.4 = (f32[2,4,64,128]{3,2,1,0:T(8,128)S(1)}, f32[2,4,64,128]{3,2,1,0:T(8,128)S(1)}, u32[]{:S(2)}, u32[]{:S(2)}) collective-permute-start(f32[2,4,64,128]{3,2,1,0:T(8,128)S(1)} %get-tuple-element.64.refs_2_), channel_id=1, source_target_pairs={{0,1},{1,0},{2,3},{3,2},{4,5},{5,4},{6,7},{7,6},{8,9},{9,8},{10,11... | collective-permute-start | bytes 786440 | tf_op jit(solution)/shard_map/ppermute | solution.py:355
  19.4 2.4 %collective-permute-start.6 = (f32[2,4,64,128]{3,2,1,0:T(8,128)S(1)}, f32[2,4,64,128]{3,2,1,0:T(8,128)S(1)}, u32[]{:S(2)}, u32[]{:S(2)}) collective-permute-start(f32[2,4,64,128]{3,2,1,0:T(8,128)S(1)} %collective-permute-done.2.refs_4_), channel_id=1, source_target_pairs={{0,1},{1,0},{2,3},{3,2},{4,5},{5,4},{6,7},{7,6},{8,9},{9,8},{10,11... | collective-permute-start | bytes 786440 | tf_op jit(solution)/shard_map/ppermute | solution.py:355
  23.0 1.7 %y_forward.2 = (f32[16,16,128]{2,1,0:T(8,128)S(1)}, f32[16,16,128]{2,1,0:T(8,128)S(1)}, f32[16,16,128]{2,1,0:T(8,128)S(1)}, f32[16,16,128]{2,1,0:T(8,128)S(1)}, ...) custom-call(s32[3]{0:T(128)S(1)} %copy-done.11, ...), custom_call_target="tpu_custom_call" | custom-call | flops 402653184 | bytes 3407872 | tf_op jit(solution)/shard_map/y_forward/pallas_call | solution.py:96
  24.7 2.4 %collective-permute-start.7 = (f32[16,16,128]{2,1,0:T(8,128)S(1)}, f32[16,16,128]{2,1,0:T(8,128)S(1)}, u32[]{:S(2)}, u32[]{:S(2)}) collective-permute-start(f32[16,16,128]{2,1,0:T(8,128)S(1)} %get-tuple-element.67), channel_id=1, source_target_pairs={{0,8},{1,9},{2,10},{3,11},{4,12},{5,13},{6,14},{7,15},{8,0},{9,1},... | collective-permute-start | bytes 393224 | tf_op jit(solution)/shard_map/ppermute | solution.py:355
  30.7 2.3 %collective-permute-done.7.refs_10_.refs_5_ = f32[16,16,128]{2,1,0:T(8,128)S(1)} collective-permute-done((f32[16,16,128]{2,1,0:T(8,128)S(1)}, f32[16,16,128]{2,1,0:T(8,128)S(1)}, u32[]{:S(2)}, u32[]{:S(2)}) %collective-permute-start.7) | collective-permute-done | bytes 131104 | tf_op jit(solution)/shard_map/ppermute | solution.py:355
  33.1 1.7 %y_forward.3 = (f32[16,16,128]{2,1,0:T(8,128)S(1)}, f32[16,16,128]{2,1,0:T(8,128)S(1)}, f32[16,16,128]{2,1,0:T(8,128)S(1)}, f32[16,16,128]{2,1,0:T(8,128)S(1)}, ...) custom-call(s32[3]{0:T(128)S(1)} %copy-done.11, ...), custom_call_target="tpu_custom_call" | custom-call | flops 402653184 | bytes 3407872 | tf_op jit(solution)/shard_map/y_forward/pallas_call | solution.py:96
  34.8 2.5 %collective-permute-start.27 = (f32[16,16,128]{2,1,0:T(8,128)S(1)}, f32[16,16,128]{2,1,0:T(8,128)S(1)}, u32[]{:S(2)}, u32[]{:S(2)}) collective-permute-start(f32[16,16,128]{2,1,0:T(8,128)S(1)} %get-tuple-element.90), channel_id=1, source_target_pairs={{0,14},{1,15},{2,12},{3,13},{4,10},{5,11},{6,8},{7,9},{8,6},{9,7},... | collective-permute-start | bytes 393224 | tf_op jit(solution)/shard_map/ppermute | solution.py:355
  37.8 2.7 %collective-permute-start.9 = (f32[16,16,128]{2,1,0:T(8,128)S(1)}, f32[16,16,128]{2,1,0:T(8,128)S(1)}, u32[]{:S(2)}, u32[]{:S(2)}) collective-permute-start(f32[16,16,128]{2,1,0:T(8,128)S(1)} %get-tuple-element.70), channel_id=1, source_target_pairs={{0,4},{1,5},{2,6},{3,7},{4,0},{5,1},{6,2},{7,3},{8,12},{9,13},{10,... | collective-permute-start | bytes 393224 | tf_op jit(solution)/shard_map/ppermute | solution.py:355
  41.4 5.7 %collective-permute-done.26.refs_7_ = f32[16,16,128]{2,1,0:T(8,128)S(1)} collective-permute-done((f32[16,16,128]{2,1,0:T(8,128)S(1)}, f32[16,16,128]{2,1,0:T(8,128)S(1)}, u32[]{:S(2)}, u32[]{:S(2)}) %collective-permute-start.26) | collective-permute-done | bytes 131104 | tf_op jit(solution)/shard_map/ppermute | solution.py:355
  47.1 4.1 %collective-permute-done.27.refs_8_ = f32[16,16,128]{2,1,0:T(8,128)S(1)} collective-permute-done((f32[16,16,128]{2,1,0:T(8,128)S(1)}, f32[16,16,128]{2,1,0:T(8,128)S(1)}, u32[]{:S(2)}, u32[]{:S(2)}) %collective-permute-start.27) | collective-permute-done | bytes 131104 | tf_op jit(solution)/shard_map/ppermute | solution.py:355
  51.2 2.3 %collective-permute-start.13 = (f32[16,16,128]{2,1,0:T(8,128)S(1)}, f32[16,16,128]{2,1,0:T(8,128)S(1)}, u32[]{:S(2)}, u32[]{:S(2)}) collective-permute-start(f32[16,16,128]{2,1,0:T(8,128)S(1)} %get-tuple-element.74), channel_id=1, source_target_pairs={{0,12},{1,13},{2,14},{3,15},{4,8},{5,9},{6,10},{7,11},{8,4},{9,5},... | collective-permute-start | bytes 393224 | tf_op jit(solution)/shard_map/ppermute | solution.py:355
  53.5 9.2 %middle.3 = (f32[16,16,128]{2,1,0:T(8,128)S(1)}, f32[16,16,128]{2,1,0:T(8,128)S(1)}, f32[16,16,128]{2,1,0:T(8,128)S(1)}, f32[16,16,128]{2,1,0:T(8,128)S(1)}, f32...) custom-call(s32[3]{0:T(128)S(1)} %copy-done.11, ...), custom_call_target="tpu_custom_call" | custom-call | flops 4831838208 | bytes 3145728 | tf_op jit(solution)/shard_map/middle/pallas_call | solution.py:96
  64.0 4.2 %collective-permute-start.29 = (f32[16,16,128]{2,1,0:T(8,128)S(1)}, f32[16,16,128]{2,1,0:T(8,128)S(1)}, u32[]{:S(2)}, u32[]{:S(2)}) collective-permute-start(f32[16,16,128]{2,1,0:T(8,128)S(1)} %get-tuple-element.93), channel_id=1, source_target_pairs={{0,4},{1,5},{2,6},{3,7},{4,0},{5,1},{6,2},{7,3},{8,12},{9,13},{10,... | collective-permute-start | bytes 393224 | tf_op jit(solution)/shard_map/ppermute | solution.py:355
  70.9 3.7 %collective-permute-done.14.refs_8_ = f32[16,16,128]{2,1,0:T(8,128)S(1)} collective-permute-done((f32[16,16,128]{2,1,0:T(8,128)S(1)}, f32[16,16,128]{2,1,0:T(8,128)S(1)}, u32[]{:S(2)}, u32[]{:S(2)}) %collective-permute-start.14) | collective-permute-done | bytes 131104 | tf_op jit(solution)/shard_map/ppermute | solution.py:355
  74.6 9.4 %middle.2 = (f32[16,16,128]{2,1,0:T(8,128)S(1)}, f32[16,16,128]{2,1,0:T(8,128)S(1)}, f32[16,16,128]{2,1,0:T(8,128)S(1)}, f32[16,16,128]{2,1,0:T(8,128)S(1)}, f32...) custom-call(s32[3]{0:T(128)S(1)} %copy-done.11, ...), custom_call_target="tpu_custom_call" | custom-call | flops 4831838208 | bytes 3145728 | tf_op jit(solution)/shard_map/middle/pallas_call | solution.py:96
  86.8 4.0 %collective-permute-start.16 = (f32[16,16,128]{2,1,0:T(8,128)S(1)}, f32[16,16,128]{2,1,0:T(8,128)S(1)}, u32[]{:S(2)}, u32[]{:S(2)}) collective-permute-start(f32[16,16,128]{2,1,0:T(8,128)S(1)} %get-tuple-element.78), channel_id=1, source_target_pairs={{0,4},{1,5},{2,6},{3,7},{4,0},{5,1},{6,2},{7,3},{8,12},{9,13},{10,... | collective-permute-start | bytes 393224 | tf_op jit(solution)/shard_map/ppermute | solution.py:355
  93.4 2.9 %collective-permute-done.34.refs_8_ = f32[16,16,128]{2,1,0:T(8,128)S(1)} collective-permute-done((f32[16,16,128]{2,1,0:T(8,128)S(1)}, f32[16,16,128]{2,1,0:T(8,128)S(1)}, u32[]{:S(2)}, u32[]{:S(2)}) %collective-permute-start.34) | collective-permute-done | bytes 131104 | tf_op jit(solution)/shard_map/ppermute | solution.py:355
  96.6 2.6 %collective-permute-start.21 = (f32[16,16,128]{2,1,0:T(8,128)S(1)}, f32[16,16,128]{2,1,0:T(8,128)S(1)}, u32[]{:S(2)}, u32[]{:S(2)}) collective-permute-start(f32[16,16,128]{2,1,0:T(8,128)S(1)} %get-tuple-element.83), channel_id=1, source_target_pairs={{0,14},{1,15},{2,12},{3,13},{4,10},{5,11},{6,8},{7,9},{8,6},{9,7},... | collective-permute-start | bytes 393224 | tf_op jit(solution)/shard_map/ppermute | solution.py:355
  99.2 2.0 %y_adjoint.5 = (f32[2,4,64,128]{3,2,1,0:T(8,128)S(1)}, f32[2,4,64,128]{3,2,1,0:T(8,128)S(1)}, f32[2,4,64,128]{3,2,1,0:T(8,128)S(1)}, f32[2,4,64,128]{3,2,1,0:T(8...) custom-call(s32[3]{0:T(128)S(1)} %copy-done.11, ...), custom_call_target="tpu_custom_call" | custom-call | flops 402653184 | bytes 3411968 | tf_op jit(solution)/shard_map/y_adjoint/pallas_call | solution.py:96
  102.2 10.7 %collective-permute-done.19.refs_6_ = f32[16,16,128]{2,1,0:T(8,128)S(1)} collective-permute-done((f32[16,16,128]{2,1,0:T(8,128)S(1)}, f32[16,16,128]{2,1,0:T(8,128)S(1)}, u32[]{:S(2)}, u32[]{:S(2)}) %collective-permute-start.19) | collective-permute-done | bytes 131104 | tf_op jit(solution)/shard_map/ppermute | solution.py:355
  112.9 2.8 %collective-permute-done.20.refs_7_ = f32[16,16,128]{2,1,0:T(8,128)S(1)} collective-permute-done((f32[16,16,128]{2,1,0:T(8,128)S(1)}, f32[16,16,128]{2,1,0:T(8,128)S(1)}, u32[]{:S(2)}, u32[]{:S(2)}) %collective-permute-start.20) | collective-permute-done | bytes 131104 | tf_op jit(solution)/shard_map/ppermute | solution.py:355
  115.7 3.9 %collective-permute-done.21.refs_8_ = f32[16,16,128]{2,1,0:T(8,128)S(1)} collective-permute-done((f32[16,16,128]{2,1,0:T(8,128)S(1)}, f32[16,16,128]{2,1,0:T(8,128)S(1)}, u32[]{:S(2)}, u32[]{:S(2)}) %collective-permute-start.21) | collective-permute-done | bytes 131104 | tf_op jit(solution)/shard_map/ppermute | solution.py:355
  120.5 2.3 %collective-permute-start.35 = (f32[2,4,64,128]{3,2,1,0:T(8,128)S(1)}, f32[2,4,64,128]{3,2,1,0:T(8,128)S(1)}, u32[]{:S(2)}, u32[]{:S(2)}) collective-permute-start(f32[2,4,64,128]{3,2,1,0:T(8,128)S(1)} %get-tuple-element.105), channel_id=1, source_target_pairs={{0,1},{1,0},{2,3},{3,2},{4,5},{5,4},{6,7},{7,6},{8,9},{9,8},{10,11... | collective-permute-start | bytes 786440 | tf_op jit(solution)/shard_map/ppermute | solution.py:355
  127.3 1.5 %y_adjoint.9 = (f32[2,4,64,128]{3,2,1,0:T(8,128)S(1)}, f32[2,4,64,128]{3,2,1,0:T(8,128)S(1)}, f32[8,128]{1,0:T(8,128)}) custom-call(s32[3]{0:T(128)S(1)} %copy-done.11, f32[16,16,128]{2,1,0:T(8,128)S(1)} %get-tuple-element.76.refs_1_, f32[16,16,128]{2,1,0:T(8,128)S(1)} %collective-permute-done.15.refs_2_, ...), custom_call_target="tpu_custom_call" | custom-call | flops 100663296 | bytes 2363392 | tf_op jit(solution)/shard_map/y_adjoint/pallas_call | solution.py:96
  130.5 2.4 %collective-permute-start.37 = (f32[4,64,128]{2,1,0:T(8,128)S(1)}, f32[4,64,128]{2,1,0:T(8,128)S(1)}, u32[]{:S(2)}, u32[]{:S(2)}) collective-permute-start(f32[4,64,128]{2,1,0:T(8,128)S(1)} %get-tuple-element.107), channel_id=1, source_target_pairs={{1,2},{2,1},{3,4},{4,3},{5,6},{6,5},{7,8},{8,7},{9,10},{10,9},{11,... | collective-permute-start | bytes 393224 | tf_op jit(solution)/shard_map/ppermute | solution.py:360
  132.9 1.4 %y_adjoint.8 = (f32[2,4,64,128]{3,2,1,0:T(8,128)S(1)}, f32[2,4,64,128]{3,2,1,0:T(8,128)S(1)}, f32[8,128]{1,0:T(8,128)}) custom-call(s32[3]{0:T(128)S(1)} %copy-done.11, f32[16,16,128]{2,1,0:T(8,128)S(1)} %get-tuple-element.76.refs_1_, f32[16,16,128]{2,1,0:T(8,128)S(1)} %collective-permute-done.15.refs_2_, ...), custom_call_target="tpu_custom_call" | custom-call | flops 100663296 | bytes 2363392 | tf_op jit(solution)/shard_map/y_adjoint/pallas_call | solution.py:96
  134.4 4.1 %collective-permute-done.37.refs_5_ = f32[4,64,128]{2,1,0:T(8,128)S(1)} collective-permute-done((f32[4,64,128]{2,1,0:T(8,128)S(1)}, f32[4,64,128]{2,1,0:T(8,128)S(1)}, u32[]{:S(2)}, u32[]{:S(2)}) %collective-permute-start.37) | collective-permute-done | bytes 131104 | tf_op jit(solution)/shard_map/ppermute | solution.py:360
  139.7 1.6 %final.2 = (f32[8,64,128]{2,1,0:T(8,128)}, f32[3,8,64,128]{3,2,1,0:T(8,128)}) custom-call(s32[3]{0:T(128)S(1)} %copy-done.11, f32[4]{0:T(128)S(1)} %pad_maximum_fusion.refs_1_, f32[4]{0:T(128)S(1)} %copy-done.13, f32[8,64,128]{2,1,0:T(8,128)S(1)} %copy-done.5, s32[8,128,128]{2,1,0:T(8,128)S(1)} %copy-done.1, f32[4,8,64,128]{3,2,1,0:T(8,128)S(1)} %laplace.1.refs_5_, ...), custom_call_target="tpu_custom_call" | custom-call | flops 1310720 | bytes 3309568 | tf_op jit(solution)/shard_map/final/pallas_call | solution.py:96
  141.3 1.5 %final.3 = (f32[8,64,128]{2,1,0:T(8,128)}, f32[3,8,64,128]{3,2,1,0:T(8,128)}) custom-call(s32[3]{0:T(128)S(1)} %copy-done.11, f32[4]{0:T(128)S(1)} %pad_maximum_fusion.refs_1_, f32[4]{0:T(128)S(1)} %copy-done.13, f32[8,64,128]{2,1,0:T(8,128)S(1)} %copy-done.5, s32[8,128,128]{2,1,0:T(8,128)S(1)} %copy-done.1, ...), custom_call_target="tpu_custom_call", output_to_operand_aliasing={{0}: (11, {}), {1}: (12, {})} | custom-call | flops 1310720 | bytes 3276800 | tf_op jit(solution)/shard_map/final/pallas_call | solution.py:96
  (114 shorter events, 34.6 us)
Async XLA Ops:
  7.2 11.7 %collective-permute-start.1 = (f32[2,4,64,128]{3,2,1,0:T(8,128)}, f32[2,4,64,128]{3,2,1,0:T(8,128)S(1)}, u32[]{:S(2)}, u32[]{:S(2)}) collective-permute-start(f32[2,4,64,128]{3,2,1,0:T(8,128)} %get-tuple-element.65.refs_5_), channel_id=1, source_target_pairs={{0,16},{16,0},{1,17},{17,1},{2,18},{18,2},{3,19},{19,3},{4,20},{20... | collective-permute-start | bytes 786440 | tf_op jit(solution)/shard_map/ppermute | solution.py:355
  9.8 9.6 %collective-permute-start.2 = (f32[2,4,64,128]{3,2,1,0:T(8,128)}, f32[2,4,64,128]{3,2,1,0:T(8,128)S(1)}, u32[]{:S(2)}, u32[]{:S(2)}) collective-permute-start(f32[2,4,64,128]{3,2,1,0:T(8,128)} %get-tuple-element.66), channel_id=1, source_target_pairs={{0,16},{16,0},{1,17},{17,1},{2,18},{18,2},{3,19},{19,3},{4,20},{20... | collective-permute-start | bytes 786440 | tf_op jit(solution)/shard_map/ppermute | solution.py:355
  24.7 8.4 %collective-permute-start.7 = (f32[16,16,128]{2,1,0:T(8,128)S(1)}, f32[16,16,128]{2,1,0:T(8,128)S(1)}, u32[]{:S(2)}, u32[]{:S(2)}) collective-permute-start(f32[16,16,128]{2,1,0:T(8,128)S(1)} %get-tuple-element.67), channel_id=1, source_target_pairs={{0,8},{1,9},{2,10},{3,11},{4,12},{5,13},{6,14},{7,15},{8,0},{9,1},... | collective-permute-start | bytes 393224 | tf_op jit(solution)/shard_map/ppermute | solution.py:355
  28.3 9.0 %collective-permute-start.23 = (f32[16,16,128]{2,1,0:T(8,128)S(1)}, f32[16,16,128]{2,1,0:T(8,128)S(1)}, u32[]{:S(2)}, u32[]{:S(2)}) collective-permute-start(f32[16,16,128]{2,1,0:T(8,128)S(1)} %get-tuple-element.86), channel_id=1, source_target_pairs={{0,4},{1,5},{2,6},{3,7},{4,0},{5,1},{6,2},{7,3},{8,12},{9,13},{10,... | collective-permute-start | bytes 393224 | tf_op jit(solution)/shard_map/ppermute | solution.py:355
  28.5 9.3 %collective-permute-start.24 = (f32[16,16,128]{2,1,0:T(8,128)S(1)}, f32[16,16,128]{2,1,0:T(8,128)S(1)}, u32[]{:S(2)}, u32[]{:S(2)}) collective-permute-start(f32[16,16,128]{2,1,0:T(8,128)S(1)} %get-tuple-element.87), channel_id=1, source_target_pairs={{0,6},{1,7},{2,4},{3,5},{4,2},{5,3},{6,0},{7,1},{8,14},{9,15},{10,... | collective-permute-start | bytes 393224 | tf_op jit(solution)/shard_map/ppermute | solution.py:355
  29.7 10.7 %collective-permute-start.25 = (f32[16,16,128]{2,1,0:T(8,128)S(1)}, f32[16,16,128]{2,1,0:T(8,128)S(1)}, u32[]{:S(2)}, u32[]{:S(2)}) collective-permute-start(f32[16,16,128]{2,1,0:T(8,128)S(1)} %get-tuple-element.88), channel_id=1, source_target_pairs={{0,10},{1,11},{2,8},{3,9},{4,14},{5,15},{6,12},{7,13},{8,2},{9,3},... | collective-permute-start | bytes 393224 | tf_op jit(solution)/shard_map/ppermute | solution.py:355
  33.1 14.0 %collective-permute-start.26 = (f32[16,16,128]{2,1,0:T(8,128)S(1)}, f32[16,16,128]{2,1,0:T(8,128)S(1)}, u32[]{:S(2)}, u32[]{:S(2)}) collective-permute-start(f32[16,16,128]{2,1,0:T(8,128)S(1)} %get-tuple-element.89), channel_id=1, source_target_pairs={{0,12},{1,13},{2,14},{3,15},{4,8},{5,9},{6,10},{7,11},{8,4},{9,5},... | collective-permute-start | bytes 393224 | tf_op jit(solution)/shard_map/ppermute | solution.py:355
  34.8 16.3 %collective-permute-start.27 = (f32[16,16,128]{2,1,0:T(8,128)S(1)}, f32[16,16,128]{2,1,0:T(8,128)S(1)}, u32[]{:S(2)}, u32[]{:S(2)}) collective-permute-start(f32[16,16,128]{2,1,0:T(8,128)S(1)} %get-tuple-element.90), channel_id=1, source_target_pairs={{0,14},{1,15},{2,12},{3,13},{4,10},{5,11},{6,8},{7,9},{8,6},{9,7},... | collective-permute-start | bytes 393224 | tf_op jit(solution)/shard_map/ppermute | solution.py:355
  37.3 13.9 %collective-permute-start.8 = (f32[16,16,128]{2,1,0:T(8,128)S(1)}, f32[16,16,128]{2,1,0:T(8,128)S(1)}, u32[]{:S(2)}, u32[]{:S(2)}) collective-permute-start(f32[16,16,128]{2,1,0:T(8,128)S(1)} %get-tuple-element.69), channel_id=1, source_target_pairs={{0,2},{1,3},{2,0},{3,1},{4,6},{5,7},{6,4},{7,5},{8,10},{9,11},{10,... | collective-permute-start | bytes 393224 | tf_op jit(solution)/shard_map/ppermute | solution.py:355
  37.8 15.7 %collective-permute-start.9 = (f32[16,16,128]{2,1,0:T(8,128)S(1)}, f32[16,16,128]{2,1,0:T(8,128)S(1)}, u32[]{:S(2)}, u32[]{:S(2)}) collective-permute-start(f32[16,16,128]{2,1,0:T(8,128)S(1)} %get-tuple-element.70), channel_id=1, source_target_pairs={{0,4},{1,5},{2,6},{3,7},{4,0},{5,1},{6,2},{7,3},{8,12},{9,13},{10,... | collective-permute-start | bytes 393224 | tf_op jit(solution)/shard_map/ppermute | solution.py:355
  40.5 22.2 %collective-permute-start.10 = (f32[16,16,128]{2,1,0:T(8,128)S(1)}, f32[16,16,128]{2,1,0:T(8,128)S(1)}, u32[]{:S(2)}, u32[]{:S(2)}) collective-permute-start(f32[16,16,128]{2,1,0:T(8,128)S(1)} %get-tuple-element.71), channel_id=1, source_target_pairs={{0,6},{1,7},{2,4},{3,5},{4,2},{5,3},{6,0},{7,1},{8,14},{9,15},{10,... | collective-permute-start | bytes 393224 | tf_op jit(solution)/shard_map/ppermute | solution.py:355
  47.1 16.9 %collective-permute-start.11 = (f32[16,16,128]{2,1,0:T(8,128)S(1)}, f32[16,16,128]{2,1,0:T(8,128)S(1)}, u32[]{:S(2)}, u32[]{:S(2)}) collective-permute-start(f32[16,16,128]{2,1,0:T(8,128)S(1)} %get-tuple-element.72), channel_id=1, source_target_pairs={{0,8},{1,9},{2,10},{3,11},{4,12},{5,13},{6,14},{7,15},{8,0},{9,1},... | collective-permute-start | bytes 393224 | tf_op jit(solution)/shard_map/ppermute | solution.py:355
  51.2 17.0 %collective-permute-start.12 = (f32[16,16,128]{2,1,0:T(8,128)S(1)}, f32[16,16,128]{2,1,0:T(8,128)S(1)}, u32[]{:S(2)}, u32[]{:S(2)}) collective-permute-start(f32[16,16,128]{2,1,0:T(8,128)S(1)} %get-tuple-element.73), channel_id=1, source_target_pairs={{0,10},{1,11},{2,8},{3,9},{4,14},{5,15},{6,12},{7,13},{8,2},{9,3},... | collective-permute-start | bytes 393224 | tf_op jit(solution)/shard_map/ppermute | solution.py:355
  51.2 19.1 %collective-permute-start.13 = (f32[16,16,128]{2,1,0:T(8,128)S(1)}, f32[16,16,128]{2,1,0:T(8,128)S(1)}, u32[]{:S(2)}, u32[]{:S(2)}) collective-permute-start(f32[16,16,128]{2,1,0:T(8,128)S(1)} %get-tuple-element.74), channel_id=1, source_target_pairs={{0,12},{1,13},{2,14},{3,15},{4,8},{5,9},{6,10},{7,11},{8,4},{9,5},... | collective-permute-start | bytes 393224 | tf_op jit(solution)/shard_map/ppermute | solution.py:355
  53.5 21.2 %collective-permute-start.14 = (f32[16,16,128]{2,1,0:T(8,128)S(1)}, f32[16,16,128]{2,1,0:T(8,128)S(1)}, u32[]{:S(2)}, u32[]{:S(2)}) collective-permute-start(f32[16,16,128]{2,1,0:T(8,128)S(1)} %get-tuple-element.75), channel_id=1, source_target_pairs={{0,14},{1,15},{2,12},{3,13},{4,10},{5,11},{6,8},{7,9},{8,6},{9,7},... | collective-permute-start | bytes 393224 | tf_op jit(solution)/shard_map/ppermute | solution.py:355
  62.7 21.4 %collective-permute-start.28 = (f32[16,16,128]{2,1,0:T(8,128)S(1)}, f32[16,16,128]{2,1,0:T(8,128)S(1)}, u32[]{:S(2)}, u32[]{:S(2)}) collective-permute-start(f32[16,16,128]{2,1,0:T(8,128)S(1)} %get-tuple-element.92), channel_id=1, source_target_pairs={{0,2},{1,3},{2,0},{3,1},{4,6},{5,7},{6,4},{7,5},{8,10},{9,11},{10,... | collective-permute-start | bytes 393224 | tf_op jit(solution)/shard_map/ppermute | solution.py:355
  64.0 21.5 %collective-permute-start.29 = (f32[16,16,128]{2,1,0:T(8,128)S(1)}, f32[16,16,128]{2,1,0:T(8,128)S(1)}, u32[]{:S(2)}, u32[]{:S(2)}) collective-permute-start(f32[16,16,128]{2,1,0:T(8,128)S(1)} %get-tuple-element.93), channel_id=1, source_target_pairs={{0,4},{1,5},{2,6},{3,7},{4,0},{5,1},{6,2},{7,3},{8,12},{9,13},{10,... | collective-permute-start | bytes 393224 | tf_op jit(solution)/shard_map/ppermute | solution.py:355
  68.2 17.3 %collective-permute-start.30 = (f32[16,16,128]{2,1,0:T(8,128)S(1)}, f32[16,16,128]{2,1,0:T(8,128)S(1)}, u32[]{:S(2)}, u32[]{:S(2)}) collective-permute-start(f32[16,16,128]{2,1,0:T(8,128)S(1)} %get-tuple-element.94), channel_id=1, source_target_pairs={{0,6},{1,7},{2,4},{3,5},{4,2},{5,3},{6,0},{7,1},{8,14},{9,15},{10,... | collective-permute-start | bytes 393224 | tf_op jit(solution)/shard_map/ppermute | solution.py:355
  70.3 16.5 %collective-permute-start.31 = (f32[16,16,128]{2,1,0:T(8,128)S(1)}, f32[16,16,128]{2,1,0:T(8,128)S(1)}, u32[]{:S(2)}, u32[]{:S(2)}) collective-permute-start(f32[16,16,128]{2,1,0:T(8,128)S(1)} %get-tuple-element.95), channel_id=1, source_target_pairs={{0,8},{1,9},{2,10},{3,11},{4,12},{5,13},{6,14},{7,15},{8,0},{9,1},... | collective-permute-start | bytes 393224 | tf_op jit(solution)/shard_map/ppermute | solution.py:355
  74.6 16.3 %collective-permute-start.32 = (f32[16,16,128]{2,1,0:T(8,128)S(1)}, f32[16,16,128]{2,1,0:T(8,128)S(1)}, u32[]{:S(2)}, u32[]{:S(2)}) collective-permute-start(f32[16,16,128]{2,1,0:T(8,128)S(1)} %get-tuple-element.96), channel_id=1, source_target_pairs={{0,10},{1,11},{2,8},{3,9},{4,14},{5,15},{6,12},{7,13},{8,2},{9,3},... | collective-permute-start | bytes 393224 | tf_op jit(solution)/shard_map/ppermute | solution.py:355
  85.5 10.8 %collective-permute-start.34 = (f32[16,16,128]{2,1,0:T(8,128)S(1)}, f32[16,16,128]{2,1,0:T(8,128)S(1)}, u32[]{:S(2)}, u32[]{:S(2)}) collective-permute-start(f32[16,16,128]{2,1,0:T(8,128)S(1)} %get-tuple-element.98), channel_id=1, source_target_pairs={{0,14},{1,15},{2,12},{3,13},{4,10},{5,11},{6,8},{7,9},{8,6},{9,7},... | collective-permute-start | bytes 393224 | tf_op jit(solution)/shard_map/ppermute | solution.py:355
  85.5 11.1 %collective-permute-start.15 = (f32[16,16,128]{2,1,0:T(8,128)S(1)}, f32[16,16,128]{2,1,0:T(8,128)S(1)}, u32[]{:S(2)}, u32[]{:S(2)}) collective-permute-start(f32[16,16,128]{2,1,0:T(8,128)S(1)} %get-tuple-element.77), channel_id=1, source_target_pairs={{0,2},{1,3},{2,0},{3,1},{4,6},{5,7},{6,4},{7,5},{8,10},{9,11},{10,... | collective-permute-start | bytes 393224 | tf_op jit(solution)/shard_map/ppermute | solution.py:355
  86.8 9.8 %collective-permute-start.16 = (f32[16,16,128]{2,1,0:T(8,128)S(1)}, f32[16,16,128]{2,1,0:T(8,128)S(1)}, u32[]{:S(2)}, u32[]{:S(2)}) collective-permute-start(f32[16,16,128]{2,1,0:T(8,128)S(1)} %get-tuple-element.78), channel_id=1, source_target_pairs={{0,4},{1,5},{2,6},{3,7},{4,0},{5,1},{6,2},{7,3},{8,12},{9,13},{10,... | collective-permute-start | bytes 393224 | tf_op jit(solution)/shard_map/ppermute | solution.py:355
  90.9 11.3 %collective-permute-start.17 = (f32[16,16,128]{2,1,0:T(8,128)S(1)}, f32[16,16,128]{2,1,0:T(8,128)S(1)}, u32[]{:S(2)}, u32[]{:S(2)}) collective-permute-start(f32[16,16,128]{2,1,0:T(8,128)S(1)} %get-tuple-element.79), channel_id=1, source_target_pairs={{0,6},{1,7},{2,4},{3,5},{4,2},{5,3},{6,0},{7,1},{8,14},{9,15},{10,... | collective-permute-start | bytes 393224 | tf_op jit(solution)/shard_map/ppermute | solution.py:355
  92.1 10.1 %collective-permute-start.18 = (f32[16,16,128]{2,1,0:T(8,128)S(1)}, f32[16,16,128]{2,1,0:T(8,128)S(1)}, u32[]{:S(2)}, u32[]{:S(2)}) collective-permute-start(f32[16,16,128]{2,1,0:T(8,128)S(1)} %get-tuple-element.80), channel_id=1, source_target_pairs={{0,8},{1,9},{2,10},{3,11},{4,12},{5,13},{6,14},{7,15},{8,0},{9,1},... | collective-permute-start | bytes 393224 | tf_op jit(solution)/shard_map/ppermute | solution.py:355
  96.3 16.6 %collective-permute-start.19 = (f32[16,16,128]{2,1,0:T(8,128)S(1)}, f32[16,16,128]{2,1,0:T(8,128)S(1)}, u32[]{:S(2)}, u32[]{:S(2)}) collective-permute-start(f32[16,16,128]{2,1,0:T(8,128)S(1)} %get-tuple-element.81), channel_id=1, source_target_pairs={{0,10},{1,11},{2,8},{3,9},{4,14},{5,15},{6,12},{7,13},{8,2},{9,3},... | collective-permute-start | bytes 393224 | tf_op jit(solution)/shard_map/ppermute | solution.py:355
  96.6 19.1 %collective-permute-start.20 = (f32[16,16,128]{2,1,0:T(8,128)S(1)}, f32[16,16,128]{2,1,0:T(8,128)S(1)}, u32[]{:S(2)}, u32[]{:S(2)}) collective-permute-start(f32[16,16,128]{2,1,0:T(8,128)S(1)} %get-tuple-element.82), channel_id=1, source_target_pairs={{0,12},{1,13},{2,14},{3,15},{4,8},{5,9},{6,10},{7,11},{8,4},{9,5},... | collective-permute-start | bytes 393224 | tf_op jit(solution)/shard_map/ppermute | solution.py:355
  96.6 22.9 %collective-permute-start.21 = (f32[16,16,128]{2,1,0:T(8,128)S(1)}, f32[16,16,128]{2,1,0:T(8,128)S(1)}, u32[]{:S(2)}, u32[]{:S(2)}) collective-permute-start(f32[16,16,128]{2,1,0:T(8,128)S(1)} %get-tuple-element.83), channel_id=1, source_target_pairs={{0,14},{1,15},{2,12},{3,13},{4,10},{5,11},{6,8},{7,9},{8,6},{9,7},... | collective-permute-start | bytes 393224 | tf_op jit(solution)/shard_map/ppermute | solution.py:355
  125.0 13.4 %collective-permute-start.38 = (f32[576,128]{1,0:T(8,128)S(1)}, f32[576,128]{1,0:T(8,128)S(1)}, u32[]{:S(2)}, u32[]{:S(2)}) collective-permute-start(f32[576,128]{1,0:T(8,128)S(1)} %pack.2.refs_4_.refs_12_), channel_id=1, source_target_pairs={{0,16},{16,0},{1,17},{17,1},{2,18},{18,2},{3,19},{19,3},{4,20},{20... | collective-permute-start | bytes 884744 | tf_op jit(solution)/shard_map/ppermute | solution.py:355
  128.8 10.9 %collective-permute-start.42 = (f32[2,4,64,128]{3,2,1,0:T(8,128)S(1)}, f32[2,4,64,128]{3,2,1,0:T(8,128)S(1)}, u32[]{:S(2)}, u32[]{:S(2)}) collective-permute-start(f32[2,4,64,128]{3,2,1,0:T(8,128)S(1)} %get-tuple-element.119), channel_id=1, source_target_pairs={{0,1},{1,0},{2,3},{3,2},{4,5},{5,4},{6,7},{7,6},{8,9},{9,8},{10,11... | collective-permute-start | bytes 786440 | tf_op jit(solution)/shard_map/ppermute | solution.py:355
  128.8 12.5 %collective-permute-start.40 = (f32[2,4,64,128]{3,2,1,0:T(8,128)S(1)}, f32[2,4,64,128]{3,2,1,0:T(8,128)S(1)}, u32[]{:S(2)}, u32[]{:S(2)}) collective-permute-start(f32[2,4,64,128]{3,2,1,0:T(8,128)S(1)} %get-tuple-element.115), channel_id=1, source_target_pairs={{0,1},{1,0},{2,3},{3,2},{4,5},{5,4},{6,7},{7,6},{8,9},{9,8},{10,11... | collective-permute-start | bytes 786440 | tf_op jit(solution)/shard_map/ppermute | solution.py:355
  129.3 12.0 %collective-permute-start.41 = (f32[512,128]{1,0:T(8,128)S(1)}, f32[512,128]{1,0:T(8,128)S(1)}, u32[]{:S(2)}, u32[]{:S(2)}) collective-permute-start(f32[512,128]{1,0:T(8,128)S(1)} %pack.3.refs_13_), channel_id=1, source_target_pairs={{0,16},{16,0},{1,17},{17,1},{2,18},{18,2},{3,19},{19,3},{4,20},{20... | collective-permute-start | bytes 786440 | tf_op jit(solution)/shard_map/ppermute | solution.py:355
  (30 other events, 518.6 us)
